TPU v7x, 32 devices: a whole 2x2x4 slice. The times are simulated.
32 devices in a mesh: img: 16 (over z, y, x), seq: 2 (over core).
Axes of the slice: x: 2, y: 2, z: 4, core: 2. Of those that a mesh axis runs over, the one named last changes fastest.
Arguments:
- inputs: bfloat16 [32, 320, 1024], P('img', 'seq'), may hold values from -6 to 6
- cotangent: bfloat16 [32, 320, 1024], P('img', 'seq'), may hold values from -6 to 6
- kept_counts: int32 [32], P('img'), may hold values from 200 to 256, as said below
- norm1_gain: bfloat16 [1024], P(('img', 'seq')), may hold values from 0.099609375 to 1.8984375
- norm1_bias: bfloat16 [1024], P(('img', 'seq')), may hold values from -4 to 4
- qkv_weight: bfloat16 [1024, 3072], P(('img', 'seq')), may hold values from -0.25 to 0.25
- qv_bias: bfloat16 [2048], P(('img', 'seq')), may hold values from -6 to 6
- proj_weight: bfloat16 [1024, 1024], P(('img', 'seq')), may hold values from -0.5 to 0.5
- proj_bias: bfloat16 [1024], P(('img', 'seq')), may hold values from -6 to 6
- norm2_gain: bfloat16 [1024], P(('img', 'seq')), may hold values from 0.099609375 to 1.8984375
- norm2_bias: bfloat16 [1024], P(('img', 'seq')), may hold values from -4 to 4
- fc1_weight: bfloat16 [1024, 4096], P(('img', 'seq')), may hold values from -0.1875 to 0.1875
- fc1_bias: bfloat16 [4096], P(('img', 'seq')), may hold values from -6 to 6
- fc2_weight: bfloat16 [4096, 1024], P(('img', 'seq')), may hold values from -0.1875 to 0.1875
- fc2_bias: bfloat16 [1024], P(('img', 'seq')), may hold values from -6 to 6
Outputs:
- outputs: bfloat16 [32, 320, 1024], P('img', 'seq')
- input_grad: float32 [32, 320, 1024], P('img', 'seq')
- norm1_gain_grad: float32 [1024], P(('img', 'seq'))
- norm1_bias_grad: float32 [1024], P(('img', 'seq'))
- qkv_weight_grad: float32 [1024, 3072], P(('img', 'seq'))
- qv_bias_grad: float32 [2048], P(('img', 'seq'))
- proj_weight_grad: float32 [1024, 1024], P(('img', 'seq'))
- proj_bias_grad: float32 [1024], P(('img', 'seq'))
- norm2_gain_grad: float32 [1024], P(('img', 'seq'))
- norm2_bias_grad: float32 [1024], P(('img', 'seq'))
- fc1_weight_grad: float32 [1024, 4096], P(('img', 'seq'))
- fc1_bias_grad: float32 [4096], P(('img', 'seq'))
- fc2_weight_grad: float32 [4096, 1024], P(('img', 'seq'))
- fc2_bias_grad: float32 [1024], P(('img', 'seq'))
Inputs may be any that keep to these rules, and one draw needn't show every extreme that they name: `kept_counts`: kept tokens of each image; some image has exactly 256 and some exactly 200.
All inputs are finite; a program needn't handle non-finite values.
Results may differ from a plain program's by a relative error of at most 0.015.
Values may be sent and summed in bfloat16 or wider, within the bound.
No kernel may reach another device: no remote copies, remote signals or barrier semaphores. Data moves between devices by JAX's collectives and lax.ppermute only.
A program may use at most 256 MiB of HBM per device.

v0:
```python
import functools

import jax
import jax.numpy as jnp
import numpy as np
from jax import lax
from jax.experimental import pallas as pl
from jax.experimental.pallas import tpu as pltpu
from jax.sharding import PartitionSpec as P

HEAD_DIM = 64
BUFFER = 64
PAIR = 2
f32 = jnp.float32
b16 = jnp.bfloat16
HIGH = lax.Precision.HIGHEST


def dot(left, right):
    return jnp.dot(left, right, preferred_element_type=f32)


def dot_tn(left, right):
    return lax.dot_general(left, right, (((0,), (0,)), ((), ())), preferred_element_type=f32)


def dot_nt(left, right):
    return lax.dot_general(left, right, (((1,), (1,)), ((), ())), preferred_element_type=f32)


def norm_parts(values):
    centre = values - jnp.mean(values, axis=-1, keepdims=True)
    scale = lax.rsqrt(jnp.mean(centre * centre, axis=-1, keepdims=True) + 1e-06)
    return centre * scale, scale


def norm_back(grad, normed, scale, gain):
    e = grad * gain
    return scale * (
        e
        - jnp.mean(e, axis=-1, keepdims=True)
        - normed * jnp.mean(e * normed, axis=-1, keepdims=True)
    )


def core_swap(value):
    return lax.ppermute(value, "seq", [(0, 1), (1, 0)])


def bit_swap(value, bits):
    n = lax.axis_size("img")
    pairs = [
        (2 * j + c, 2 * (j ^ (1 << bits[c])) + c) for j in range(n) for c in range(2)
    ]
    return lax.ppermute(value, ("img", "seq"), pairs)


def after(value, *others):
    return lax.optimization_barrier((value, *others))[0]


class Gather:
    def __init__(self, block, orders):
        self.held = None if block is None else block[None]
        self.steps = list(zip(*orders))

    def step(self, *others):
        self.sent = after(self.held, *others) if others else self.held
        self.got = bit_swap(self.sent, self.steps.pop(0))
        self.held = jnp.concatenate([self.sent, self.got], axis=0)
        return self.got


class Scatter:
    def __init__(self, send, keep, orders):
        self.send, self.keep = send, keep
        self.steps = list(zip(*orders))[::-1]

    def step(self, *others):
        send = after(self.send, *others) if others else self.send
        self.got = bit_swap(send, self.steps.pop(0))
        total = self.keep + self.got.astype(f32)
        cut = total.shape[0] // 2
        if cut:
            self.send = total[cut:].astype(send.dtype)
        self.keep = total[: max(cut, 1)]


def spread(position, order):
    return sum((((position >> k) & 1) << bit) for k, bit in enumerate(order))


def onehot(left, right):
    return (left[:, None] == right[None, :]).astype(b16)


class Places:
    def __init__(self, n, width, units, full, most):
        rows, half, few = width // (2 * n), width // 2, n // 2
        place, chips = np.arange(width), np.arange(few)
        col = np.arange(few * units)
        names = ("qkv", "fc1", "proj", "heads", "units", "chips", "owners")
        found = {name: [] for name in names}
        for me in range(n):
            for core in range(2):
                chip = me ^ spread(place // (2 * rows), full[core])
                found["qkv"].append((2 * chip + (core ^ (place // rows % 2))) * rows + place % rows)
                chip = me ^ spread(place // (4 * rows), most[core])
                chip = chip ^ ((place // (2 * rows) % 2) << PAIR)
                found["fc1"].append((2 * chip + (core ^ (place // rows % 2))) * rows + place % rows)
                source = core ^ (place // half)
                chip = me ^ np.where(
                    source == 0,
                    spread(place // rows % n, full[0]),
                    spread(place // rows % n, full[1]),
                )
                found["proj"].append((2 * chip + source) * rows + place % rows)
                found["heads"].append(source * half + place % half)
                short = lambda chip: (chip >> (PAIR + 1) << PAIR) + chip % (1 << PAIR)
                owner = me ^ spread(chips, most[core])
                found["units"].append(short(owner)[col // units] * units + col % units)
                side = (me >> PAIR) & 1
                low = 1 << PAIR
                found["owners"].append(chips // low * 2 * low + side * low + chips % low)
                found["chips"].append(me ^ spread(np.arange(n), full[core]))
        for name in names:
            setattr(self, name, np.stack(found[name]).astype(np.int32))


def live_slots(meta_ref, local, axis):
    shape = (2 * local, 1) if axis == 0 else (1, 2 * local)
    place = lax.broadcasted_iota(jnp.int32, shape, axis)
    core = meta_ref[0]
    slot = jnp.where(place < local, place + core * local, place - core * local)
    return slot < BUFFER + meta_ref[1]


def attend_kernel(meta_ref, q_ref, k_ref, v_ref, o_ref):
    live = live_slots(meta_ref, q_ref.shape[0] // 2, 1)
    outs = []
    for e in range(2):
        part = slice(e * HEAD_DIM, (e + 1) * HEAD_DIM)
        raw = dot_nt(q_ref[:, part], k_ref[:, part]) * (HEAD_DIM**-0.5)
        raw = jnp.where(live, raw, -1e30)
        expo = jnp.exp(raw - jnp.max(raw, axis=-1, keepdims=True))
        probs = expo * (1.0 / jnp.sum(expo, axis=-1, keepdims=True))
        outs.append(dot(probs.astype(b16), v_ref[:, part]))
    o_ref[...] = jnp.concatenate(outs, axis=1).astype(b16)


def attend_back_kernel(meta_ref, q_ref, k_ref, v_ref, g_ref, o_ref):
    pairs = o_ref.shape[1] // (3 * 2 * HEAD_DIM)
    live = live_slots(meta_ref, q_ref.shape[0] // 2, 0)
    scale = HEAD_DIM**-0.5
    parts = ([], [], [])
    for e in range(2):
        part = slice(e * HEAD_DIM, (e + 1) * HEAD_DIM)
        qe, ke, ve, ge = (r[:, part] for r in (q_ref, k_ref, v_ref, g_ref))
        raw = jnp.where(live, dot_nt(ke, qe) * scale, -1e30)
        expo = jnp.exp(raw - jnp.max(raw, axis=0, keepdims=True))
        probs = expo * (1.0 / jnp.sum(expo, axis=0, keepdims=True))
        d_probs = dot_nt(ve, ge)
        inner = jnp.sum(probs * d_probs, axis=0, keepdims=True)
        d_scores = (probs * (d_probs - inner)).astype(b16)
        parts[0].append(dot_tn(d_scores, ke) * scale)
        parts[1].append(dot(d_scores, qe) * scale)
        parts[2].append(dot(probs.astype(b16), ge))
    for which in range(3):
        at = pl.multiple_of((which * pairs + pl.program_id(0)) * 2 * HEAD_DIM, 2 * HEAD_DIM)
        o_ref[:, pl.ds(at, 2 * HEAD_DIM)] = jnp.concatenate(parts[which], axis=1).astype(b16)


def attention(mixed, meta, grad=None):
    slots, wide = mixed.shape
    pairs = wide // (3 * 2 * HEAD_DIM)
    block = (slots, 2 * HEAD_DIM)
    spec = lambda first: pl.BlockSpec(block, lambda h, m, f=first: (0, f + h))
    specs = [spec(0), spec(pairs), spec(2 * pairs)]
    dots = 2 * pairs * 2 * slots * slots * HEAD_DIM
    if grad is None:
        kernel, extra, out_wide, out_spec, count = attend_kernel, (), wide // 3, spec(0), 2
    else:
        kernel, extra, out_wide, count = attend_back_kernel, (grad,), wide, 5
        specs.append(spec(0))
        out_spec = pl.BlockSpec((slots, wide), lambda h, m: (0, 0))
    return pl.pallas_call(
        kernel,
        out_shape=jax.ShapeDtypeStruct((slots, out_wide), b16),
        grid_spec=pltpu.PrefetchScalarGridSpec(
            num_scalar_prefetch=1, grid=(pairs,), in_specs=specs, out_specs=out_spec
        ),
        cost_estimate=pl.CostEstimate(
            flops=4 * count * dots, bytes_accessed=4 * mixed.size, transcendentals=0
        ),
    )(meta, mixed, mixed, mixed, *extra)


def plain_body(
    inputs,
    cotangent,
    kept_counts,
    norm1_gain,
    norm1_bias,
    qkv_weight,
    qv_bias,
    proj_weight,
    proj_bias,
    norm2_gain,
    norm2_bias,
    fc1_weight,
    fc1_bias,
    fc2_weight,
    fc2_bias,
):
    images, local, width = inputs.shape
    n = lax.axis_size("img")
    me = lax.axis_index("img")
    core = lax.axis_index("seq")
    levels = n.bit_length() - 1
    half = width // 2
    rows = width // (2 * n)
    units = fc2_weight.shape[0]
    few = n // 2
    hidden = units * few
    low = 1 << PAIR
    side = (me >> PAIR) & 1

    full = tuple(tuple(range(levels - 1, 1, -1)) + last for last in ((0, 1), (1, 0)))
    most = tuple(
        (first,) + tuple(b for b in range(levels - 1, 1, -1) if b != PAIR) + (1 - first,)
        for first in (0, 1)
    )

    table = Places(n, width, units, full, most)
    dev = 2 * me + core
    pick = lambda rows_of: lax.dynamic_index_in_dim(jnp.asarray(rows_of), dev, 0, False)

    mine_of = lambda a, axis: lax.dynamic_index_in_dim(a, core, axis, False)
    theirs_of = lambda a, axis: lax.dynamic_index_in_dim(a, 1 - core, axis, False)
    smalls = (norm1_gain, norm1_bias, qv_bias, proj_bias, norm2_gain, norm2_bias, fc1_bias, fc2_bias)
    ends = [0]
    for item in smalls:
        ends.append(ends[-1] + item.shape[0])
    pair = (PAIR, PAIR)
    qkv_cut = qkv_weight.reshape(rows, 3, 2, half)
    qkv_got = core_swap(theirs_of(qkv_cut, 2))
    qkv_block = jnp.concatenate([mine_of(qkv_cut, 2), qkv_got], axis=0)
    qkv = Gather(qkv_block.reshape(2 * rows, 3 * half), full)
    x_other = core_swap(inputs)
    q_got = [qkv.step()]

    small_own = jnp.concatenate(smalls)
    small_other = core_swap(small_own)
    small = jnp.where(
        core == 0, jnp.stack([small_own, small_other]), jnp.stack([small_other, small_own])
    )
    small = Gather(small, full)
    small.step(qkv_got)

    fc1_cut = after(fc1_weight, qkv_got).reshape(rows, few // low, 2, low, 2, units)
    fc1_got = core_swap(theirs_of(fc1_cut, 4))
    fc1_block = jnp.stack([mine_of(fc1_cut, 4), fc1_got])
    side_of = lambda which: lax.dynamic_index_in_dim(fc1_block, which, 3, False)
    fc1_block = jnp.stack([side_of(side), bit_swap(side_of(1 - side), pair)])
    fc1 = Gather(fc1_block.reshape(4 * rows, hidden), most)
    fc2 = Gather(fc2_weight, most)

    q_got.append(qkv.step())
    small.step(q_got[0])
    fc2_got = fc2.step(q_got[0])
    while len(qkv.steps) > 2:
        q_got.append(qkv.step())
        small.step(q_got[-2])
    qkv.step()
    q_got.append(qkv.got)
    small.step(q_got[-2])
    proj = Gather(proj_weight, full)
    proj_got = proj.step(q_got[-2])
    fc1_first = fc1.step(fc2_got)
    qkv.step()
    q_got.append(qkv.got)
    small.step(q_got[-2])
    while len(proj.steps) > 2:
        proj_got = proj.step(q_got[-2])
    slot = core * local + lax.iota(jnp.int32, local)
    row_live = [(slot < BUFFER + kept_counts[i])[:, None] for i in range(images)]

    def to_four(own, *others):
        two = jnp.concatenate([own, bit_swap(after(own, *others), pair)], axis=0)
        return jnp.concatenate([two, core_swap(two)], axis=0)

    cotangent = after(cotangent, q_got[-3])
    up_low = [jnp.where(live, c, 0).astype(b16) for live, c in zip(row_live, cotangent)]
    up_all = [to_four(u) for u in up_low]

    dev = after(dev, q_got[0])
    abs_rows = lax.iota(jnp.int32, width)
    qkv_perm = onehot(abs_rows, pick(table.qkv))
    fc1_perm = onehot(abs_rows, pick(table.fc1))
    proj_perm = onehot(pick(table.heads), pick(table.proj))
    col_perm = onehot(lax.iota(jnp.int32, hidden), pick(table.units))
    chip_perm = onehot(lax.iota(jnp.int32, n), pick(table.chips))
    unit_perm = onehot(pick(table.owners), lax.iota(jnp.int32, n))
    x_all = jnp.stack([inputs, x_other], axis=1).reshape(images * 2 * local, width)
    normed_all, _ = norm_parts(x_all.astype(f32))
    small = dot(chip_perm, small.held.reshape(n, -1)).reshape(n, 2, -1)
    gain_one, shift_one, b_qv, b_proj, gain_two, shift_two, b_fc1, b_fc2 = (
        small[:, :, a:b].reshape(-1) for a, b in zip(ends, ends[1:])
    )
    bias_fc1 = jnp.dot(
        unit_perm.astype(f32), mine_of(b_fc1.reshape(n, 2, units), 1), precision=HIGH
    ).reshape(-1)
    qv_cut = mine_of(b_qv.reshape(2, 2, half), 1)
    bias_qkv = jnp.concatenate([qv_cut[0], jnp.zeros((half,), f32), qv_cut[1]])
    first = (normed_all * gain_one + shift_one).astype(b16)
    first = dot(first, qkv_perm).astype(b16)

    w_qkv = qkv.held.reshape(width, 3 * half)
    mixed = (dot(first, w_qkv) + bias_qkv).astype(b16).reshape(images, 2 * local, 3 * half)
    metas = [jnp.stack([core.astype(jnp.int32), kept_counts[i]]) for i in range(images)]
    proj.step(q_got[-1])
    proj.step()
    w_proj = proj.held.reshape(half, width)
    w_proj = jnp.concatenate([w_proj, core_swap(w_proj)], axis=0)
    w_proj = dot(proj_perm, w_proj).astype(b16)
    fc2_got = fc2.step(q_got[-1])
    fc1_got = fc1.step(fc2_got)
    while fc2.steps:
        fc2.step()
    w_fc2 = dot(col_perm, fc2.held.reshape(hidden, width)).astype(b16)
    while fc1.steps:
        fc1.step()
    w_fc1 = dot(fc1_perm, fc1.held.reshape(width, hidden)).astype(b16)

    attended, middle, second, normed_two, scale_two = [], [], [], [], []
    for i in range(images):
        heads = attention(mixed[i], metas[i])
        heads = jnp.concatenate([heads[:local], core_swap(heads[local:])], axis=1)
        attended.append(heads)
        middle.append(inputs[i].astype(f32) + dot(heads, w_proj) + b_proj)
        normed, scale = norm_parts(middle[i])
        normed_two.append(normed)
        scale_two.append(scale)
        second.append(to_four((normed * gain_two + shift_two).astype(b16)))

    activated, slope = [], []
    for i in range(images):
        pre = dot(second[i], w_fc1) + bias_fc1
        phi = 0.5 * (1.0 + lax.erf(pre * (0.5**0.5)))
        activated.append((pre * phi).astype(b16))
        slope.append((phi + pre * jnp.exp(-0.5 * pre * pre) * 0.3989422804014327).astype(b16))

    def core_sum(part):
        return part[: 2 * local] + core_swap(part[2 * local :].astype(b16)).astype(f32)

    def pair_sum(two):
        return two[:local] + bit_swap(two[local:].astype(b16), pair).astype(f32)

    d_pre, d_two = [], []
    for i in range(images):
        d_pre.append((slope[i].astype(f32) * dot_nt(up_all[i], w_fc2)).astype(b16))
        d_two.append(core_sum(dot_nt(d_pre[i], w_fc1)))
    out_two = [core_sum(dot(activated[i], w_fc2)) for i in range(images)]
    d_second = [pair_sum(d) for d in d_two]

    cat = lambda parts: jnp.concatenate(parts, axis=0)
    cut = hidden // 2
    up_cat = cat(up_all)
    activated = after(cat(activated), *d_two)
    activated_rel = dot(activated, col_perm).astype(b16)
    grad_fc2 = Scatter(
        dot_tn(activated_rel[:, cut:], up_cat).astype(b16).reshape(-1, units, width),
        dot_tn(activated_rel[:, :cut], up_cat).reshape(-1, units, width),
        most,
    )
    second_rel = dot(cat(second), fc1_perm).astype(b16)
    d_pre_cat = cat(d_pre)
    grad_fc1 = Scatter(
        dot_tn(second_rel[:, half:], d_pre_cat).astype(b16).reshape(-1, 4 * rows, hidden),
        dot_tn(second_rel[:, :half], d_pre_cat).reshape(-1, 4 * rows, hidden),
        most,
    )
    grad_fc2.step()
    grad_fc1.step(grad_fc2.got)
    while grad_fc2.steps:
        grad_fc2.step()
    while grad_fc1.steps:
        grad_fc1.step()

    outputs = [
        jnp.where(row_live[i], middle[i] + pair_sum(after(out_two[i], *d_second)) + b_fc2, 0.0)
        for i in range(images)
    ]
    outputs = jnp.stack(outputs).astype(b16)

    d_middle, d_branch, d_mixed = [], [], []
    for i in range(images):
        back = norm_back(d_second[i], normed_two[i], scale_two[i], gain_two)
        d_middle.append(up_low[i].astype(f32) + back)
        d_branch.append(d_middle[i].astype(b16))
        d_att = dot_nt(d_branch[i], w_proj).astype(b16)
        d_att = jnp.concatenate([d_att[:, :half], core_swap(d_att[:, half:])], axis=0)
        d_mixed.append(attention(mixed[i], metas[i], d_att))

    attended_rel = dot(cat(attended), proj_perm).astype(b16)
    attended_rel = jnp.concatenate(
        [attended_rel[:, :half], core_swap(attended_rel[:, half:])], axis=0
    )
    branch = cat(d_branch)
    branch_all = jnp.concatenate([branch, core_swap(branch)], axis=0)
    parts = lambda a: a.reshape(-1, rows, a.shape[-1])
    proj_send = dot_tn(attended_rel[:, half // 2 :], branch_all).astype(b16)
    proj_keep = dot_tn(attended_rel[:, : half // 2], branch_all)
    grad_proj = Scatter(parts(proj_send), parts(proj_keep), full)
    while grad_proj.steps:
        grad_proj.step()

    d_mixed = cat(d_mixed)
    qkv_send = dot_tn(first[:, half:], d_mixed).astype(b16)
    d_first = dot_nt(dot_nt(after(d_mixed, qkv_send), w_qkv).astype(b16), qkv_perm).astype(b16)
    d_first = d_first.reshape(images, 2, local, width)
    d_first = d_first[:, 0].astype(f32) + core_swap(d_first[:, 1]).astype(f32)
    qkv_keep = dot_tn(first[:, :half], after(d_mixed, d_first))
    cut3 = lambda a: a.reshape(-1, 2 * rows, 3 * half)
    grad_qkv = Scatter(cut3(qkv_send), cut3(qkv_keep), full)
    normed_one, scale_one = norm_parts(inputs.astype(f32))
    input_grad = jnp.stack(d_middle) + norm_back(d_first, normed_one, scale_one, gain_one)

    placed = lambda a, axis: jnp.stack(
        [jnp.where(core == 0, a, 0.0), jnp.where(core == 1, a, 0.0)], axis=axis
    )
    total = lambda a: jnp.sum(a.astype(f32).reshape(-1, a.shape[-1]), axis=0)
    d_mixed_sum = total(d_mixed).reshape(3, half)
    d_pre_sum = jnp.dot(
        unit_perm.astype(f32).T, total(d_pre_cat).reshape(few, units), precision=HIGH
    )
    d_second = jnp.stack(d_second)
    small_grads = (
        total(d_first * normed_one),
        total(d_first),
        placed(d_mixed_sum[::2], 1),
        total(branch),
        total(d_second * jnp.stack(normed_two)),
        total(d_second),
        placed(d_pre_sum, 1),
        total(jnp.stack(up_low)),
    )
    small_grads = jnp.concatenate([g.reshape(n, 2, -1) for g in small_grads], axis=2)
    small_grads = mine_of(small_grads, 1) + core_swap(theirs_of(small_grads, 1))
    small_grads = jnp.dot(chip_perm.astype(f32).T, small_grads, precision=HIGH)
    small_grads = small_grads[:, None]
    small_grads = Scatter(small_grads[few:], small_grads[:few], full)
    small_grads.step()
    grad_qkv.step()
    while grad_qkv.steps:
        small_grads.step(grad_qkv.got)
        grad_qkv.step()
    small_grads = small_grads.keep[0, 0]
    small_grads = [small_grads[a:b] for a, b in zip(ends, ends[1:])]
    grad_fc1, grad_fc2, grad_proj, grad_qkv = (
        g.keep[0] for g in (grad_fc1, grad_fc2, grad_proj, grad_qkv)
    )

    qkv_other = core_swap(grad_qkv[rows:])
    both = lambda own, other, which, axis: jnp.where(
        which == 0, jnp.stack([own, other], axis=axis), jnp.stack([other, own], axis=axis)
    )
    cut3 = lambda a: a.reshape(rows, 3, half)
    grad_qkv = both(cut3(grad_qkv[:rows]), cut3(qkv_other), core, 2).reshape(qkv_weight.shape)

    pair_other = bit_swap(grad_fc1[2 * rows :], pair)
    cut4 = lambda a: a.reshape(2 * rows, few // low, low, units)
    grad_fc1 = both(cut4(grad_fc1[: 2 * rows]), cut4(pair_other), side, 2)
    core_other = core_swap(grad_fc1[rows:])
    grad_fc1 = both(grad_fc1[:rows], core_other, core, 4).reshape(fc1_weight.shape)
    return (
        outputs,
        input_grad,
        small_grads[0],
        small_grads[1],
        grad_qkv,
        small_grads[2],
        grad_proj,
        small_grads[3],
        small_grads[4],
        small_grads[5],
        grad_fc1,
        small_grads[6],
        grad_fc2,
        small_grads[7],
    )


def pack_units_kernel(where_ref, w_ref, mine_ref, theirs_ref):
    wide = mine_ref.shape[2]
    units = 128
    low = 1 << PAIR
    for ref, core in ((mine_ref, where_ref[0]), (theirs_ref, 1 - where_ref[0])):
        for p in range(2):
            side = where_ref[1] ^ p
            for b in range(wide // units):
                chip = (b // low) * 2 * low + side * low + b % low
                at = pl.multiple_of((2 * chip + core) * units, units)
                ref[p, :, b * units : (b + 1) * units] = w_ref[:, pl.ds(at, units)]


def pack_units(weight, units, core, side):
    rows, hidden = weight.shape
    if units == 128:
        out = jax.ShapeDtypeStruct((2, rows, hidden // 4), weight.dtype)
        return pl.pallas_call(
            pack_units_kernel,
            out_shape=(out, out),
            in_specs=[pl.BlockSpec(memory_space=pltpu.SMEM), pl.BlockSpec(memory_space=pltpu.VMEM)],
            out_specs=(pl.BlockSpec(memory_space=pltpu.VMEM),) * 2,
        )(jnp.stack([core, side]), weight)
    low = 1 << PAIR
    cut = weight.reshape(rows, -1, 2, low, 2, units)

    def part(c, p):
        block = lax.dynamic_index_in_dim(cut, c, 4, False)
        return lax.dynamic_index_in_dim(block, p, 2, False).reshape(rows, hidden // 4)

    return tuple(jnp.stack([part(c, side), part(c, 1 - side)]) for c in (core, 1 - core))


LANES = 128
MEASURED_US = {
    "k_pack_heads": 1.6, "k_heads": 7, "k_attend": 6, "k_proj_weight": 3, "k_project": 3.4,
    "k_unpack_units": 4.5, "k_feed": 20, "k_feed_out": 6, "k_pair_send": 5, "k_grad_feed": 15,
    "k_middle_back": 4.4, "k_attend_back": 8.3, "k_grad_proj": 5.5, "k_grad_heads": 8.7,
    "k_first_back": 6, "k_input_back": 4.3, "k_small": 1.8, "k_output": 2.5, "k_columns": 2, "k_rows": 1.8,
}
FLOPS_PER_US = 0.5e9
VMEM_LIMIT = 56 * 1024 * 1024
SMALL_ROWS = 8
GAIN1, BIAS1, QV, PROJ_B, GAIN2, BIAS2, FC1_B, FC2_B = range(8)


def spread_of(position, orders, core):
    a, b = (spread(position, order) for order in orders)
    return a if a == b else jnp.where(core == 0, a, b)


def position_of(bits, orders, core):
    a, b = (
        sum((((bits >> bit) & 1) << k) for k, bit in enumerate(order)) for order in orders
    )
    return jnp.where(core == 0, a, b)


def call(kernel, out, args, grid=None, in_specs=None, out_specs=None, scratch=(), deps=(), place=None):
    whole = pl.BlockSpec(memory_space=pltpu.VMEM)
    outs = out if isinstance(out, tuple) else (out,)
    specs = [pl.BlockSpec(memory_space=pltpu.SMEM)] + list(in_specs or [whole] * len(args))
    out_specs = out_specs if out_specs is not None else tuple(whole for _ in outs)
    extra = {} if grid is None else {"grid": grid}
    name = getattr(kernel, "func", kernel).__name__
    flops = int(MEASURED_US[name] * FLOPS_PER_US)
    if deps:
        specs += [pl.BlockSpec(memory_space=pl.ANY)] * len(deps)
        inner, count = kernel, 1 + len(args)

        def kernel(*refs):
            return inner(*refs[:count], *refs[count + len(deps) :])

    result = pl.pallas_call(
        kernel,
        out_shape=outs,
        in_specs=specs,
        out_specs=tuple(out_specs),
        scratch_shapes=list(scratch),
        compiler_params=pltpu.CompilerParams(vmem_limit_bytes=VMEM_LIMIT),
        cost_estimate=pl.CostEstimate(flops=flops, bytes_accessed=1000, transcendentals=0),
        **extra,
    )(place, *args, *deps)
    return result if isinstance(out, tuple) else result[0]


class Order:
    def __init__(self, place):
        self.place, self.last = place, ()

    def call(self, *args, wait=(), **named):
        result = call(*args, deps=tuple(wait) + self.last, place=self.place, **named)
        found = result if isinstance(result, tuple) else (result,)
        self.last = (min(found, key=lambda a: a.size),)
        return result

    def now(self, *values):
        values = lax.optimization_barrier((*values, *self.last))
        self.last = tuple(values[len(values) - len(self.last) :])
        values = values[: len(values) - len(self.last)]
        return values if len(values) > 1 else values[0]


def tie(*values):
    return lax.optimization_barrier(values)


def shape(dims, dtype=f32):
    return jax.ShapeDtypeStruct(tuple(dims), dtype)


def aligned(index, step):
    return pl.multiple_of(index * step, step)


def k_pack_heads(place, w, small, theirs, mine):
    three = w.shape[1]
    half = three // 6
    me_core = lax.axis_index("seq")
    for ref, core in ((mine, me_core), (theirs, 1 - me_core)):
        for which in range(3):
            at = pl.multiple_of((which * 2 + core) * half, half)
            ref[:, which * half : (which + 1) * half] = w[:, pl.ds(at, half)]
        ref[:, 3 * half :] = jnp.zeros((w.shape[0], LANES), b16)
        ref[:SMALL_ROWS, 3 * half :] = small[...]


def k_heads(orders, place, sent, got, x_own, x_other, w_qkv, vectors, first, mixed, small):
    me, core, side = place[0], place[1], place[2]
    blocks, two_rows, lanes = sent.shape
    n = 2 * blocks
    rows = two_rows // 2
    three = w_qkv.shape[1]
    half = three // 3
    for p in range(n):
        block = sent if p < blocks else got
        at = p % blocks
        chip = me ^ spread_of(p, orders, core)
        for c in range(2):
            dev = 2 * chip + (core ^ c)
            part = slice(c * rows, (c + 1) * rows)
            w_qkv[pl.ds(aligned(dev, rows), rows), :] = block[at, part, :three]
            small[dev] = block[at, c * rows : c * rows + SMALL_ROWS, three:].astype(f32)

    def lane_block(first_dev, vector, size):
        total = small[first_dev, vector : vector + 1, :]
        for i in range(1, LANES // size):
            total += pltpu.roll(small[first_dev + i, vector : vector + 1, :], i * size, 1)
        return total

    width = w_qkv.shape[0]
    per = width // (2 * n)
    for row, vector in enumerate((GAIN1, BIAS1, PROJ_B, GAIN2, BIAS2, FC2_B)):
        for q in range(width // LANES):
            vectors[row : row + 1, q * LANES : (q + 1) * LANES] = lane_block(
                q * (LANES // per), vector, per
            )
    for which in range(2):
        for q in range(half // LANES):
            dev = (which * 2 + core) * (half // (2 * per)) + q * (LANES // (2 * per))
            at = which * half + q * LANES
            vectors[6:7, at : at + LANES] = lane_block(dev, QV, 2 * per)
    low = 1 << PAIR
    for b in range(n // 2):
        chip = (b // low) * 2 * low + side * low + b % low
        vectors[7:8, b * LANES : (b + 1) * LANES] = small[2 * chip + core, FC1_B : FC1_B + 1, :]

    images, local, _ = x_own.shape
    for i in range(images):
        for c, ref in enumerate((x_own, x_other)):
            normed, _ = norm_parts(ref[i].astype(f32))
            at = (2 * i + c) * local
            first[at : at + local, :] = (
                normed * vectors[0:1, :] + vectors[1:2, :]
            ).astype(b16)
    for which in range(3):
        part = slice(which * half, (which + 1) * half)
        total = dot(first[...], w_qkv[:, part])
        if which != 1:
            total += vectors[6:7, (which // 2) * half : (which // 2 + 1) * half]
        mixed[:, part] = total.astype(b16)


def k_proj_weight(orders, place, sent, got, sent_far, got_far, w_proj):
    me, core = place[0], place[1]
    blocks, rows, _ = sent.shape
    for c, refs in enumerate(((sent, got), (sent_far, got_far))):
        for p in range(2 * blocks):
            chip = me ^ spread_of(p, orders, core ^ c)
            at = aligned(2 * chip + (core ^ c), rows)
            w_proj[pl.ds(at, rows), :] = refs[p // blocks][p % blocks]


def k_pair_send(place, pair, got, send):
    send[...] = (pair[...] + got[pair.shape[0] :, :].astype(f32)).astype(b16)


def k_output(image, place, middle, own, got, pair_got, vectors, out):
    local = own.shape[0]
    slot = place[1] * local + lax.broadcasted_iota(jnp.int32, (local, 1), 0)
    total = middle[...] + vectors[5:6, :] + own[...]
    total += got[:local, :].astype(f32) + pair_got[...].astype(f32)
    out[...] = jnp.where(slot < BUFFER + place[3 + image], total, 0.0).astype(b16)


def k_unpack_units(orders, place, sent, got, w_fc1, w_fc2):
    me, core = place[0], place[1]
    blocks = sent.shape[0]
    units = LANES
    rows = (sent.shape[1] - units) // 4
    low = 1 << PAIR
    for p in range(2 * blocks):
        block = sent if p < blocks else got
        at = p % blocks
        chip = me ^ spread_of(p, orders, core)
        for c2 in range(2):
            for c in range(2):
                dev = 2 * (chip ^ (c2 << PAIR)) + (core ^ c)
                k = 2 * c2 + c
                w_fc1[pl.ds(aligned(dev, rows), rows), :] = block[at, k * rows : (k + 1) * rows, :]
        short = ((chip >> (PAIR + 1)) << PAIR) + (chip & (low - 1))
        w_fc2[pl.ds(aligned(short, units), units), :] = block[at, 4 * rows :, :]


def live_of(place, image, local, axis):
    dims = (2 * local, 1) if axis == 0 else (1, 2 * local)
    at = lax.broadcasted_iota(jnp.int32, dims, axis)
    core = place[1]
    slot = jnp.where(at < local, at + core * local, at - core * local)
    return slot < BUFFER + place[3 + image]


def k_attend(image, place, q, k, v, own, other):
    local = own.shape[0]
    live = live_of(place, image, local, 1)
    outs = []
    for e in range(2):
        part = slice(e * HEAD_DIM, (e + 1) * HEAD_DIM)
        raw = dot_nt(q[:, part], k[:, part]) * (HEAD_DIM**-0.5)
        raw = jnp.where(live, raw, -1e30)
        expo = jnp.exp(raw - jnp.max(raw, axis=-1, keepdims=True))
        probs = expo * (1.0 / jnp.sum(expo, axis=-1, keepdims=True))
        outs.append(dot(probs.astype(b16), v[:, part]))
    both = jnp.concatenate(outs, axis=1).astype(b16)
    own[...] = both[:local]
    other[...] = both[local:]


def k_attend_back(image, place, q, k, v, g_own, g_other, d_mixed, sums):
    local = g_own.shape[0]
    pairs = pl.num_programs(0)
    live = live_of(place, image, local, 0)
    scale = HEAD_DIM**-0.5
    g = jnp.concatenate([g_own[...], g_other[...]], axis=0)
    parts = ([], [], [])
    for e in range(2):
        part = slice(e * HEAD_DIM, (e + 1) * HEAD_DIM)
        qe, ke, ve, ge = q[:, part], k[:, part], v[:, part], g[:, part]
        raw = jnp.where(live, dot_nt(ke, qe) * scale, -1e30)
        expo = jnp.exp(raw - jnp.max(raw, axis=0, keepdims=True))
        probs = expo * (1.0 / jnp.sum(expo, axis=0, keepdims=True))
        d_probs = dot_nt(ve, ge)
        inner = jnp.sum(probs * d_probs, axis=0, keepdims=True)
        d_scores = (probs * (d_probs - inner)).astype(b16)
        parts[0].append(dot_tn(d_scores, ke) * scale)
        parts[1].append(dot(d_scores, qe) * scale)
        parts[2].append(dot(probs.astype(b16), ge))
    for which in range(3):
        at = pl.multiple_of((which * pairs + pl.program_id(0)) * LANES, LANES)
        value = jnp.concatenate(parts[which], axis=1).astype(b16)
        d_mixed[:, pl.ds(at, LANES)] = value
        total = jnp.sum(value.astype(f32), axis=0, keepdims=True)
        sums[:, pl.ds(at, LANES)] = jnp.broadcast_to(total, (8, LANES))


def k_project(place, att_own, att_got, w, x, vectors, middle, second):
    core = place[1]
    half = att_own.shape[1]
    own = w[pl.ds(aligned(core, half), half), :]
    other = w[pl.ds(aligned(1 - core, half), half), :]
    total = dot(att_own[...], own) + dot(att_got[...], other)
    mid = x[0].astype(f32) + total + vectors[2:3, :]
    middle[...] = mid
    normed, _ = norm_parts(mid)
    second[...] = (normed * vectors[3:4, :] + vectors[4:5, :]).astype(b16)


def k_feed(image, place, s0, s1, s2, s3, u0, u1, u2, u3, w1, w2, vectors,
           act, d_pre, ds_own, ds_pair, ds_other, sums, sec, up):
    local = s0.shape[0]
    tile = 256
    for k, (s, u) in enumerate(((s0, u0), (s1, u1), (s2, u2), (s3, u3))):
        sec[k * local : (k + 1) * local, :] = s[...]
        up[k * local : (k + 1) * local, :] = u[image]
    for at in range(0, w1.shape[1], tile):
        part = slice(at, at + tile)
        pre = dot(sec[...], w1[:, part]) + vectors[7:8, part]
        phi = 0.5 * (1.0 + lax.erf(pre * (0.5**0.5)))
        act[:, part] = (pre * phi).astype(b16)
        slope = phi + pre * jnp.exp(-0.5 * pre * pre) * 0.3989422804014327
        grad = (slope * dot_nt(up[...], w2[part, :])).astype(b16)
        d_pre[:, part] = grad
        total = jnp.sum(grad.astype(f32), axis=0, keepdims=True)
        sums[:, part] = jnp.broadcast_to(total, (8, tile))
    ds_other[...] = dot_nt(d_pre[2 * local :, :], w1[...]).astype(b16)
    ds_pair[...] = dot_nt(d_pre[local : 2 * local, :], w1[...])
    ds_own[...] = dot_nt(d_pre[:local, :], w1[...])


def k_feed_out(place, act, w2, own, pair, other):
    local = own.shape[0]
    other[...] = dot(act[2 * local :, :], w2[...]).astype(b16)
    pair[...] = dot(act[local : 2 * local, :], w2[...])
    own[...] = dot(act[:local, :], w2[...])


def k_middle_back(place, ds_own, ds_got, pair_got, middle, up, w, vectors,
                  d_middle, d_branch, att_own, att_other, sums):
    core = place[1]
    local = ds_own.shape[0]
    half = att_own.shape[1]
    d_second = ds_own[...] + ds_got[:local, :].astype(f32) + pair_got[...].astype(f32)
    normed, scale = norm_parts(middle[...])
    upstream = up[0].astype(f32)
    d_mid = upstream + norm_back(d_second, normed, scale, vectors[3:4, :])
    d_middle[...] = d_mid
    branch = d_mid.astype(b16)
    d_branch[...] = branch
    att_own[...] = dot_nt(branch, w[pl.ds(aligned(core, half), half), :]).astype(b16)
    att_other[...] = dot_nt(branch, w[pl.ds(aligned(1 - core, half), half), :]).astype(b16)
    total = lambda a: jnp.sum(a, axis=0, keepdims=True)
    sums[0:1, :] = total(d_second * normed)
    sums[1:2, :] = total(d_second)
    sums[2:3, :] = total(branch.astype(f32))
    sums[3:4, :] = total(upstream)
    sums[4:, :] = jnp.zeros((4, sums.shape[1]), f32)


def put(send, keep, place_at, rows_at, value, half_count, per):
    @pl.when(place_at >= half_count)
    def _():
        at = pl.multiple_of((place_at - half_count) * per + rows_at, value.shape[0])
        send[pl.ds(at, value.shape[0]), :] = value.astype(b16)

    @pl.when(place_at < half_count)
    def _():
        at = pl.multiple_of(place_at * per + rows_at, value.shape[0])
        keep[pl.ds(at, value.shape[0]), :] = value


def k_grad_heads(orders, n, place, left, r0, r1, send, keep):
    me, core = place[0], place[1]
    step = pl.program_id(0)
    cut = left.shape[0] // 2
    tile = left.shape[1]
    rows = 2 * send.shape[0] // (2 * n)
    total = dot_tn(left[:cut, :], r0[...]) + dot_tn(left[cut:, :], r1[...])
    for i in range(tile // (2 * rows)):
        chip = step * (tile // (2 * rows)) + i
        at = position_of(me ^ chip, orders, core)
        for c in range(2):
            value = total[(2 * i + c) * rows : (2 * i + c + 1) * rows, :]
            put(send, keep, at, (core ^ c) * rows, value, n // 2, 2 * rows)


def k_grad_feed(orders, n, place, a0, a1, u0, u1, s0, s1, d0, d1, send, keep):
    me, core, side = place[0], place[1], place[2]
    low = 1 << PAIR
    tile = 256
    per = 2 * send.shape[0] // (n // 2)
    rows = (per - LANES) // 4
    for step in range(a0.shape[1] // tile):
        part = slice(step * tile, (step + 1) * tile)
        total = dot_tn(a0[:, part], u0[...]) + dot_tn(a1[:, part], u1[...])
        for i in range(tile // LANES):
            b = step * (tile // LANES) + i
            chip = (b // low) * 2 * low + side * low + b % low
            at = position_of(me ^ chip, orders, core)
            put(send, keep, at, 0, total[i * LANES : (i + 1) * LANES, :], n // 4, per)
    for step in range(s0.shape[1] // tile):
        part = slice(step * tile, (step + 1) * tile)
        total = dot_tn(s0[:, part], d0[...]) + dot_tn(s1[:, part], d1[...])
        for i in range(tile // rows):
            dev = step * (tile // rows) + i
            bits = me ^ (dev // 2)
            at = position_of(bits, orders, core)
            inner = LANES + (((bits >> PAIR) & 1) * 2 + (core ^ (i % 2))) * rows
            put(send, keep, at, inner, total[i * rows : (i + 1) * rows, :], n // 4, per)


def k_grad_proj(orders, place, *refs):
    lefts, rights, (send, keep) = (refs[:4], refs[4:8]), refs[8:12], refs[12:]
    me, core = place[0], place[1]
    rows = 32
    right = jnp.concatenate([a[...] for a in rights], axis=0)
    count = lefts[0][0].shape[1] // (2 * rows)
    for which in range(2):
        left = jnp.concatenate([a[...] for a in lefts[which]], axis=0)
        total = dot_tn(left, right)
        for i in range(count):
            chip = (core ^ which) * count + i
            at = position_of(me ^ chip, orders, core)
            value = jnp.where(
                core == 0,
                total[2 * i * rows : (2 * i + 1) * rows, :],
                total[(2 * i + 1) * rows : (2 * i + 2) * rows, :],
            )
            put(send, keep, at, 0, value, count, rows)


def k_first_back(place, d0, d1, w, own, other):
    local = own.shape[1]
    for i, d in enumerate((d0, d1)):
        total = dot_nt(d[...], w[...])
        own[i] = total[:local]
        other[i] = total[local:].astype(b16)


def k_input_back(place, x, own, got, m0, m1, vectors, grad, sums):
    total = lambda a: jnp.sum(a, axis=0, keepdims=True)
    gains = biases = 0.0
    for i, mid in enumerate((m0, m1)):
        normed, scale = norm_parts(x[i].astype(f32))
        d_first = own[i] + got[i].astype(f32)
        grad[i] = mid[...] + norm_back(d_first, normed, scale, vectors[0:1, :])
        gains += total(d_first * normed)
        biases += total(d_first)
    sums[0:1, :] = gains
    sums[1:2, :] = biases
    sums[2:, :] = jnp.zeros((6, sums.shape[1]), f32)


def k_small(orders, n, place, one, mid0, mid1, pre0, pre1, mix0, mix1, mine, theirs, small):
    me, core, side = place[0], place[1], place[2]
    width = one.shape[1]
    per = width // (2 * n)
    half = width // 2
    mids = mid0[...] + mid1[...]
    pres = pre0[...] + pre1[...]
    mixes = mix0[...] + mix1[...]
    small[...] = jnp.zeros(small.shape, f32)
    rows = (
        (GAIN1, one[0:1, :]),
        (BIAS1, one[1:2, :]),
        (GAIN2, mids[0:1, :]),
        (BIAS2, mids[1:2, :]),
        (PROJ_B, mids[2:3, :]),
        (FC2_B, mids[3:4, :]),
    )
    lane = lambda row, q: row[:, q * LANES : (q + 1) * LANES]
    for vector, row in rows:
        for dev in range(2 * n):
            q, i = divmod(dev * per, LANES)
            part = lane(row, q)
            small[dev, vector : vector + 1, :] = part if i == 0 else pltpu.roll(part, LANES - i, 1)
    for which in range(2):
        row = mixes[0:1, 2 * which * half : (2 * which + 1) * half]
        for dev in range(half // (2 * per)):
            q, i = divmod(dev * 2 * per, LANES)
            part = lane(row, q)
            part = part if i == 0 else pltpu.roll(part, LANES - i, 1)
            small[(2 * which + core) * (half // (2 * per)) + dev, QV : QV + 1, :] = part
    low = 1 << PAIR
    for b in range(n // 2):
        chip = (b // low) * 2 * low + side * low + b % low
        small[2 * chip + core, FC1_B : FC1_B + 1, :] = lane(pres[0:1, :], b)
    for p in range(n):
        mine[p] = small[2 * (me ^ spread_of(p, orders, core)) + core]
        theirs[p] = small[2 * (me ^ spread_of(p, orders, 1 - core)) + 1 - core]


def k_rows(place, own, got, out):
    core = place[1]
    half = out.shape[1] // 6
    for which in range(3):
        part = slice(which * half, (which + 1) * half)
        at = pl.multiple_of((2 * which + core) * half, half)
        out[:, pl.ds(at, half)] = own[: out.shape[0], part]
        at = pl.multiple_of((2 * which + 1 - core) * half, half)
        out[:, pl.ds(at, half)] = got[:, part]


def k_columns(place, own, own_pair, got, got_pair, out):
    core, side = place[1], place[2]
    low = 1 << PAIR
    rows = out.shape[0]
    for ref, c, s in (
        (own, core, side),
        (own_pair, core, 1 - side),
        (got, 1 - core, side),
        (got_pair, 1 - core, 1 - side),
    ):
        for b in range(ref.shape[1] // LANES):
            chip = (b // low) * 2 * low + s * low + b % low
            at = pl.multiple_of((2 * chip + c) * LANES, LANES)
            out[:, pl.ds(at, LANES)] = ref[:rows, b * LANES : (b + 1) * LANES]


class Sums:
    def __init__(self, run, send, keep, orders):
        self.run, self.send, self.keep, self.got = run, send, keep, None
        self.steps = list(zip(*orders))[::-1]
        self.step()

    def settle(self):
        got = self.run.now(self.got)
        cut = got.shape[0] // 2
        if cut:
            self.send = (self.keep[cut:] + got[cut:].astype(f32)).astype(self.send.dtype)
            self.keep = self.keep[:cut] + got[:cut].astype(f32)
        else:
            self.keep = self.keep + got.astype(f32)
        self.got = None

    def step(self):
        if self.got is not None:
            self.settle()
        self.got = bit_swap(self.send, self.steps.pop(0))

    def sum(self):
        while self.steps:
            self.step()
        self.settle()
        return self.keep[0]


def fast_body(
    inputs,
    cotangent,
    kept_counts,
    norm1_gain,
    norm1_bias,
    qkv_weight,
    qv_bias,
    proj_weight,
    proj_bias,
    norm2_gain,
    norm2_bias,
    fc1_weight,
    fc1_bias,
    fc2_weight,
    fc2_bias,
):
    images, local, width = inputs.shape
    n = lax.axis_size("img")
    me = lax.axis_index("img")
    core = lax.axis_index("seq")
    levels = n.bit_length() - 1
    half = width // 2
    rows = width // (2 * n)
    units = fc2_weight.shape[0]
    few = n // 2
    hidden = units * few
    side = (me >> PAIR) & 1
    pair = (PAIR, PAIR)
    full = tuple(tuple(range(levels - 1, 1, -1)) + last for last in ((0, 1), (1, 0)))
    most = tuple(tuple(b for b in order if b != PAIR) for order in full)
    last = tuple(order[-2:] + order[:-2] for order in full)
    place = jnp.concatenate([jnp.stack([me, core, side]).astype(jnp.int32), kept_counts])
    run = Order(place)
    on = run.call
    bind = functools.partial
    block = lambda dims, index: pl.BlockSpec(dims, index)
    whole = pl.BlockSpec(memory_space=pltpu.VMEM)

    smalls = (norm1_gain, norm1_bias, qv_bias, proj_bias, norm2_gain, norm2_bias, fc1_bias, fc2_bias)
    small = sum(
        jnp.pad(a[None], ((i, 7 - i), (0, LANES - a.shape[0]))) for i, a in enumerate(smalls)
    )
    packed = shape((rows, 3 * half + LANES), b16)
    theirs, mine = call(k_pack_heads, (packed, packed), (qkv_weight, small), place=kept_counts)
    fc1_mine, fc1_theirs = pack_units(fc1_weight, units, core, side)
    heads = Gather(jnp.concatenate([mine, core_swap(theirs)], axis=0), full)
    fc1_got = core_swap(fc1_theirs)
    x_other = core_swap(inputs)
    slot = core * local + lax.iota(jnp.int32, local)
    row_live = slot[None, :] < BUFFER + kept_counts[:, None]
    up = jnp.where(row_live[:, :, None], cotangent, 0).astype(b16)
    up_other = core_swap(up)
    fc1_send = jnp.concatenate([fc1_mine[1], fc1_got[1]], axis=0)
    proj = Gather(proj_weight, last)

    heads.step()
    heads.held, proj.held, fc1_send, x_other, up_other = tie(
        heads.held, proj.held, fc1_send, x_other, up_other
    )
    heads.step()
    proj.step()
    fc2 = Gather(fc2_weight, most)
    heads.held, proj.held, fc1_send, fc2.held = tie(heads.held, proj.held, fc1_send, fc2.held)
    while len(heads.steps) > 1:
        heads.step()
    proj.step()
    fc1_pair = bit_swap(fc1_send, pair)
    fc2.step()
    fc1 = Gather(jnp.concatenate([fc1_mine[0], fc1_got[0], fc1_pair], axis=0), most)
    heads.held, proj.held, fc1.held, fc2.held = tie(heads.held, proj.held, fc1.held, fc2.held)
    heads.step()
    proj.step()
    fc1.step()
    feed = Gather(None, most)
    feed.steps = fc1.steps
    feed.held = jnp.concatenate([fc1.held, fc2.held], axis=1)
    feed.held, up, heads.got, proj.held = tie(feed.held, up, heads.got, proj.held)
    feed.step()
    proj.step()
    up_pair = bit_swap(up, pair)

    tokens = images * 2 * local
    w_qkv, vectors, first, mixed = on(
        bind(k_heads, full),
        (
            shape((width, 3 * half), b16),
            shape((8, width)),
            shape((tokens, width), b16),
            shape((tokens, 3 * half), b16),
        ),
        (heads.sent, heads.got, inputs, x_other),
        scratch=[pltpu.VMEM((2 * n, SMALL_ROWS, LANES), f32)],
    )
    pairs = half // LANES
    slots = 2 * local
    head_specs = lambda i: [
        block((slots, LANES), lambda h, i=i, f=f: (i, f + h)) for f in (0, pairs, 2 * pairs)
    ]
    lane_spec = block((local, LANES), lambda h: (0, h))
    att_own, att_got, att_other = [], [], []
    for i in range(images):
        own, other = on(
            bind(k_attend, i),
            (shape((local, half), b16),) * 2,
            (mixed, mixed, mixed),
            grid=(pairs,),
            in_specs=head_specs(i),
            out_specs=[lane_spec, lane_spec],
        )
        att_own.append(own)
        att_other.append(other)
        att_got.append(core_swap(other))
        if i == 0:
            proj.got, feed.got = run.now(proj.got, feed.got)
            proj_far = core_swap(proj.sent), core_swap(proj.got)
            feed.held = jnp.concatenate([feed.sent, feed.got], axis=0)
            feed.step()
    w_proj = on(
        bind(k_proj_weight, last),
        shape((width, width), b16),
        (proj.sent, proj.got, *proj_far),
    )
    middle, second = [], []
    for i in range(images):
        mid, sec = on(
            k_project,
            (shape((local, width)), shape((local, width), b16)),
            (att_own[i], att_got[i], w_proj, inputs, vectors),
            grid=(1,),
            in_specs=[whole, whole, whole, block((1, local, width), lambda t, i=i: (i, 0, 0)), whole],
        )
        middle.append(mid)
        second.append((sec, bit_swap(sec, pair), core_swap(sec)))
        if i == 0:
            up_pair = run.now(up_pair)
            up_other_pair = core_swap(up_pair)
    ups = (up, up_pair, up_other, up_other_pair)
    w_fc1, w_fc2 = on(
        bind(k_unpack_units, most),
        (shape((width, hidden), b16), shape((hidden, width), b16)),
        (feed.sent, feed.got),
    )

    tile = 256
    tiles = hidden // tile
    part = shape((local, width))
    other_part = shape((2 * local, width), b16)
    fixed = lambda dims: block(dims, lambda t: (0,) * len(dims))
    feeds, outs, ds_got, ds_sends, out_got = [], [], [], [], []
    send_shape = shape((local, width), b16)
    for i in range(images):
        sec, sec_pair, sec_other = second[i]
        if i == 0:
            sec_pair = run.now(sec_pair)
        second[i] = (sec, sec_pair, sec_other, core_swap(sec_pair))
        feeds.append(
            on(
                bind(k_feed, i),
                (
                    shape((4 * local, hidden), b16),
                    shape((4 * local, hidden), b16),
                    part, part, other_part,
                    shape((8, hidden)),
                    shape((4 * local, width), b16),
                    shape((4 * local, width), b16),
                ),
                second[i] + ups + (w_fc1, w_fc2, vectors),
            )
        )
        ds_got.append(core_swap(feeds[i][4]))
        outs.append(on(k_feed_out, (part, part, other_part), (feeds[i][0], w_fc2)))
        out_got.append(core_swap(outs[i][2]))
        if i == 0:
            sec, sec_pair, sec_other = second[1]
            second[1] = (sec, run.now(sec_pair), sec_other)
        ds_sends.append(on(k_pair_send, send_shape, (feeds[i][3], ds_got[i])))
    pair_got = [bit_swap(s, pair) for s in ds_sends]

    acts = [f[0] for f in feeds]
    d_pres = [f[1] for f in feeds]

    halves = lambda count, cols: (shape((count, cols), b16), shape((count, cols)))
    cut = lambda a, per: a.reshape(-1, per, a.shape[-1])
    feed_send, feed_keep = on(
        bind(k_grad_feed, most, n),
        halves(few // 2 * (4 * rows + units), width),
        (*acts, *[f[7] for f in feeds], *[f[6] for f in feeds], *d_pres),
    )
    grad_feed = Sums(run, cut(feed_send, 4 * rows + units), cut(feed_keep, 4 * rows + units), most)

    d_middle, d_branch, mid_sums, d_mixed, mix_sums, att_grads = [], [], [], [], [], []
    for i in range(images):
        d_mid, branch, own, other, sums = on(
            k_middle_back,
            (part, shape((local, width), b16)) + (shape((local, half), b16),) * 2 + (shape((8, width)),),
            (feeds[i][2], ds_got[i], pair_got[i], middle[i], up, w_proj, vectors),
            grid=(1,),
            in_specs=[whole] * 4 + [block((1, local, width), lambda t, i=i: (i, 0, 0)), whole, whole],
        )
        d_middle.append(d_mid)
        d_branch.append(branch)
        mid_sums.append(sums)
        att_grads.append((own, core_swap(other)))
    def attend_back(i, *wait):
        d, sums = on(
            bind(k_attend_back, i),
            (shape((slots, 3 * half), b16), shape((8, 3 * half))),
            (mixed, mixed, mixed) + att_grads[i],
            grid=(pairs,),
            in_specs=head_specs(i) + [lane_spec, lane_spec],
            out_specs=[fixed((slots, 3 * half)), fixed((8, 3 * half))],
            wait=wait,
        )
        d_mixed.append(d)
        mix_sums.append(sums)

    att_far = [core_swap(a) for a in att_own]
    d_branch_far = [core_swap(b) for b in d_branch]
    attend_back(0)
    grad_feed.step()
    proj_send, proj_keep = on(
        bind(k_grad_proj, full),
        halves(half // 2, width),
        (*att_own, *att_other, *att_got, *att_far, *d_branch, *d_branch_far),
    )
    grad_proj = Sums(run, cut(proj_send, rows), cut(proj_keep, rows), full)
    attend_back(1)
    grad_feed.step()
    qkv_send, qkv_keep = on(
        bind(k_grad_heads, full, n),
        halves(half, 3 * half),
        (first, *d_mixed),
        grid=(width // tile,),
        in_specs=[block((tokens, tile), lambda t: (0, t)), whole, whole],
        out_specs=[fixed((half, 3 * half))] * 2,
    )
    grad_qkv = Sums(run, cut(qkv_send, 2 * rows), cut(qkv_keep, 2 * rows), full)
    grad_proj.step()
    df_own, df_other = on(
        k_first_back,
        (shape(inputs.shape), shape(inputs.shape, b16)),
        (*d_mixed, w_qkv),
    )
    df_got = core_swap(df_other)
    out_sends = [on(k_pair_send, send_shape, (f[1], g)) for f, g in zip(outs, out_got)]
    out_pair = [bit_swap(s, pair) for s in out_sends]
    input_grad, one_sums = on(
        k_input_back,
        (shape(inputs.shape), shape((8, width))),
        (inputs, df_own, df_got, d_middle[0], d_middle[1], vectors),
    )
    small_shape = shape((n, SMALL_ROWS, LANES))
    grad_proj.step()
    small_mine, small_theirs = on(
        bind(k_small, full, n),
        (small_shape, small_shape),
        (one_sums, *mid_sums, feeds[0][5], feeds[1][5], *mix_sums),
        scratch=[pltpu.VMEM((2 * n, SMALL_ROWS, LANES), f32)],
    )
    small_got = core_swap(small_theirs)
    grad_proj.step()
    grad_feed = grad_feed.sum()
    grad_fc2, fc1_own = grad_feed[:units], grad_feed[units:]
    fc1_from = bit_swap(fc1_own[2 * rows :], pair)
    fc1_core = core_swap(fc1_own[rows : 2 * rows])
    small_sum = small_mine + run.now(small_got)
    small_sums = Sums(run, small_sum[few:], small_sum[:few], full)
    grad_qkv.step()
    small_sums.step()
    outputs = [
        on(bind(k_output, i), send_shape, (middle[i], f[0], out_got[i], out_pair[i], vectors))
        for i, f in enumerate(outs)
    ]
    outputs = jnp.stack(outputs)
    fc1_from = run.now(fc1_from)
    fc1_from_core = core_swap(fc1_from[rows:])
    grad_qkv.step()
    small_sums.step()
    fc1_rows = on(
        k_columns, shape(fc1_weight.shape), (fc1_own, fc1_from, fc1_core, fc1_from_core)
    )
    while grad_qkv.steps:
        grad_qkv.step()
        small_sums.step()
    small_sums.settle()

    final = small_sums.keep[0]
    vector_grads = [final[v, : a.shape[0]] for v, a in enumerate(smalls)]
    grad_proj = grad_proj.sum()
    qkv_own = grad_qkv.sum()
    qkv_rows = on(
        k_rows, shape((rows, 6 * half)), (qkv_own, core_swap(qkv_own[rows:]))
    )
    return (
        outputs,
        input_grad,
        vector_grads[GAIN1],
        vector_grads[BIAS1],
        qkv_rows,
        vector_grads[QV],
        grad_proj,
        vector_grads[PROJ_B],
        vector_grads[GAIN2],
        vector_grads[BIAS2],
        fc1_rows,
        vector_grads[FC1_B],
        grad_fc2,
        vector_grads[FC2_B],
    )


def body(*args):
    whole_tiles = args[3].shape[0] % 32 == 0 and args[12].shape[0] == LANES
    return (fast_body if whole_tiles else plain_body)(*args)


def solution(mesh):
    row = P(("img", "seq"))
    mat = P(("img", "seq"), None)
    act = P("img", "seq", None)
    return jax.shard_map(
        body,
        mesh=mesh,
        in_specs=(act, act, P("img"), row, row, mat, row, mat, row, row, row, mat, row, mat, row),
        out_specs=(act, act, row, row, mat, row, mat, row, row, row, mat, row, mat, row),
        check_vma=False,
    )
```

profile of v0, /device:TPU:0, one launch (start us, length us, event | category | flops | bytes accessed | tf_op | source)
XLA Modules:
  0.0 337.0 jit_solution(8831292038768321633)
XLA Ops:
  9.4 3.9 %collective-permute-start.1 = (bf16[1,64,1664]{2,1,0:T(8,128)(2,1)S(1)}, bf16[1,64,1664]{2,1,0:T(8,128)(2,1)S(1)}, u32[]{:S(2)}, u32[]{:S(2)}) collective-permute-start(bf16[1,64,1664]{2,1,0:T(8,128)(2,1)S(1)} %maximum_bitcast_fusion.1), channel_id=1, source_target_pairs={{0,16},{1,17},{2,18},{3,19},{4,20},{5,21},{6,22},{7,23},{8,24},{9,... | collective-permute-start | bytes 638984 | tf_op jit(solution)/shard_map/ppermute | solution.py:55
  13.4 10.2 %collective-permute-done.1 = bf16[1,64,1664]{2,1,0:T(8,128)(2,1)S(1)} collective-permute-done((bf16[1,64,1664]{2,1,0:T(8,128)(2,1)S(1)}, bf16[1,64,1664]{2,1,0:T(8,128)(2,1)S(1)}, u32[]{:S(2)}, u32[]{:S(2)}) %collective-permute-start.1) | collective-permute-done | bytes 213024 | tf_op jit(solution)/shard_map/ppermute | solution.py:55
  25.9 2.8 collective-permute-done.6
  28.7 6.4 %collective-permute-done.5 = bf16[2,64,1664]{2,1,0:T(8,128)(2,1)S(1)} collective-permute-done((bf16[2,64,1664]{2,1,0:T(8,128)(2,1)S(1)}, bf16[2,64,1664]{2,1,0:T(8,128)(2,1)S(1)}, u32[]{:S(2)}, u32[]{:S(2)}) %collective-permute-start.5) | collective-permute-done | bytes 426016 | tf_op jit(solution)/shard_map/ppermute | solution.py:55
  38.1 2.9 collective-permute-start.10
  43.0 5.5 %collective-permute-done.9 = bf16[64,1024]{1,0:T(8,128)(2,1)S(1)} collective-permute-done((bf16[64,1024]{1,0:T(8,128)(2,1)S(1)}, bf16[64,1024]{1,0:T(8,128)(2,1)S(1)}, u32[]{:S(2)}, u32[]{:S(2)}) %collective-permute-start.9) | collective-permute-done | bytes 131104 | tf_op jit(solution)/shard_map/ppermute | solution.py:55
  48.6 3.5 %collective-permute-done.10 = bf16[1,128,1024]{2,1,0:T(8,128)(2,1)S(1)} collective-permute-done((bf16[1,128,1024]{2,1,0:T(8,128)(2,1)S(1)}, bf16[1,128,1024]{2,1,0:T(8,128)(2,1)S(1)}, u32[]{:S(2)}, u32[]{:S(2)}) %collective-permute-start.10) | collective-permute-done | bytes 262176 | tf_op jit(solution)/shard_map/ppermute | solution.py:55
  52.9 2.9 collective-permute-start.11
  55.8 18.2 %collective-permute-done.13 = bf16[4,32,1024]{2,1,0:T(8,128)(2,1)S(1)} collective-permute-done((bf16[4,32,1024]{2,1,0:T(8,128)(2,1)S(1)}, bf16[4,32,1024]{2,1,0:T(8,128)(2,1)S(1)}, u32[]{:S(2)}, u32[]{:S(2)}) %collective-permute-start.13) | collective-permute-done | bytes 262176 | tf_op jit(solution)/shard_map/ppermute | solution.py:55
  74.0 3.7 %collective-permute-done.11 = bf16[1,128,1024]{2,1,0:T(8,128)(2,1)S(1)} collective-permute-done((bf16[1,128,1024]{2,1,0:T(8,128)(2,1)S(1)}, bf16[1,128,1024]{2,1,0:T(8,128)(2,1)S(1)}, u32[]{:S(2)}, u32[]{:S(2)}) %collective-permute-start.11) | collective-permute-done | bytes 262176 | tf_op jit(solution)/shard_map/ppermute | solution.py:55
  80.0 6.9 %shard_map.256 = (bf16[1024,1536]{1,0:T(8,128)(2,1)}, f32[8,1024]{1,0:T(8,128)}, bf16[640,1024]{1,0:T(8,128)(2,1)}, bf16[640,1536]{1,0:T(8,128)(2,1)}) custom-call(s32[5]{0:T(128)} %pad_add_fusion.1.place.refs_0_, bf16[8,64,1664]{2,1,0:T(8,128)(2,1)} %copy-done.2, bf16[8,64,1664]{2,1,0:T(8,128)(2,1)} %collective-permute-done.12.got, ...), custom_call_target="tpu_custom_call" | custom-call | flops 3500000000 | bytes 1000 | tf_op jit(solution)/shard_map/pallas_call | solution.py:567
  86.9 6.1 %shard_map.257 = (bf16[160,512]{1,0:T(8,128)(2,1)}, bf16[160,512]{1,0:T(8,128)(2,1)}) custom-call(s32[5]{0:T(128)} %pad_add_fusion.1.place.refs_0_, bf16[640,1536]{1,0:T(8,128)(2,1)} %get-tuple-element.157.refs_1_.refs_2_.refs_3_, bf16[640,1536]{1,0:T(8,128)(2,1)} %get-tuple-element.157.refs_1_.refs_2_.refs_3_, ...), custom_call_target="tpu_custom_call" | custom-call | flops 3000000000 | bytes 1000 | tf_op jit(solution)/shard_map/pallas_call | solution.py:567
  96.3 6.2 %shard_map.258 = (bf16[160,512]{1,0:T(8,128)(2,1)}, bf16[160,512]{1,0:T(8,128)(2,1)}) custom-call(s32[5]{0:T(128)} %pad_add_fusion.1.place.refs_0_, bf16[640,1536]{1,0:T(8,128)(2,1)} %get-tuple-element.157.refs_1_.refs_2_.refs_3_, bf16[640,1536]{1,0:T(8,128)(2,1)} %get-tuple-element.157.refs_1_.refs_2_.refs_3_, ...), custom_call_target="tpu_custom_call" | custom-call | flops 3000000000 | bytes 1000 | tf_op jit(solution)/shard_map/pallas_call | solution.py:567
  103.9 3.0 shard_map.259.refs_3_.refs_6_
  107.6 3.4 shard_map.260
  112.2 3.4 shard_map.261
  115.6 3.7 %collective-permute-done.20.refs_2_ = bf16[4,256,1024]{2,1,0:T(8,128)(2,1)S(1)} collective-permute-done((bf16[4,256,1024]{2,1,0:T(8,128)(2,1)S(1)}, bf16[4,256,1024]{2,1,0:T(8,128)(2,1)S(1)}, u32[]{:S(2)}, u32[]{:S(2)}) %collective-permute-start.20) | collective-permute-done | bytes 2097184 | tf_op jit(solution)/shard_map/ppermute | solution.py:55
  120.6 4.5 %shard_map.262 = (bf16[1024,1024]{1,0:T(8,128)(2,1)}, bf16[1024,1024]{1,0:T(8,128)(2,1)}) custom-call(s32[5]{0:T(128)} %pad_add_fusion.1.place.refs_0_, bf16[4,256,1024]{2,1,0:T(8,128)(2,1)} %copy-done.9, bf16[4,256,1024]{2,1,0:T(8,128)(2,1)} %copy-done.18, f32[160,1024]{1,0:T(8,128)} %get-tuple-element.172.refs_3_.refs_4_.refs_1_), custom_call_target="tpu_custom_call" | custom-call | flops 2249999872 | bytes 1000 | tf_op jit(solution)/shard_map/pallas_call | solution.py:567
  127.4 10.2 %shard_map.263 = (bf16[640,1024]{1,0:T(8,128)(2,1)}, bf16[640,1024]{1,0:T(8,128)(2,1)}, f32[160,1024]{1,0:T(8,128)}, f32[160,1024]{1,0:T(8,128)}, bf16[320,1024]...) custom-call(s32[5]{0:T(128)} %pad_add_fusion.1.place.refs_0_, ...), custom_call_target="tpu_custom_call" | custom-call | flops 10000000000 | bytes 1000 | tf_op jit(solution)/shard_map/pallas_call | solution.py:567
  139.9 4.5 %shard_map.264 = (f32[160,1024]{1,0:T(8,128)}, f32[160,1024]{1,0:T(8,128)}, bf16[320,1024]{1,0:T(8,128)(2,1)}) custom-call(s32[5]{0:T(128)} %pad_add_fusion.1.place.refs_0_, bf16[640,1024]{1,0:T(8,128)(2,1)} %get-tuple-element.179.refs_1_, bf16[1024,1024]{1,0:T(8,128)(2,1)} %get-tuple-element.177.refs_10_.refs_2_, f32[8,1024]{1,0:T(8,128)} %get-tuple-element.180.refs_3_.refs_4_), custom_call_target="tpu_custom_call" | custom-call | flops 3000000000 | bytes 1000 | tf_op jit(solution)/shard_map/pallas_call | solution.py:567
  144.4 3.7 %collective-permute-done.28.refs_2_ = bf16[160,1024]{1,0:T(8,128)(2,1)S(1)} collective-permute-done((bf16[160,1024]{1,0:T(8,128)(2,1)S(1)}, bf16[160,1024]{1,0:T(8,128)(2,1)S(1)}, u32[]{:S(2)}, u32[]{:S(2)}) %collective-permute-start.28) | collective-permute-done | bytes 327712 | tf_op jit(solution)/shard_map/ppermute | solution.py:55
  149.0 2.1 shard_map.265.refs_12_
  152.5 10.3 %shard_map.266 = (bf16[640,1024]{1,0:T(8,128)(2,1)}, bf16[640,1024]{1,0:T(8,128)(2,1)}, f32[160,1024]{1,0:T(8,128)}, f32[160,1024]{1,0:T(8,128)}, bf16[320,1024]...) custom-call(s32[5]{0:T(128)} %pad_add_fusion.1.place.refs_0_, ...), custom_call_target="tpu_custom_call" | custom-call | flops 10000000000 | bytes 1000 | tf_op jit(solution)/shard_map/pallas_call | solution.py:567
  163.4 4.5 %shard_map.267 = (f32[160,1024]{1,0:T(8,128)}, f32[160,1024]{1,0:T(8,128)}, bf16[320,1024]{1,0:T(8,128)(2,1)}) custom-call(s32[5]{0:T(128)} %pad_add_fusion.1.place.refs_0_, bf16[640,1024]{1,0:T(8,128)(2,1)} %get-tuple-element.190.refs_1_.refs_2_, bf16[1024,1024]{1,0:T(8,128)(2,1)} %get-tuple-element.177.refs_10_.refs_2_, ...), custom_call_target="tpu_custom_call" | custom-call | flops 3000000000 | bytes 1000 | tf_op jit(solution)/shard_map/pallas_call | solution.py:567
  168.7 2.1 shard_map.268.refs_9_
  170.8 15.9 %shard_map.269 = (bf16[1024,1024]{1,0:T(8,128)(2,1)}, f32[1024,1024]{1,0:T(8,128)}) custom-call(s32[5]{0:T(128)} %pad_add_fusion.1.place.refs_0_, bf16[640,1024]{1,0:T(8,128)(2,1)} %get-tuple-element.179.refs_1_, bf16[640,1024]{1,0:T(8,128)(2,1)} %get-tuple-element.190.refs_1_.refs_2_, bf16[640,1024]{1,0:T(8,128)(2,1)} %get-tuple-element.191.refs_3_, ...), custom_call_target="tpu_custom_call" | custom-call | flops 7500000256 | bytes 1000 | tf_op jit(solution)/shard_map/pallas_call | solution.py:567
  189.8 8.0 %collective-permute-done.29.refs_3_ = bf16[160,1024]{1,0:T(8,128)(2,1)S(1)} collective-permute-done((bf16[160,1024]{1,0:T(8,128)(2,1)S(1)}, bf16[160,1024]{1,0:T(8,128)(2,1)S(1)}, u32[]{:S(2)}, u32[]{:S(2)}) %collective-permute-start.29) | collective-permute-done | bytes 327712 | tf_op jit(solution)/shard_map/ppermute | solution.py:55
  198.5 4.3 %shard_map.270 = (f32[160,1024]{1,0:T(8,128)}, bf16[160,1024]{1,0:T(8,128)(2,1)}, bf16[160,512]{1,0:T(8,128)(2,1)}, bf16[160,512]{1,0:T(8,128)(2,1)}, f32[8,1024]{1,0:T(8,128)}) custom-call(s32[5]{0:T(128)} %pad_add_fusion.1.place.refs_0_, f32[160,1024]{1,0:T(8,128)} %get-tuple-element.184.refs_1_, bf16[320,1024]{1,0:T(8,128)(2,1)} %copy-done.23, ...), custom_call_target="tpu_custom_call" | custom-call | flops 2200000000 | bytes 1000 | tf_op jit(solution)/shard_map/pallas_call | solution.py:567
  202.9 2.8 fusion.10
  206.4 4.3 %shard_map.271 = (f32[160,1024]{1,0:T(8,128)}, bf16[160,1024]{1,0:T(8,128)(2,1)}, bf16[160,512]{1,0:T(8,128)(2,1)}, bf16[160,512]{1,0:T(8,128)(2,1)}, f32[8,1024]{1,0:T(8,128)}) custom-call(s32[5]{0:T(128)} %pad_add_fusion.1.place.refs_0_, f32[160,1024]{1,0:T(8,128)} %get-tuple-element.204.refs_1_, bf16[320,1024]{1,0:T(8,128)(2,1)} %copy-done.25, ...), custom_call_target="tpu_custom_call" | custom-call | flops 2200000000 | bytes 1000 | tf_op jit(solution)/shard_map/pallas_call | solution.py:567
  211.4 8.3 %shard_map.272 = (bf16[320,1536]{1,0:T(8,128)(2,1)}, f32[8,1536]{1,0:T(8,128)}) custom-call(s32[5]{0:T(128)} %pad_add_fusion.1.place.refs_0_, bf16[640,1536]{1,0:T(8,128)(2,1)} %get-tuple-element.157.refs_1_.refs_2_.refs_3_, bf16[640,1536]{1,0:T(8,128)(2,1)} %get-tuple-element.157.refs_1_.refs_2_.refs_3_, ...), custom_call_target="tpu_custom_call" | custom-call | flops 4150000128 | bytes 1000 | tf_op jit(solution)/shard_map/pallas_call | solution.py:567
  221.0 2.4 convert_add_fusion
  226.7 5.5 %shard_map.273 = (bf16[256,1024]{1,0:T(8,128)(2,1)}, f32[256,1024]{1,0:T(8,128)}) custom-call(s32[5]{0:T(128)} %pad_add_fusion.1.place.refs_0_, bf16[160,512]{1,0:T(8,128)(2,1)} %get-tuple-element.164.refs_4_.refs_1_, bf16[160,512]{1,0:T(8,128)(2,1)} %get-tuple-element.165.refs_5_.refs_1_.refs_2_, bf16[160,512]{1,0:T(8,128)(2,1)} %get-tuple-element.160.refs_3_, ...), custom_call_target="tpu_custom_call" | custom-call | flops 2750000128 | bytes 1000 | tf_op jit(solution)/shard_map/pallas_call | solution.py:567
  233.9 8.4 %shard_map.274 = (bf16[320,1536]{1,0:T(8,128)(2,1)}, f32[8,1536]{1,0:T(8,128)}) custom-call(s32[5]{0:T(128)} %pad_add_fusion.1.place.refs_0_, bf16[640,1536]{1,0:T(8,128)(2,1)} %get-tuple-element.157.refs_1_.refs_2_.refs_3_, bf16[640,1536]{1,0:T(8,128)(2,1)} %get-tuple-element.157.refs_1_.refs_2_.refs_3_, ...), custom_call_target="tpu_custom_call" | custom-call | flops 4150000128 | bytes 1000 | tf_op jit(solution)/shard_map/pallas_call | solution.py:567
  242.3 8.9 %shard_map.275 = (bf16[512,1536]{1,0:T(8,128)(2,1)}, f32[512,1536]{1,0:T(8,128)}) custom-call(s32[5]{0:T(128)} %pad_add_fusion.1.place.refs_0_, bf16[640,1024]{1,0:T(8,128)(2,1)} %get-tuple-element.217.refs_1_, bf16[320,1536]{1,0:T(8,128)(2,1)} %get-tuple-element.207.refs_2_.refs_1_, bf16[320,1536]{1,0:T(8,128)(2,1)} %get-tuple-element.215.refs_3_.refs_2_, ...), custom_call_target="tpu_custom_call" | custom-call | flops 4350000128 | bytes 1000 | tf_op jit(solution)/shard_map/pallas_call | solution.py:567
  251.3 5.9 %shard_map.276 = (f32[2,160,1024]{2,1,0:T(8,128)}, bf16[2,160,1024]{2,1,0:T(8,128)(2,1)}) custom-call(s32[5]{0:T(128)} %pad_add_fusion.1.place.refs_0_, bf16[320,1536]{1,0:T(8,128)(2,1)} %get-tuple-element.207.refs_2_.refs_1_, bf16[320,1536]{1,0:T(8,128)(2,1)} %get-tuple-element.215.refs_3_.refs_2_, bf16[1024,1536]{1,0:T(8,128)(2,1)} %get-tuple-element.216.refs_3_, ...), custom_call_target="tpu_custom_call" | custom-call | flops 3000000000 | bytes 1000 | tf_op jit(solution)/shard_map/pallas_call | solution.py:567
  257.3 2.1 shard_map.277.refs_3_
  260.2 2.1 shard_map.278.refs_7_
  268.3 4.2 %shard_map.279 = (f32[2,160,1024]{2,1,0:T(8,128)}, f32[8,1024]{1,0:T(8,128)}) custom-call(s32[5]{0:T(128)} %pad_add_fusion.1.place.refs_0_, bf16[2,160,1024]{2,1,0:T(8,128)(2,1)} %refs_1_.1, f32[2,160,1024]{2,1,0:T(8,128)} %get-tuple-element.224.refs_3_.refs_2_, bf16[2,160,1024]{2,1,0:T(8,128)(2,1)} %copy-done.26, f32[160,1024]{1,0:T(8,128)} %get-tuple-element.226.refs_4_, ...), custom_call_target="tpu_custom_call" | custom-call | flops 2150000128 | bytes 1000 | tf_op jit(solution)/shard_map/pallas_call | solution.py:567
  277.3 8.4 %collective-permute-done.49 = bf16[2,32,1024]{2,1,0:T(8,128)(2,1)S(1)} collective-permute-done((bf16[2,32,1024]{2,1,0:T(8,128)(2,1)S(1)}, bf16[2,32,1024]{2,1,0:T(8,128)(2,1)S(1)}, u32[]{:S(2)}, u32[]{:S(2)}) %collective-permute-start.49) | collective-permute-done | bytes 131104 | tf_op jit(solution)/shard_map/ppermute | solution.py:55
  285.7 2.5 collective-permute-start.43
  288.2 4.7 %collective-permute-done.48 = bf16[1,256,1024]{2,1,0:T(8,128)(2,1)S(1)} collective-permute-done((bf16[1,256,1024]{2,1,0:T(8,128)(2,1)}, bf16[1,256,1024]{2,1,0:T(8,128)(2,1)S(1)}, u32[]{:S(2)}, u32[]{:S(2)}) %collective-permute-start.48) | collective-permute-done | bytes 524320 | tf_op jit(solution)/shard_map/ppermute | solution.py:55
  296.8 2.7 collective-permute-done.50
  300.6 2.5 shard_map.281.refs_6_
  304.5 2.5 shard_map.282.refs_5_
  313.1 5.9 %collective-permute-done.57 = bf16[2,64,1536]{2,1,0:T(8,128)(2,1)S(1)} collective-permute-done((bf16[2,64,1536]{2,1,0:T(8,128)(2,1)S(1)}, bf16[2,64,1536]{2,1,0:T(8,128)(2,1)S(1)}, u32[]{:S(2)}, u32[]{:S(2)}) %collective-permute-start.57) | collective-permute-done | bytes 393248 | tf_op jit(solution)/shard_map/ppermute | solution.py:55
  319.1 2.3 collective-permute-start.60
  325.3 7.4 %collective-permute-done.61 = bf16[1,64,1536]{2,1,0:T(8,128)(2,1)S(1)} collective-permute-done((bf16[1,64,1536]{2,1,0:T(8,128)(2,1)S(1)}, bf16[1,64,1536]{2,1,0:T(8,128)(2,1)S(1)}, u32[]{:S(2)}, u32[]{:S(2)}) %collective-permute-start.61) | collective-permute-done | bytes 196640 | tf_op jit(solution)/shard_map/ppermute | solution.py:55
  (274 shorter events, 79.0 us)
Async XLA Ops:
  6.6 17.0 %collective-permute-start.3 = (bf16[2,160,1024]{2,1,0:T(8,128)(2,1)S(1)}, bf16[2,160,1024]{2,1,0:T(8,128)(2,1)}, u32[]{:S(2)}, u32[]{:S(2)}) collective-permute-start(bf16[2,160,1024]{2,1,0:T(8,128)(2,1)S(1)} %copy-done.19), channel_id=1, source_target_pairs={{0,1},{1,0},{2,3},{3,2},{4,5},{5,4},{6,7},{7,6},{8,9},{9,8},{10,11... | collective-permute-start | bytes 1966088 | tf_op jit(solution)/shard_map/ppermute | solution.py:47
  7.3 16.3 %collective-permute-start.4 = (bf16[2,160,1024]{2,1,0:T(8,128)(2,1)S(1)}, bf16[2,160,1024]{2,1,0:T(8,128)(2,1)S(1)}, u32[]{:S(2)}, u32[]{:S(2)}) collective-permute-start(bf16[2,160,1024]{2,1,0:T(8,128)(2,1)S(1)} %broadcast_select_fusion.refs_5_), channel_id=1, source_target_pairs={{0,1},{1,0},{2,3},{3,2},{4,5},{5,4},{6,7},{7,6},{8,9},{9,8},{10,11... | collective-permute-start | bytes 1966088 | tf_op jit(solution)/shard_map/ppermute | solution.py:47
  9.4 14.1 %collective-permute-start.1 = (bf16[1,64,1664]{2,1,0:T(8,128)(2,1)S(1)}, bf16[1,64,1664]{2,1,0:T(8,128)(2,1)S(1)}, u32[]{:S(2)}, u32[]{:S(2)}) collective-permute-start(bf16[1,64,1664]{2,1,0:T(8,128)(2,1)S(1)} %maximum_bitcast_fusion.1), channel_id=1, source_target_pairs={{0,16},{1,17},{2,18},{3,19},{4,20},{5,21},{6,22},{7,23},{8,24},{9,... | collective-permute-start | bytes 638984 | tf_op jit(solution)/shard_map/ppermute | solution.py:55
  23.6 11.5 %collective-permute-start.5 = (bf16[2,64,1664]{2,1,0:T(8,128)(2,1)S(1)}, bf16[2,64,1664]{2,1,0:T(8,128)(2,1)S(1)}, u32[]{:S(2)}, u32[]{:S(2)}) collective-permute-start(bf16[2,64,1664]{2,1,0:T(8,128)(2,1)S(1)} %pad_maximum_fusion.6), channel_id=1, source_target_pairs={{0,8},{1,9},{2,10},{3,11},{4,12},{5,13},{6,14},{7,15},{8,0},{9,1},... | collective-permute-start | bytes 1277960 | tf_op jit(solution)/shard_map/ppermute | solution.py:55
  35.2 16.8 %collective-permute-start.7 = (bf16[4,64,1664]{2,1,0:T(8,128)(2,1)S(1)}, bf16[4,64,1664]{2,1,0:T(8,128)(2,1)S(1)}, u32[]{:S(2)}, u32[]{:S(2)}) collective-permute-start(bf16[4,64,1664]{2,1,0:T(8,128)(2,1)S(1)} %pad_maximum_fusion.2), channel_id=1, source_target_pairs={{0,2},{1,5},{2,0},{3,7},{4,6},{5,1},{6,4},{7,3},{8,10},{9,13},{10,... | collective-permute-start | bytes 2555912 | tf_op jit(solution)/shard_map/ppermute | solution.py:55
  38.1 14.0 %collective-permute-start.10 = (bf16[1,128,1024]{2,1,0:T(8,128)(2,1)S(1)}, bf16[1,128,1024]{2,1,0:T(8,128)(2,1)S(1)}, u32[]{:S(2)}, u32[]{:S(2)}) collective-permute-start(bf16[1,128,1024]{2,1,0:T(8,128)(2,1)S(1)} %bitcast.75), channel_id=1, source_target_pairs={{0,16},{1,17},{2,18},{3,19},{4,20},{5,21},{6,22},{7,23},{8,24},{9,... | collective-permute-start | bytes 786440 | tf_op jit(solution)/shard_map/ppermute | solution.py:55
  52.3 25.4 %collective-permute-start.12 = (bf16[8,64,1664]{2,1,0:T(8,128)(2,1)S(1)}, bf16[8,64,1664]{2,1,0:T(8,128)(2,1)}, u32[]{:S(2)}, u32[]{:S(2)}) collective-permute-start(bf16[8,64,1664]{2,1,0:T(8,128)(2,1)S(1)} %pad_maximum_fusion.sent), channel_id=1, source_target_pairs={{0,4},{1,3},{2,6},{3,1},{4,0},{5,7},{6,2},{7,5},{8,12},{9,11},{10,... | collective-permute-start | bytes 5111816 | tf_op jit(solution)/shard_map/ppermute | solution.py:55
  52.9 21.1 %collective-permute-start.13 = (bf16[4,32,1024]{2,1,0:T(8,128)(2,1)S(1)}, bf16[4,32,1024]{2,1,0:T(8,128)(2,1)S(1)}, u32[]{:S(2)}, u32[]{:S(2)}) collective-permute-start(bf16[4,32,1024]{2,1,0:T(8,128)(2,1)S(1)} %pad_maximum_fusion.7), channel_id=1, source_target_pairs={{0,16},{1,17},{2,18},{3,19},{4,20},{5,21},{6,22},{7,23},{8,24},{9,... | collective-permute-start | bytes 786440 | tf_op jit(solution)/shard_map/ppermute | solution.py:55
  52.9 24.8 %collective-permute-start.11 = (bf16[1,128,1024]{2,1,0:T(8,128)(2,1)S(1)}, bf16[1,128,1024]{2,1,0:T(8,128)(2,1)S(1)}, u32[]{:S(2)}, u32[]{:S(2)}) collective-permute-start(bf16[1,128,1024]{2,1,0:T(8,128)(2,1)S(1)} %maximum_bitcast_fusion), channel_id=1, source_target_pairs={{0,16},{1,17},{2,18},{3,19},{4,20},{5,21},{6,22},{7,23},{8,24},{9,... | collective-permute-start | bytes 786440 | tf_op jit(solution)/shard_map/ppermute | solution.py:55
  77.8 15.3 %collective-permute-start.16 = (bf16[2,256,1024]{2,1,0:T(8,128)(2,1)S(1)}, bf16[2,256,1024]{2,1,0:T(8,128)(2,1)S(1)}, u32[]{:S(2)}, u32[]{:S(2)}) collective-permute-start(bf16[2,256,1024]{2,1,0:T(8,128)(2,1)S(1)} %pad_maximum_fusion.1), channel_id=1, source_target_pairs={{0,2},{1,5},{2,0},{3,7},{4,6},{5,1},{6,4},{7,3},{8,10},{9,13},{10,... | collective-permute-start | bytes 3145736 | tf_op jit(solution)/shard_map/ppermute | solution.py:55
  79.9 13.1 %collective-permute-start.15 = (bf16[8,32,1024]{2,1,0:T(8,128)(2,1)S(1)}, bf16[8,32,1024]{2,1,0:T(8,128)(2,1)S(1)}, u32[]{:S(2)}, u32[]{:S(2)}) collective-permute-start(bf16[8,32,1024]{2,1,0:T(8,128)(2,1)S(1)} %pad_maximum_fusion.5.refs_1_), channel_id=1, source_target_pairs={{0,8},{1,9},{2,10},{3,11},{4,12},{5,13},{6,14},{7,15},{8,0},{9,1},... | collective-permute-start | bytes 1572872 | tf_op jit(solution)/shard_map/ppermute | solution.py:55
  93.2 26.1 %collective-permute-start.20 = (bf16[4,256,1024]{2,1,0:T(8,128)(2,1)S(1)}, bf16[4,256,1024]{2,1,0:T(8,128)(2,1)S(1)}, u32[]{:S(2)}, u32[]{:S(2)}) collective-permute-start(bf16[4,256,1024]{2,1,0:T(8,128)(2,1)S(1)} %constant_dynamic-update-slice_fusion.refs_1_), channel_id=1, source_target_pairs={{0,4},{1,3},{2,6},{3,1},{4,0},{5,7},{6,2},{7,5},{8,12},{9,11},{10,... | collective-permute-start | bytes 6291464 | tf_op jit(solution)/shard_map/ppermute | solution.py:55
  93.7 8.8 %collective-permute-start.17 = (bf16[8,32,1024]{2,1,0:T(8,128)(2,1)S(1)}, bf16[8,32,1024]{2,1,0:T(8,128)(2,1)S(1)}, u32[]{:S(2)}, u32[]{:S(2)}) collective-permute-start(bf16[8,32,1024]{2,1,0:T(8,128)(2,1)S(1)} %pad_maximum_fusion.5.refs_1_), channel_id=1, source_target_pairs={{0,1},{1,0},{2,3},{3,2},{4,5},{5,4},{6,7},{7,6},{8,9},{9,8},{10,11... | collective-permute-start | bytes 1572872 | tf_op jit(solution)/shard_map/ppermute | solution.py:47
  93.7 9.4 %collective-permute-start.18 = (bf16[8,32,1024]{2,1,0:T(8,128)(2,1)S(1)}, bf16[8,32,1024]{2,1,0:T(8,128)(2,1)S(1)}, u32[]{:S(2)}, u32[]{:S(2)}) collective-permute-start(bf16[8,32,1024]{2,1,0:T(8,128)(2,1)S(1)} %collective-permute-done.15.refs_2_), channel_id=1, source_target_pairs={{0,1},{1,0},{2,3},{3,2},{4,5},{5,4},{6,7},{7,6},{8,9},{9,8},{10,11... | collective-permute-start | bytes 1572872 | tf_op jit(solution)/shard_map/ppermute | solution.py:47
  94.3 16.9 %collective-permute-start.22 = (bf16[2,160,1024]{2,1,0:T(8,128)(2,1)S(1)}, bf16[2,160,1024]{2,1,0:T(8,128)(2,1)S(1)}, u32[]{:S(2)}, u32[]{:S(2)}) collective-permute-start(bf16[2,160,1024]{2,1,0:T(8,128)(2,1)S(1)} %broadcast_select_fusion.refs_5_), channel_id=1, source_target_pairs={{0,8},{1,9},{2,10},{3,11},{4,12},{5,13},{6,14},{7,15},{8,0},{9,1},... | collective-permute-start | bytes 1966088 | tf_op jit(solution)/shard_map/ppermute | solution.py:55
  96.3 10.7 %collective-permute-start.14 = (bf16[160,512]{1,0:T(8,128)(2,1)S(1)}, bf16[160,512]{1,0:T(8,128)(2,1)S(1)}, u32[]{:S(2)}, u32[]{:S(2)}) collective-permute-start(bf16[160,512]{1,0:T(8,128)(2,1)S(1)} %copy-done.46), channel_id=1, source_target_pairs={{0,1},{1,0},{2,3},{3,2},{4,5},{5,4},{6,7},{7,6},{8,9},{9,8},{10,11... | collective-permute-start | bytes 491528 | tf_op jit(solution)/shard_map/ppermute | solution.py:47
  102.6 9.0 %collective-permute-start.21 = (bf16[160,512]{1,0:T(8,128)(2,1)}, bf16[160,512]{1,0:T(8,128)(2,1)S(1)}, u32[]{:S(2)}, u32[]{:S(2)}) collective-permute-start(bf16[160,512]{1,0:T(8,128)(2,1)} %get-tuple-element.169.refs_4_), channel_id=1, source_target_pairs={{0,1},{1,0},{2,3},{3,2},{4,5},{5,4},{6,7},{7,6},{8,9},{9,8},{10,11... | collective-permute-start | bytes 491528 | tf_op jit(solution)/shard_map/ppermute | solution.py:47
  111.0 14.1 %collective-permute-start.19 = (bf16[160,1024]{1,0:T(8,128)(2,1)}, bf16[160,1024]{1,0:T(8,128)(2,1)S(1)}, u32[]{:S(2)}, u32[]{:S(2)}) collective-permute-start(bf16[160,1024]{1,0:T(8,128)(2,1)} %get-tuple-element.167.refs_1_), channel_id=1, source_target_pairs={{0,8},{1,9},{2,10},{3,11},{4,12},{5,13},{6,14},{7,15},{8,0},{9,1},... | collective-permute-start | bytes 983048 | tf_op jit(solution)/shard_map/ppermute | solution.py:55
  111.0 14.1 %collective-permute-start.23 = (bf16[160,1024]{1,0:T(8,128)(2,1)}, bf16[160,1024]{1,0:T(8,128)(2,1)S(1)}, u32[]{:S(2)}, u32[]{:S(2)}) collective-permute-start(bf16[160,1024]{1,0:T(8,128)(2,1)} %get-tuple-element.167.refs_1_), channel_id=1, source_target_pairs={{0,1},{1,0},{2,3},{3,2},{4,5},{5,4},{6,7},{7,6},{8,9},{9,8},{10,11... | collective-permute-start | bytes 983048 | tf_op jit(solution)/shard_map/ppermute | solution.py:47
  111.2 13.9 %collective-permute-start.25 = (bf16[2,160,1024]{2,1,0:T(8,128)(2,1)S(1)}, bf16[2,160,1024]{2,1,0:T(8,128)(2,1)S(1)}, u32[]{:S(2)}, u32[]{:S(2)}) collective-permute-start(bf16[2,160,1024]{2,1,0:T(8,128)(2,1)S(1)} %collective-permute-done.22.refs_6_), channel_id=1, source_target_pairs={{0,1},{1,0},{2,3},{3,2},{4,5},{5,4},{6,7},{7,6},{8,9},{9,8},{10,11... | collective-permute-start | bytes 1966088 | tf_op jit(solution)/shard_map/ppermute | solution.py:47
  137.6 10.5 %collective-permute-start.27 = (bf16[320,1024]{1,0:T(8,128)(2,1)}, bf16[320,1024]{1,0:T(8,128)(2,1)S(1)}, u32[]{:S(2)}, u32[]{:S(2)}) collective-permute-start(bf16[320,1024]{1,0:T(8,128)(2,1)} %get-tuple-element.185), channel_id=1, source_target_pairs={{0,1},{1,0},{2,3},{3,2},{4,5},{5,4},{6,7},{7,6},{8,9},{9,8},{10,11... | collective-permute-start | bytes 1966088 | tf_op jit(solution)/shard_map/ppermute | solution.py:47
  137.8 10.3 %collective-permute-start.28 = (bf16[160,1024]{1,0:T(8,128)(2,1)S(1)}, bf16[160,1024]{1,0:T(8,128)(2,1)S(1)}, u32[]{:S(2)}, u32[]{:S(2)}) collective-permute-start(bf16[160,1024]{1,0:T(8,128)(2,1)S(1)} %copy-done.32), channel_id=1, source_target_pairs={{0,8},{1,9},{2,10},{3,11},{4,12},{5,13},{6,14},{7,15},{8,0},{9,1},... | collective-permute-start | bytes 983048 | tf_op jit(solution)/shard_map/ppermute | solution.py:55
  139.8 11.2 %collective-permute-start.30 = (bf16[160,1024]{1,0:T(8,128)(2,1)S(1)}, bf16[160,1024]{1,0:T(8,128)(2,1)S(1)}, u32[]{:S(2)}, u32[]{:S(2)}) collective-permute-start(bf16[160,1024]{1,0:T(8,128)(2,1)S(1)} %copy-done.32), channel_id=1, source_target_pairs={{0,1},{1,0},{2,3},{3,2},{4,5},{5,4},{6,7},{7,6},{8,9},{9,8},{10,11... | collective-permute-start | bytes 983048 | tf_op jit(solution)/shard_map/ppermute | solution.py:47
  186.7 33.0 %collective-permute-start.40 = (bf16[4,256,1024]{2,1,0:T(8,128)(2,1)}, bf16[4,256,1024]{2,1,0:T(8,128)(2,1)S(1)}, u32[]{:S(2)}, u32[]{:S(2)}) collective-permute-start(bf16[4,256,1024]{2,1,0:T(8,128)(2,1)} %bitcast.89), channel_id=1, source_target_pairs={{0,4},{1,3},{2,6},{3,1},{4,0},{5,7},{6,2},{7,5},{8,12},{9,11},{10,... | collective-permute-start | bytes 6291464 | tf_op jit(solution)/shard_map/ppermute | solution.py:55
  187.2 10.6 %collective-permute-start.29 = (bf16[160,1024]{1,0:T(8,128)(2,1)S(1)}, bf16[160,1024]{1,0:T(8,128)(2,1)S(1)}, u32[]{:S(2)}, u32[]{:S(2)}) collective-permute-start(bf16[160,1024]{1,0:T(8,128)(2,1)S(1)} %copy-done.34), channel_id=1, source_target_pairs={{0,8},{1,9},{2,10},{3,11},{4,12},{5,13},{6,14},{7,15},{8,0},{9,1},... | collective-permute-start | bytes 983048 | tf_op jit(solution)/shard_map/ppermute | solution.py:55
  189.0 35.2 %collective-permute-start.36 = (bf16[160,512]{1,0:T(8,128)(2,1)S(1)}, bf16[160,512]{1,0:T(8,128)(2,1)S(1)}, u32[]{:S(2)}, u32[]{:S(2)}) collective-permute-start(bf16[160,512]{1,0:T(8,128)(2,1)S(1)} %copy-done.45), channel_id=1, source_target_pairs={{0,1},{1,0},{2,3},{3,2},{4,5},{5,4},{6,7},{7,6},{8,9},{9,8},{10,11... | collective-permute-start | bytes 491528 | tf_op jit(solution)/shard_map/ppermute | solution.py:47
  189.0 36.3 %collective-permute-start.37 = (bf16[160,512]{1,0:T(8,128)(2,1)S(1)}, bf16[160,512]{1,0:T(8,128)(2,1)S(1)}, u32[]{:S(2)}, u32[]{:S(2)}) collective-permute-start(bf16[160,512]{1,0:T(8,128)(2,1)S(1)} %copy-done.48), channel_id=1, source_target_pairs={{0,1},{1,0},{2,3},{3,2},{4,5},{5,4},{6,7},{7,6},{8,9},{9,8},{10,11... | collective-permute-start | bytes 491528 | tf_op jit(solution)/shard_map/ppermute | solution.py:47
  189.5 16.2 %collective-permute-start.34 = (bf16[160,1024]{1,0:T(8,128)(2,1)S(1)}, bf16[160,1024]{1,0:T(8,128)(2,1)S(1)}, u32[]{:S(2)}, u32[]{:S(2)}) collective-permute-start(bf16[160,1024]{1,0:T(8,128)(2,1)S(1)} %copy-done.35), channel_id=1, source_target_pairs={{0,8},{1,9},{2,10},{3,11},{4,12},{5,13},{6,14},{7,15},{8,0},{9,1},... | collective-permute-start | bytes 983048 | tf_op jit(solution)/shard_map/ppermute | solution.py:55
  205.7 20.9 %collective-permute-start.38 = (bf16[160,1024]{1,0:T(8,128)(2,1)S(1)}, bf16[160,1024]{1,0:T(8,128)(2,1)}, u32[]{:S(2)}, u32[]{:S(2)}) collective-permute-start(bf16[160,1024]{1,0:T(8,128)(2,1)S(1)} %copy-done.31), channel_id=1, source_target_pairs={{0,1},{1,0},{2,3},{3,2},{4,5},{5,4},{6,7},{7,6},{8,9},{9,8},{10,11... | collective-permute-start | bytes 983048 | tf_op jit(solution)/shard_map/ppermute | solution.py:47
  210.8 15.9 %collective-permute-start.39 = (bf16[160,1024]{1,0:T(8,128)(2,1)}, bf16[160,1024]{1,0:T(8,128)(2,1)}, u32[]{:S(2)}, u32[]{:S(2)}) collective-permute-start(bf16[160,1024]{1,0:T(8,128)(2,1)} %get-tuple-element.211.refs_10_), channel_id=1, source_target_pairs={{0,1},{1,0},{2,3},{3,2},{4,5},{5,4},{6,7},{7,6},{8,9},{9,8},{10,11... | collective-permute-start | bytes 983048 | tf_op jit(solution)/shard_map/ppermute | solution.py:47
  223.5 18.9 %collective-permute-start.42 = (bf16[2,256,1024]{2,1,0:T(8,128)(2,1)S(1)}, bf16[2,256,1024]{2,1,0:T(8,128)(2,1)S(1)}, u32[]{:S(2)}, u32[]{:S(2)}) collective-permute-start(bf16[2,256,1024]{2,1,0:T(8,128)(2,1)S(1)} %get-tuple-element.273), channel_id=1, source_target_pairs={{0,2},{1,5},{2,0},{3,7},{4,6},{5,1},{6,4},{7,3},{8,10},{9,13},{10,... | collective-permute-start | bytes 3145736 | tf_op jit(solution)/shard_map/ppermute | solution.py:55
  224.2 33.1 %collective-permute-start.26 = (bf16[320,1024]{1,0:T(8,128)(2,1)}, bf16[320,1024]{1,0:T(8,128)(2,1)}, u32[]{:S(2)}, u32[]{:S(2)}) collective-permute-start(bf16[320,1024]{1,0:T(8,128)(2,1)} %get-tuple-element.182), channel_id=1, source_target_pairs={{0,1},{1,0},{2,3},{3,2},{4,5},{5,4},{6,7},{7,6},{8,9},{9,8},{10,11... | collective-permute-start | bytes 1966088 | tf_op jit(solution)/shard_map/ppermute | solution.py:47
  226.0 33.3 %collective-permute-start.45 = (bf16[320,1024]{1,0:T(8,128)(2,1)}, bf16[320,1024]{1,0:T(8,128)(2,1)S(1)}, u32[]{:S(2)}, u32[]{:S(2)}) collective-permute-start(bf16[320,1024]{1,0:T(8,128)(2,1)} %get-tuple-element.229), channel_id=1, source_target_pairs={{0,1},{1,0},{2,3},{3,2},{4,5},{5,4},{6,7},{7,6},{8,9},{9,8},{10,11... | collective-permute-start | bytes 1966088 | tf_op jit(solution)/shard_map/ppermute | solution.py:47
  232.2 19.1 %collective-permute-start.41 = (bf16[8,32,1024]{2,1,0:T(8,128)(2,1)}, bf16[8,32,1024]{2,1,0:T(8,128)(2,1)S(1)}, u32[]{:S(2)}, u32[]{:S(2)}) collective-permute-start(bf16[8,32,1024]{2,1,0:T(8,128)(2,1)} %bitcast.90), channel_id=1, source_target_pairs={{0,4},{1,3},{2,6},{3,1},{4,0},{5,7},{6,2},{7,5},{8,12},{9,11},{10,... | collective-permute-start | bytes 1572872 | tf_op jit(solution)/shard_map/ppermute | solution.py:55
  257.2 10.2 %collective-permute-start.44 = (bf16[2,160,1024]{2,1,0:T(8,128)(2,1)}, bf16[2,160,1024]{2,1,0:T(8,128)(2,1)S(1)}, u32[]{:S(2)}, u32[]{:S(2)}) collective-permute-start(bf16[2,160,1024]{2,1,0:T(8,128)(2,1)} %get-tuple-element.225), channel_id=1, source_target_pairs={{0,1},{1,0},{2,3},{3,2},{4,5},{5,4},{6,7},{7,6},{8,9},{9,8},{10,11... | collective-permute-start | bytes 1966088 | tf_op jit(solution)/shard_map/ppermute | solution.py:47
  262.3 40.8 %collective-permute-start.52 = (bf16[160,1024]{1,0:T(8,128)(2,1)}, bf16[160,1024]{1,0:T(8,128)(2,1)}, u32[]{:S(2)}, u32[]{:S(2)}) collective-permute-start(bf16[160,1024]{1,0:T(8,128)(2,1)} %shard_map.278.refs_7_), channel_id=1, source_target_pairs={{0,8},{1,9},{2,10},{3,11},{4,12},{5,13},{6,14},{7,15},{8,0},{9,1},... | collective-permute-start | bytes 983048 | tf_op jit(solution)/shard_map/ppermute | solution.py:55
  266.5 26.5 %collective-permute-start.48 = (bf16[1,256,1024]{2,1,0:T(8,128)(2,1)}, bf16[1,256,1024]{2,1,0:T(8,128)(2,1)S(1)}, u32[]{:S(2)}, u32[]{:S(2)}) collective-permute-start(bf16[1,256,1024]{2,1,0:T(8,128)(2,1)} %fusion.1), channel_id=1, source_target_pairs={{0,16},{1,17},{2,18},{3,19},{4,20},{5,21},{6,22},{7,23},{8,24},{9,... | collective-permute-start | bytes 1572872 | tf_op jit(solution)/shard_map/ppermute | solution.py:55
  266.8 27.4 %collective-permute-start.51 = (bf16[8,64,1536]{2,1,0:T(8,128)(2,1)}, bf16[8,64,1536]{2,1,0:T(8,128)(2,1)S(1)}, u32[]{:S(2)}, u32[]{:S(2)}) collective-permute-start(bf16[8,64,1536]{2,1,0:T(8,128)(2,1)} %bitcast.25), channel_id=1, source_target_pairs={{0,4},{1,3},{2,6},{3,1},{4,0},{5,7},{6,2},{7,5},{8,12},{9,11},{10,... | collective-permute-start | bytes 4718600 | tf_op jit(solution)/shard_map/ppermute | solution.py:55
  274.5 18.4 %collective-permute-start.47 = (f32[16,8,128]{2,1,0:T(8,128)}, f32[16,8,128]{2,1,0:T(8,128)S(1)}, u32[]{:S(2)}, u32[]{:S(2)}) collective-permute-start(f32[16,8,128]{2,1,0:T(8,128)} %get-tuple-element.235), channel_id=1, source_target_pairs={{0,1},{1,0},{2,3},{3,2},{4,5},{5,4},{6,7},{7,6},{8,9},{9,8},{10,11... | collective-permute-start | bytes 196616 | tf_op jit(solution)/shard_map/ppermute | solution.py:47
  275.5 10.2 %collective-permute-start.49 = (bf16[2,32,1024]{2,1,0:T(8,128)(2,1)S(1)}, bf16[2,32,1024]{2,1,0:T(8,128)(2,1)S(1)}, u32[]{:S(2)}, u32[]{:S(2)}) collective-permute-start(bf16[2,32,1024]{2,1,0:T(8,128)(2,1)S(1)} %get-tuple-element.281), channel_id=1, source_target_pairs={{0,8},{1,9},{2,10},{3,11},{4,12},{5,13},{6,14},{7,15},{8,0},{9,1},... | collective-permute-start | bytes 393224 | tf_op jit(solution)/shard_map/ppermute | solution.py:55
  285.7 14.2 %collective-permute-start.43 = (bf16[160,1024]{1,0:T(8,128)(2,1)S(1)}, bf16[160,1024]{1,0:T(8,128)(2,1)S(1)}, u32[]{:S(2)}, u32[]{:S(2)}) collective-permute-start(bf16[160,1024]{1,0:T(8,128)(2,1)S(1)} %copy-done.30), channel_id=1, source_target_pairs={{0,8},{1,9},{2,10},{3,11},{4,12},{5,13},{6,14},{7,15},{8,0},{9,1},... | collective-permute-start | bytes 983048 | tf_op jit(solution)/shard_map/ppermute | solution.py:55
  294.8 12.4 %collective-permute-start.54 = (bf16[4,64,1536]{2,1,0:T(8,128)(2,1)S(1)}, bf16[4,64,1536]{2,1,0:T(8,128)(2,1)S(1)}, u32[]{:S(2)}, u32[]{:S(2)}) collective-permute-start(bf16[4,64,1536]{2,1,0:T(8,128)(2,1)S(1)} %get-tuple-element.275), channel_id=1, source_target_pairs={{0,2},{1,5},{2,0},{3,7},{4,6},{5,1},{6,4},{7,3},{8,10},{9,13},{10,... | collective-permute-start | bytes 2359304 | tf_op jit(solution)/shard_map/ppermute | solution.py:55
  296.8 10.3 %collective-permute-start.55 = (f32[64,1024]{1,0:T(8,128)S(1)}, f32[64,1024]{1,0:T(8,128)S(1)}, u32[]{:S(2)}, u32[]{:S(2)}) collective-permute-start(f32[64,1024]{1,0:T(8,128)S(1)} %slice_bitcast_fusion.2), channel_id=1, source_target_pairs={{0,8},{1,9},{2,10},{3,11},{4,12},{5,13},{6,14},{7,15},{8,0},{9,1},... | collective-permute-start | bytes 786440 | tf_op jit(solution)/shard_map/ppermute | solution.py:55
  299.5 10.9 %collective-permute-start.58 = (f32[32,1024]{1,0:T(8,128)S(1)}, f32[32,1024]{1,0:T(8,128)S(1)}, u32[]{:S(2)}, u32[]{:S(2)}) collective-permute-start(f32[32,1024]{1,0:T(8,128)S(1)} %slice_bitcast_fusion.4), channel_id=1, source_target_pairs={{0,1},{1,0},{2,3},{3,2},{4,5},{5,4},{6,7},{7,6},{8,9},{9,8},{10,11... | collective-permute-start | bytes 393224 | tf_op jit(solution)/shard_map/ppermute | solution.py:47
  299.9 24.2 %collective-permute-start.62 = (bf16[1,32,1024]{2,1,0:T(8,128)(2,1)S(1)}, bf16[1,32,1024]{2,1,0:T(8,128)(2,1)S(1)}, u32[]{:S(2)}, u32[]{:S(2)}) collective-permute-start(bf16[1,32,1024]{2,1,0:T(8,128)(2,1)S(1)} %fusion.8), channel_id=1, source_target_pairs={{0,16},{1,17},{2,18},{3,19},{4,20},{5,21},{6,22},{7,23},{8,24},{9,... | collective-permute-start | bytes 196616 | tf_op jit(solution)/shard_map/ppermute | solution.py:55
  307.3 11.7 %collective-permute-start.57 = (bf16[2,64,1536]{2,1,0:T(8,128)(2,1)S(1)}, bf16[2,64,1536]{2,1,0:T(8,128)(2,1)S(1)}, u32[]{:S(2)}, u32[]{:S(2)}) collective-permute-start(bf16[2,64,1536]{2,1,0:T(8,128)(2,1)S(1)} %get-tuple-element.271), channel_id=1, source_target_pairs={{0,8},{1,9},{2,10},{3,11},{4,12},{5,13},{6,14},{7,15},{8,0},{9,1},... | collective-permute-start | bytes 1179656 | tf_op jit(solution)/shard_map/ppermute | solution.py:55
  309.6 9.5 %collective-permute-start.56 = (f32[2,8,128]{2,1,0:T(8,128)S(1)}, f32[2,8,128]{2,1,0:T(8,128)S(1)}, u32[]{:S(2)}, u32[]{:S(2)}) collective-permute-start(f32[2,8,128]{2,1,0:T(8,128)S(1)} %get-tuple-element.290), channel_id=1, source_target_pairs={{0,8},{1,9},{2,10},{3,11},{4,12},{5,13},{6,14},{7,15},{8,0},{9,1},... | collective-permute-start | bytes 24584 | tf_op jit(solution)/shard_map/ppermute | solution.py:55
  321.4 11.3 %collective-permute-start.61 = (bf16[1,64,1536]{2,1,0:T(8,128)(2,1)S(1)}, bf16[1,64,1536]{2,1,0:T(8,128)(2,1)S(1)}, u32[]{:S(2)}, u32[]{:S(2)}) collective-permute-start(bf16[1,64,1536]{2,1,0:T(8,128)(2,1)S(1)} %fusion.3), channel_id=1, source_target_pairs={{0,16},{1,17},{2,18},{3,19},{4,20},{5,21},{6,22},{7,23},{8,24},{9,... | collective-permute-start | bytes 589832 | tf_op jit(solution)/shard_map/ppermute | solution.py:55
  (72 other events, 498.9 us)
where the time goes:
time: 343 us; the launch traced here: 337 us
  Pallas kernels  151 us (44%)
  waiting for transfers between devices  99.6 us (29%)
  starting transfers between devices  51.4 us (15%)
  local copies, waits for them, and re-layouts  21.9 us (6%)
  other arithmetic  11.4 us (3%)
    pallas_call x30, Pallas kernels, call(): pl.pallas_call(kernel, out_shape=outs, in_specs=specs, out_specs=tuple(ou...  149 us
    ppermute x36, waiting for transfers between devices, bit_swap(): return lax.ppermute(value, ('img', 'seq'), pairs)  97.1 us
    ppermute x36, starting transfers between devices, bit_swap(): return lax.ppermute(value, ('img', 'seq'), pairs)  44.4 us
    unnamed x113, local copies, waits for them, and re-layouts  14.9 us
    ppermute x28, starting transfers between devices, core_swap(): return lax.ppermute(value, 'seq', [(0, 1), (1, 0)])  7.02 us
  transfers between devices with their start and end apart: 64, of which 22 were waited for; matrix products, arithmetic and copies ran while one was open for 5% of the time, Pallas kernels for 32%

commit v1 on v0

--- a/solution.py
+++ b/solution.py
@@ -526,12 +526,12 @@
 
 LANES = 128
 MEASURED_US = {
-    "k_pack_heads": 1.6, "k_heads": 7, "k_attend": 6, "k_proj_weight": 3, "k_project": 3.4,
-    "k_unpack_units": 4.5, "k_feed": 20, "k_feed_out": 6, "k_pair_send": 5, "k_grad_feed": 15,
-    "k_middle_back": 4.4, "k_attend_back": 8.3, "k_grad_proj": 5.5, "k_grad_heads": 8.7,
-    "k_first_back": 6, "k_input_back": 4.3, "k_small": 1.8, "k_output": 2.5, "k_columns": 2, "k_rows": 1.8,
+    "k_pack_heads": 1.6, "k_heads": 7, "k_attend": 6, "k_project": 0.1,
+    "k_unpack_units": 4.5, "k_feed": 10, "k_feed_out": 3, "k_pair_send": 0.2, "k_grad_feed": 15,
+    "k_middle_back": 30, "k_attend_back": 8, "k_grad_proj": 0.2, "k_grad_heads": 8.7,
+    "k_first_back": 6, "k_input_back": 4.3, "k_small": 2, "k_output": 4, "k_columns": 2, "k_rows": 1.8,
 }
-FLOPS_PER_US = 0.5e9
+FLOPS_PER_US = 3e9
 VMEM_LIMIT = 56 * 1024 * 1024
 SMALL_ROWS = 8
 GAIN1, BIAS1, QV, PROJ_B, GAIN2, BIAS2, FC1_B, FC2_B = range(8)
@@ -549,14 +549,14 @@
     return jnp.where(core == 0, a, b)
 
 
-def call(kernel, out, args, grid=None, in_specs=None, out_specs=None, scratch=(), deps=(), place=None):
+def call(kernel, out, args, grid=None, in_specs=None, out_specs=None, scratch=(), deps=(), kept=0, us=None, place=None):
     whole = pl.BlockSpec(memory_space=pltpu.VMEM)
     outs = out if isinstance(out, tuple) else (out,)
     specs = [pl.BlockSpec(memory_space=pltpu.SMEM)] + list(in_specs or [whole] * len(args))
     out_specs = out_specs if out_specs is not None else tuple(whole for _ in outs)
     extra = {} if grid is None else {"grid": grid}
     name = getattr(kernel, "func", kernel).__name__
-    flops = int(MEASURED_US[name] * FLOPS_PER_US)
+    flops = int((us or MEASURED_US[name]) * FLOPS_PER_US)
     if deps:
         specs += [pl.BlockSpec(memory_space=pl.ANY)] * len(deps)
         inner, count = kernel, 1 + len(args)
@@ -564,6 +564,7 @@
         def kernel(*refs):
             return inner(*refs[:count], *refs[count + len(deps) :])
 
+        extra["input_output_aliases"] = {count + k: k for k in range(kept)}
     result = pl.pallas_call(
         kernel,
         out_shape=outs,
@@ -674,26 +675,19 @@
         mixed[:, part] = total.astype(b16)
 
 
-def k_proj_weight(orders, place, sent, got, sent_far, got_far, w_proj):
-    me, core = place[0], place[1]
-    blocks, rows, _ = sent.shape
-    for c, refs in enumerate(((sent, got), (sent_far, got_far))):
-        for p in range(2 * blocks):
-            chip = me ^ spread_of(p, orders, core ^ c)
-            at = aligned(2 * chip + (core ^ c), rows)
-            w_proj[pl.ds(at, rows), :] = refs[p // blocks][p % blocks]
-
-
-def k_pair_send(place, pair, got, send):
-    send[...] = (pair[...] + got[pair.shape[0] :, :].astype(f32)).astype(b16)
-
-
-def k_output(image, place, middle, own, got, pair_got, vectors, out):
-    local = own.shape[0]
+def k_pair_send(place, own0, got0, own1, got1, send0, send1):
+    for own, got, send in ((own0, got0, send0), (own1, got1, send1)):
+        send[...] = (own[...] + got[...].astype(f32)).astype(b16)
+
+
+def k_output(place, middle, own, got, pair_got, vectors, out):
+    images, local, _ = out.shape
     slot = place[1] * local + lax.broadcasted_iota(jnp.int32, (local, 1), 0)
-    total = middle[...] + vectors[5:6, :] + own[...]
-    total += got[:local, :].astype(f32) + pair_got[...].astype(f32)
-    out[...] = jnp.where(slot < BUFFER + place[3 + image], total, 0.0).astype(b16)
+    for i in range(images):
+        part = slice(i * local, (i + 1) * local)
+        total = middle[part, :] + vectors[5:6, :] + own[part, :]
+        total += got[part, :].astype(f32) + pair_got[part, :].astype(f32)
+        out[i] = jnp.where(slot < BUFFER + place[3 + i], total, 0.0).astype(b16)
 
 
 def k_unpack_units(orders, place, sent, got, w_fc1, w_fc2):
@@ -766,25 +760,37 @@
         sums[:, pl.ds(at, LANES)] = jnp.broadcast_to(total, (8, LANES))
 
 
-def k_project(place, att_own, att_got, w, x, vectors, middle, second):
-    core = place[1]
-    half = att_own.shape[1]
-    own = w[pl.ds(aligned(core, half), half), :]
-    other = w[pl.ds(aligned(1 - core, half), half), :]
-    total = dot(att_own[...], own) + dot(att_got[...], other)
-    mid = x[0].astype(f32) + total + vectors[2:3, :]
-    middle[...] = mid
-    normed, _ = norm_parts(mid)
-    second[...] = (normed * vectors[3:4, :] + vectors[4:5, :]).astype(b16)
-
-
-def k_feed(image, place, s0, s1, s2, s3, u0, u1, u2, u3, w1, w2, vectors,
-           act, d_pre, ds_own, ds_pair, ds_other, sums, sec, up):
-    local = s0.shape[0]
+def k_project(orders, place, sent, got, sent_far, got_far, own0, own1, got0, got1, x, vectors,
+              w, middle, second):
+    me, core = place[0], place[1]
+    blocks, rows, _ = sent.shape
+    for c, refs in enumerate(((sent, got), (sent_far, got_far))):
+        for p in range(2 * blocks):
+            chip = me ^ spread_of(p, orders, core ^ c)
+            at = aligned(2 * chip + (core ^ c), rows)
+            w[pl.ds(at, rows), :] = refs[p // blocks][p % blocks]
+    half = own0.shape[1]
+    images, local, _ = x.shape
+    both = lambda a, b: jnp.concatenate([a[...], b[...]], axis=0)
+    total = dot(both(own0, own1), w[pl.ds(aligned(core, half), half), :])
+    total += dot(both(got0, got1), w[pl.ds(aligned(1 - core, half), half), :])
+    for i in range(images):
+        part = slice(i * local, (i + 1) * local)
+        mid = x[i].astype(f32) + total[part] + vectors[2:3, :]
+        middle[part, :] = mid
+        normed, _ = norm_parts(mid)
+        second[part, :] = (normed * vectors[3:4, :] + vectors[4:5, :]).astype(b16)
+
+
+def k_feed(place, s0, s1, u0, u1, w1, w2, vectors, act, d_pre, ds_own, ds_other, sums, sec, up):
+    images, local, _ = u0.shape
+    tokens = images * local
     tile = 256
-    for k, (s, u) in enumerate(((s0, u0), (s1, u1), (s2, u2), (s3, u3))):
-        sec[k * local : (k + 1) * local, :] = s[...]
-        up[k * local : (k + 1) * local, :] = u[image]
+    for k, (s, u) in enumerate(((s0, u0), (s1, u1))):
+        sec[k * tokens : (k + 1) * tokens, :] = s[...]
+        for i in range(images):
+            at = k * tokens + i * local
+            up[at : at + local, :] = u[i]
     for at in range(0, w1.shape[1], tile):
         part = slice(at, at + tile)
         pre = dot(sec[...], w1[:, part]) + vectors[7:8, part]
@@ -795,68 +801,69 @@
         d_pre[:, part] = grad
         total = jnp.sum(grad.astype(f32), axis=0, keepdims=True)
         sums[:, part] = jnp.broadcast_to(total, (8, tile))
-    ds_other[...] = dot_nt(d_pre[2 * local :, :], w1[...]).astype(b16)
-    ds_pair[...] = dot_nt(d_pre[local : 2 * local, :], w1[...])
-    ds_own[...] = dot_nt(d_pre[:local, :], w1[...])
-
-
-def k_feed_out(place, act, w2, own, pair, other):
-    local = own.shape[0]
-    other[...] = dot(act[2 * local :, :], w2[...]).astype(b16)
-    pair[...] = dot(act[local : 2 * local, :], w2[...])
-    own[...] = dot(act[:local, :], w2[...])
+    ds_other[...] = dot_nt(d_pre[tokens:, :], w1[...]).astype(b16)
+    ds_own[...] = dot_nt(d_pre[:tokens, :], w1[...])
+
+
+def k_feed_out(place, act, w2, own, other):
+    tokens = own.shape[0]
+    other[...] = dot(act[tokens:, :], w2[...]).astype(b16)
+    own[...] = dot(act[:tokens, :], w2[...])
 
 
 def k_middle_back(place, ds_own, ds_got, pair_got, middle, up, w, vectors,
                   d_middle, d_branch, att_own, att_other, sums):
     core = place[1]
-    local = ds_own.shape[0]
+    images, local, _ = up.shape
     half = att_own.shape[1]
-    d_second = ds_own[...] + ds_got[:local, :].astype(f32) + pair_got[...].astype(f32)
-    normed, scale = norm_parts(middle[...])
-    upstream = up[0].astype(f32)
-    d_mid = upstream + norm_back(d_second, normed, scale, vectors[3:4, :])
-    d_middle[...] = d_mid
-    branch = d_mid.astype(b16)
-    d_branch[...] = branch
+    total = lambda a: jnp.sum(a, axis=0, keepdims=True)
+    rows = [0.0] * 4
+    for i in range(images):
+        part = slice(i * local, (i + 1) * local)
+        d_second = ds_own[part, :] + ds_got[part, :].astype(f32) + pair_got[part, :].astype(f32)
+        normed, scale = norm_parts(middle[part, :])
+        upstream = up[i].astype(f32)
+        d_mid = upstream + norm_back(d_second, normed, scale, vectors[3:4, :])
+        d_middle[part, :] = d_mid
+        branch = d_mid.astype(b16)
+        d_branch[part, :] = branch
+        rows[0] += total(d_second * normed)
+        rows[1] += total(d_second)
+        rows[2] += total(branch.astype(f32))
+        rows[3] += total(upstream)
+    branch = d_branch[...]
+    att_other[...] = dot_nt(branch, w[pl.ds(aligned(1 - core, half), half), :]).astype(b16)
     att_own[...] = dot_nt(branch, w[pl.ds(aligned(core, half), half), :]).astype(b16)
-    att_other[...] = dot_nt(branch, w[pl.ds(aligned(1 - core, half), half), :]).astype(b16)
-    total = lambda a: jnp.sum(a, axis=0, keepdims=True)
-    sums[0:1, :] = total(d_second * normed)
-    sums[1:2, :] = total(d_second)
-    sums[2:3, :] = total(branch.astype(f32))
-    sums[3:4, :] = total(upstream)
+    for r in range(4):
+        sums[r : r + 1, :] = rows[r]
     sums[4:, :] = jnp.zeros((4, sums.shape[1]), f32)
 
 
-def put(send, keep, place_at, rows_at, value, half_count, per):
-    @pl.when(place_at >= half_count)
-    def _():
-        at = pl.multiple_of((place_at - half_count) * per + rows_at, value.shape[0])
-        send[pl.ds(at, value.shape[0]), :] = value.astype(b16)
-
-    @pl.when(place_at < half_count)
-    def _():
-        at = pl.multiple_of(place_at * per + rows_at, value.shape[0])
-        keep[pl.ds(at, value.shape[0]), :] = value
-
-
-def k_grad_heads(orders, n, place, left, r0, r1, send, keep):
+def put(held, row, value):
+    held[pl.ds(pl.multiple_of(row, value.shape[0]), value.shape[0]), :] = value.astype(b16)
+
+
+def split(held, send, keep):
+    cut = send.shape[0]
+    send[...] = held[cut:, :]
+    keep[...] = held[:cut, :]
+
+
+def k_grad_heads(orders, n, place, left, right, send, keep, held):
     me, core = place[0], place[1]
-    step = pl.program_id(0)
-    cut = left.shape[0] // 2
-    tile = left.shape[1]
-    rows = 2 * send.shape[0] // (2 * n)
-    total = dot_tn(left[:cut, :], r0[...]) + dot_tn(left[cut:, :], r1[...])
-    for i in range(tile // (2 * rows)):
-        chip = step * (tile // (2 * rows)) + i
-        at = position_of(me ^ chip, orders, core)
-        for c in range(2):
-            value = total[(2 * i + c) * rows : (2 * i + c + 1) * rows, :]
-            put(send, keep, at, (core ^ c) * rows, value, n // 2, 2 * rows)
-
-
-def k_grad_feed(orders, n, place, a0, a1, u0, u1, s0, s1, d0, d1, send, keep):
+    tile = 256
+    rows = held.shape[0] // (2 * n)
+    for step in range(left.shape[1] // tile):
+        total = dot_tn(left[:, step * tile : (step + 1) * tile], right[...])
+        for i in range(tile // rows):
+            dev = step * (tile // rows) + i
+            at = position_of(me ^ (dev // 2), orders, core)
+            value = total[i * rows : (i + 1) * rows, :]
+            put(held, at * 2 * rows + (core ^ (dev % 2)) * rows, value)
+    split(held, send, keep)
+
+
+def k_grad_feed(orders, n, place, a0, a1, u0, u1, s0, s1, d0, d1, send, keep, held):
     me, core, side = place[0], place[1], place[2]
     low = 1 << PAIR
     tile = 256
@@ -869,7 +876,7 @@
             b = step * (tile // LANES) + i
             chip = (b // low) * 2 * low + side * low + b % low
             at = position_of(me ^ chip, orders, core)
-            put(send, keep, at, 0, total[i * LANES : (i + 1) * LANES, :], n // 4, per)
+            put(held, at * per, total[i * LANES : (i + 1) * LANES, :])
     for step in range(s0.shape[1] // tile):
         part = slice(step * tile, (step + 1) * tile)
         total = dot_tn(s0[:, part], d0[...]) + dot_tn(s1[:, part], d1[...])
@@ -878,11 +885,12 @@
             bits = me ^ (dev // 2)
             at = position_of(bits, orders, core)
             inner = LANES + (((bits >> PAIR) & 1) * 2 + (core ^ (i % 2))) * rows
-            put(send, keep, at, inner, total[i * rows : (i + 1) * rows, :], n // 4, per)
+            put(held, at * per + inner, total[i * rows : (i + 1) * rows, :])
+    split(held, send, keep)
 
 
 def k_grad_proj(orders, place, *refs):
-    lefts, rights, (send, keep) = (refs[:4], refs[4:8]), refs[8:12], refs[12:]
+    lefts, rights, (send, keep, held) = (refs[:4], refs[4:8]), refs[8:10], refs[10:]
     me, core = place[0], place[1]
     rows = 32
     right = jnp.concatenate([a[...] for a in rights], axis=0)
@@ -898,24 +906,31 @@
                 total[2 * i * rows : (2 * i + 1) * rows, :],
                 total[(2 * i + 1) * rows : (2 * i + 2) * rows, :],
             )
-            put(send, keep, at, 0, value, count, rows)
-
-
-def k_first_back(place, d0, d1, w, own, other):
-    local = own.shape[1]
-    for i, d in enumerate((d0, d1)):
-        total = dot_nt(d[...], w[...])
-        own[i] = total[:local]
-        other[i] = total[local:].astype(b16)
-
-
-def k_input_back(place, x, own, got, m0, m1, vectors, grad, sums):
+            put(held, at * rows, value)
+    split(held, send, keep)
+
+
+def k_first_back(place, d, w, own, other):
+    images, local, width = own.shape
+    tile = 256
+    for step in range(width // tile):
+        part = slice(step * tile, (step + 1) * tile)
+        total = dot_nt(d[...], w[part, :])
+        for i in range(images):
+            at = 2 * i * local
+            own[i, :, part] = total[at : at + local]
+            other[i, :, part] = total[at + local : at + 2 * local].astype(b16)
+
+
+def k_input_back(place, x, own, got, mid, vectors, grad, sums):
     total = lambda a: jnp.sum(a, axis=0, keepdims=True)
+    images, local, _ = x.shape
     gains = biases = 0.0
-    for i, mid in enumerate((m0, m1)):
+    for i in range(images):
         normed, scale = norm_parts(x[i].astype(f32))
         d_first = own[i] + got[i].astype(f32)
-        grad[i] = mid[...] + norm_back(d_first, normed, scale, vectors[0:1, :])
+        back = norm_back(d_first, normed, scale, vectors[0:1, :])
+        grad[i] = mid[i * local : (i + 1) * local, :] + back
         gains += total(d_first * normed)
         biases += total(d_first)
     sums[0:1, :] = gains
@@ -923,14 +938,13 @@
     sums[2:, :] = jnp.zeros((6, sums.shape[1]), f32)
 
 
-def k_small(orders, n, place, one, mid0, mid1, pre0, pre1, mix0, mix1, mine, theirs, small):
+def k_small(orders, n, place, one, mids, pre0, pre1, mix, mine, theirs, small):
     me, core, side = place[0], place[1], place[2]
     width = one.shape[1]
     per = width // (2 * n)
     half = width // 2
-    mids = mid0[...] + mid1[...]
     pres = pre0[...] + pre1[...]
-    mixes = mix0[...] + mix1[...]
+    mixes = mix[:8, :] + mix[8:, :]
     small[...] = jnp.zeros(small.shape, f32)
     rows = (
         (GAIN1, one[0:1, :]),
@@ -999,10 +1013,11 @@
         got = self.run.now(self.got)
         cut = got.shape[0] // 2
         if cut:
-            self.send = (self.keep[cut:] + got[cut:].astype(f32)).astype(self.send.dtype)
-            self.keep = self.keep[:cut] + got[:cut].astype(f32)
+            total = self.keep[cut:].astype(f32) + got[cut:].astype(f32)
+            self.send = total.astype(self.send.dtype)
+            self.keep = self.keep[:cut].astype(f32) + got[:cut].astype(f32)
         else:
-            self.keep = self.keep + got.astype(f32)
+            self.keep = self.keep.astype(f32) + got.astype(f32)
         self.got = None
 
     def step(self):
@@ -1074,30 +1089,23 @@
     proj = Gather(proj_weight, last)
 
     heads.step()
-    heads.held, proj.held, fc1_send, x_other, up_other = tie(
-        heads.held, proj.held, fc1_send, x_other, up_other
+    fc1_pair = bit_swap(fc1_send, pair)
+    heads.held, proj.held, fc1_pair, x_other, up_other = tie(
+        heads.held, proj.held, fc1_pair, x_other, up_other
     )
     heads.step()
     proj.step()
-    fc2 = Gather(fc2_weight, most)
-    heads.held, proj.held, fc1_send, fc2.held = tie(heads.held, proj.held, fc1_send, fc2.held)
+    feed = Gather(jnp.concatenate([fc1_mine[0], fc1_got[0], fc1_pair, fc2_weight], axis=0), most)
+    heads.held, proj.held, feed.held = tie(heads.held, proj.held, feed.held)
     while len(heads.steps) > 1:
         heads.step()
     proj.step()
-    fc1_pair = bit_swap(fc1_send, pair)
-    fc2.step()
-    fc1 = Gather(jnp.concatenate([fc1_mine[0], fc1_got[0], fc1_pair], axis=0), most)
-    heads.held, proj.held, fc1.held, fc2.held = tie(heads.held, proj.held, fc1.held, fc2.held)
+    heads.held, proj.held, feed.held = tie(heads.held, proj.held, feed.held)
     heads.step()
-    proj.step()
-    fc1.step()
-    feed = Gather(None, most)
-    feed.steps = fc1.steps
-    feed.held = jnp.concatenate([fc1.held, fc2.held], axis=1)
-    feed.held, up, heads.got, proj.held = tie(feed.held, up, heads.got, proj.held)
+    feed.step()
+    heads.got, feed.held, proj.held = tie(heads.got, feed.held, proj.held)
     feed.step()
     proj.step()
-    up_pair = bit_swap(up, pair)
 
     tokens = images * 2 * local
     w_qkv, vectors, first, mixed = on(
@@ -1117,7 +1125,9 @@
         block((slots, LANES), lambda h, i=i, f=f: (i, f + h)) for f in (0, pairs, 2 * pairs)
     ]
     lane_spec = block((local, LANES), lambda h: (0, h))
-    att_own, att_got, att_other = [], [], []
+    tok = images * local
+    flat = lambda cols, dtype=f32: shape((tok, cols), dtype)
+    att_own, att_other, att_got = [], [], []
     for i in range(images):
         own, other = on(
             bind(k_attend, i),
@@ -1132,181 +1142,162 @@
         att_got.append(core_swap(other))
         if i == 0:
             proj.got, feed.got = run.now(proj.got, feed.got)
-            proj_far = core_swap(proj.sent), core_swap(proj.got)
+            proj.held = jnp.concatenate([proj.sent, proj.got], axis=0)
             feed.held = jnp.concatenate([feed.sent, feed.got], axis=0)
             feed.step()
-    w_proj = on(
-        bind(k_proj_weight, last),
-        shape((width, width), b16),
-        (proj.sent, proj.got, *proj_far),
-    )
-    middle, second = [], []
-    for i in range(images):
-        mid, sec = on(
-            k_project,
-            (shape((local, width)), shape((local, width), b16)),
-            (att_own[i], att_got[i], w_proj, inputs, vectors),
-            grid=(1,),
-            in_specs=[whole, whole, whole, block((1, local, width), lambda t, i=i: (i, 0, 0)), whole],
-        )
-        middle.append(mid)
-        second.append((sec, bit_swap(sec, pair), core_swap(sec)))
-        if i == 0:
-            up_pair = run.now(up_pair)
-            up_other_pair = core_swap(up_pair)
-    ups = (up, up_pair, up_other, up_other_pair)
+            proj.step()
+            proj_sent_far = core_swap(proj.sent)
+    proj.got, up = run.now(proj.got, up)
+    up_pair = bit_swap(up, pair)
+    proj_far = proj_sent_far, core_swap(proj.got)
+    w_proj, middle, second = on(
+        bind(k_project, last),
+        (shape((width, width), b16), flat(width), flat(width, b16)),
+        (proj.sent, proj.got, *proj_far, *att_own, *att_got, inputs, vectors),
+    )
+    second_other = core_swap(second)
+    second_pair = bit_swap(second, pair)
     w_fc1, w_fc2 = on(
         bind(k_unpack_units, most),
         (shape((width, hidden), b16), shape((hidden, width), b16)),
         (feed.sent, feed.got),
     )
-
+    up_pair = run.now(up_pair)
+    up_other_pair = core_swap(up_pair)
     tile = 256
-    tiles = hidden // tile
-    part = shape((local, width))
-    other_part = shape((2 * local, width), b16)
-    fixed = lambda dims: block(dims, lambda t: (0,) * len(dims))
-    feeds, outs, ds_got, ds_sends, out_got = [], [], [], [], []
-    send_shape = shape((local, width), b16)
-    for i in range(images):
-        sec, sec_pair, sec_other = second[i]
-        if i == 0:
-            sec_pair = run.now(sec_pair)
-        second[i] = (sec, sec_pair, sec_other, core_swap(sec_pair))
-        feeds.append(
-            on(
-                bind(k_feed, i),
-                (
-                    shape((4 * local, hidden), b16),
-                    shape((4 * local, hidden), b16),
-                    part, part, other_part,
-                    shape((8, hidden)),
-                    shape((4 * local, width), b16),
-                    shape((4 * local, width), b16),
-                ),
-                second[i] + ups + (w_fc1, w_fc2, vectors),
-            )
+    fixed = lambda dims: block(dims, lambda *_: (0,) * len(dims))
+    wide_rows = lambda cols: shape((2 * tok, cols), b16)
+    feed_shapes = (
+        wide_rows(hidden), wide_rows(hidden), flat(width), flat(width, b16), shape((8, hidden)),
+        wide_rows(width), wide_rows(width),
+    )
+    feeds = []
+    feeds.append(
+        on(k_feed, feed_shapes, (second, second_other, up, up_other, w_fc1, w_fc2, vectors))
+    )
+    second_pair = run.now(second_pair)
+    second_other_pair = core_swap(second_pair)
+    feeds.append(
+        on(
+            k_feed,
+            feed_shapes,
+            (second_pair, second_other_pair, up_pair, up_other_pair, w_fc1, w_fc2, vectors),
         )
-        ds_got.append(core_swap(feeds[i][4]))
-        outs.append(on(k_feed_out, (part, part, other_part), (feeds[i][0], w_fc2)))
-        out_got.append(core_swap(outs[i][2]))
-        if i == 0:
-            sec, sec_pair, sec_other = second[1]
-            second[1] = (sec, run.now(sec_pair), sec_other)
-        ds_sends.append(on(k_pair_send, send_shape, (feeds[i][3], ds_got[i])))
-    pair_got = [bit_swap(s, pair) for s in ds_sends]
+    )
+    ds_pair_got = core_swap(feeds[1][3])
+    out_shapes = (flat(width), flat(width, b16))
+    out_pair_own, out_pair_other = on(k_feed_out, out_shapes, (feeds[1][0], w_fc2))
+    out_pair_got = core_swap(out_pair_other)
 
     acts = [f[0] for f in feeds]
     d_pres = [f[1] for f in feeds]
-
-    halves = lambda count, cols: (shape((count, cols), b16), shape((count, cols)))
+    ds_send, out_send = on(
+        k_pair_send,
+        (flat(width, b16),) * 2,
+        (feeds[1][2], ds_pair_got, out_pair_own, out_pair_got),
+    )
+    pair_got = bit_swap(ds_send, pair)
+    ds_got = core_swap(run.now(feeds[0][3]))
+    halves = lambda count, cols: (shape((count, cols), b16), shape((count, cols), b16))
+    held = lambda count, cols: [pltpu.VMEM((2 * count, cols), b16)]
     cut = lambda a, per: a.reshape(-1, per, a.shape[-1])
     feed_send, feed_keep = on(
         bind(k_grad_feed, most, n),
         halves(few // 2 * (4 * rows + units), width),
-        (*acts, *[f[7] for f in feeds], *[f[6] for f in feeds], *d_pres),
+        (*acts, *[f[6] for f in feeds], *[f[5] for f in feeds], *d_pres),
+        scratch=held(few // 2 * (4 * rows + units), width),
     )
     grad_feed = Sums(run, cut(feed_send, 4 * rows + units), cut(feed_keep, 4 * rows + units), most)
 
-    d_middle, d_branch, mid_sums, d_mixed, mix_sums, att_grads = [], [], [], [], [], []
+    out_pair = bit_swap(run.now(out_send), pair)
+    d_middle, d_branch, d_att, d_att_other, mid_sums = on(
+        k_middle_back,
+        (flat(width), flat(width, b16), flat(half, b16), flat(half, b16), shape((8, width))),
+        (feeds[0][2], ds_got, pair_got, middle, up, w_proj, vectors),
+    )
+    d_att_got = core_swap(d_att_other)
+    att_far, d_branch_far = [core_swap(a) for a in att_own], core_swap(d_branch)
+    d_mixed, mix_sums = (), ()
     for i in range(images):
-        d_mid, branch, own, other, sums = on(
-            k_middle_back,
-            (part, shape((local, width), b16)) + (shape((local, half), b16),) * 2 + (shape((8, width)),),
-            (feeds[i][2], ds_got[i], pair_got[i], middle[i], up, w_proj, vectors),
-            grid=(1,),
-            in_specs=[whole] * 4 + [block((1, local, width), lambda t, i=i: (i, 0, 0)), whole, whole],
+        part = block((local, LANES), lambda h, i=i: (i, h))
+        d_mixed, mix_sums = on(
+            bind(k_attend_back, i),
+            (shape((tokens, 3 * half), b16), shape((8 * images, 3 * half))),
+            (mixed, mixed, mixed, d_att, d_att_got),
+            grid=(pairs,),
+            in_specs=head_specs(i) + [part, part],
+            out_specs=[
+                block((slots, 3 * half), lambda h, i=i: (i, 0)),
+                block((8, 3 * half), lambda h, i=i: (i, 0)),
+            ],
+            wait=(d_mixed, mix_sums) if i > 0 else (),
+            kept=2 if i > 0 else 0,
+            us=8 if i > 0 else 0.2,
         )
-        d_middle.append(d_mid)
-        d_branch.append(branch)
-        mid_sums.append(sums)
-        att_grads.append((own, core_swap(other)))
-    def attend_back(i, *wait):
-        d, sums = on(
-            bind(k_attend_back, i),
-            (shape((slots, 3 * half), b16), shape((8, 3 * half))),
-            (mixed, mixed, mixed) + att_grads[i],
-            grid=(pairs,),
-            in_specs=head_specs(i) + [lane_spec, lane_spec],
-            out_specs=[fixed((slots, 3 * half)), fixed((8, 3 * half))],
-            wait=wait,
-        )
-        d_mixed.append(d)
-        mix_sums.append(sums)
-
-    att_far = [core_swap(a) for a in att_own]
-    d_branch_far = [core_swap(b) for b in d_branch]
-    attend_back(0)
-    grad_feed.step()
-    proj_send, proj_keep = on(
-        bind(k_grad_proj, full),
-        halves(half // 2, width),
-        (*att_own, *att_other, *att_got, *att_far, *d_branch, *d_branch_far),
-    )
-    grad_proj = Sums(run, cut(proj_send, rows), cut(proj_keep, rows), full)
-    attend_back(1)
-    grad_feed.step()
+        if i == 0:
+            proj_send, proj_keep = on(
+                bind(k_grad_proj, full),
+                halves(half // 2, width),
+                (*att_own, *att_other, *att_got, *att_far, d_branch, d_branch_far),
+                scratch=held(half // 2, width),
+            )
+            grad_proj = Sums(run, cut(proj_send, rows), cut(proj_keep, rows), full)
+            grad_feed.step()
     qkv_send, qkv_keep = on(
         bind(k_grad_heads, full, n),
         halves(half, 3 * half),
-        (first, *d_mixed),
-        grid=(width // tile,),
-        in_specs=[block((tokens, tile), lambda t: (0, t)), whole, whole],
-        out_specs=[fixed((half, 3 * half))] * 2,
+        (first, d_mixed),
+        scratch=held(half, 3 * half),
     )
     grad_qkv = Sums(run, cut(qkv_send, 2 * rows), cut(qkv_keep, 2 * rows), full)
+    grad_feed.step()
     grad_proj.step()
     df_own, df_other = on(
         k_first_back,
         (shape(inputs.shape), shape(inputs.shape, b16)),
-        (*d_mixed, w_qkv),
+        (d_mixed, w_qkv),
     )
     df_got = core_swap(df_other)
-    out_sends = [on(k_pair_send, send_shape, (f[1], g)) for f, g in zip(outs, out_got)]
-    out_pair = [bit_swap(s, pair) for s in out_sends]
+    out_own, out_other = on(k_feed_out, out_shapes, (acts[0], w_fc2))
+    out_got = core_swap(run.now(out_other))
+    grad_qkv.step()
+    grad_proj.step()
     input_grad, one_sums = on(
         k_input_back,
         (shape(inputs.shape), shape((8, width))),
-        (inputs, df_own, df_got, d_middle[0], d_middle[1], vectors),
+        (inputs, df_own, df_got, d_middle, vectors),
     )
     small_shape = shape((n, SMALL_ROWS, LANES))
-    grad_proj.step()
     small_mine, small_theirs = on(
         bind(k_small, full, n),
         (small_shape, small_shape),
-        (one_sums, *mid_sums, feeds[0][5], feeds[1][5], *mix_sums),
+        (one_sums, mid_sums, feeds[0][4], feeds[1][4], mix_sums),
         scratch=[pltpu.VMEM((2 * n, SMALL_ROWS, LANES), f32)],
     )
     small_got = core_swap(small_theirs)
-    grad_proj.step()
     grad_feed = grad_feed.sum()
     grad_fc2, fc1_own = grad_feed[:units], grad_feed[units:]
-    fc1_from = bit_swap(fc1_own[2 * rows :], pair)
-    fc1_core = core_swap(fc1_own[rows : 2 * rows])
     small_sum = small_mine + run.now(small_got)
     small_sums = Sums(run, small_sum[few:], small_sum[:few], full)
     grad_qkv.step()
     small_sums.step()
-    outputs = [
-        on(bind(k_output, i), send_shape, (middle[i], f[0], out_got[i], out_pair[i], vectors))
-        for i, f in enumerate(outs)
-    ]
-    outputs = jnp.stack(outputs)
+    grad_qkv.step()
+    grad_proj.step()
+    fc1_from = bit_swap(fc1_own[2 * rows :], pair)
+    fc1_core = core_swap(fc1_own[rows : 2 * rows])
+    small_sums.step()
+    outputs = on(k_output, shape(inputs.shape, b16), (middle, out_own, out_got, out_pair, vectors))
+    small_sums.step()
     fc1_from = run.now(fc1_from)
     fc1_from_core = core_swap(fc1_from[rows:])
-    grad_qkv.step()
-    small_sums.step()
+    grad_proj = grad_proj.sum()
     fc1_rows = on(
         k_columns, shape(fc1_weight.shape), (fc1_own, fc1_from, fc1_core, fc1_from_core)
     )
-    while grad_qkv.steps:
-        grad_qkv.step()
-        small_sums.step()
     small_sums.settle()
 
     final = small_sums.keep[0]
     vector_grads = [final[v, : a.shape[0]] for v, a in enumerate(smalls)]
-    grad_proj = grad_proj.sum()
     qkv_own = grad_qkv.sum()
     qkv_rows = on(
         k_rows, shape((rows, 6 * half)), (qkv_own, core_swap(qkv_own[rows:]))

time: 343 us -> 311 us (0.907)
  Pallas kernels: 151 us -> 129 us
  starting transfers between devices: 51.4 us -> 43.7 us
  local copies, waits for them, and re-layouts: 21.9 us -> 14.6 us
  waiting for transfers between devices: 99.6 us -> 106 us
    pallas_call x30 -> x23, Pallas kernels: 149 us -> 128 us  [call(): pl.pallas_call(kernel, out_shape=outs, in_specs=specs, out_specs=tuple(ou...]
    ppermute x28 -> x24, waiting for transfers between devices: 2.55 us -> 10.4 us  [core_swap(): return lax.ppermute(value, 'seq', [(0, 1), (1, 0)])]
    unnamed x113 -> x98, local copies, waits for them, and re-layouts: 14.9 us -> 8.38 us
    ppermute x36 -> x32, starting transfers between devices: 44.4 us -> 39.8 us  [bit_swap(): return lax.ppermute(value, ('img', 'seq'), pairs)]
    ppermute x28 -> x24, starting transfers between devices: 7.02 us -> 3.97 us  [core_swap(): return lax.ppermute(value, 'seq', [(0, 1), (1, 0)])]
    ppermute x36 -> x32, waiting for transfers between devices: 97.1 us -> 95.8 us  [bit_swap(): return lax.ppermute(value, ('img', 'seq'), pairs)]
  transfers between devices with their start and end apart: 64 -> 56, of which waited for: 22 -> 27; matrix products, arithmetic and copies ran while one was open for 5% -> 5% of each run, Pallas kernels for 32% -> 35%
where the time goes in v1:
time: 311 us; the launch traced here: 305 us
  Pallas kernels  129 us (41%)
  waiting for transfers between devices  106 us (34%)
  starting transfers between devices  43.7 us (14%)
  local copies, waits for them, and re-layouts  14.6 us (5%)
  other arithmetic  9.92 us (3%)
    pallas_call x23, Pallas kernels, call(): pl.pallas_call(kernel, out_shape=outs, in_specs=specs, out_specs=tuple(ou...  128 us
    ppermute x32, waiting for transfers between devices, bit_swap(): return lax.ppermute(value, ('img', 'seq'), pairs)  95.8 us
    ppermute x32, starting transfers between devices, bit_swap(): return lax.ppermute(value, ('img', 'seq'), pairs)  39.8 us
    ppermute x24, waiting for transfers between devices, core_swap(): return lax.ppermute(value, 'seq', [(0, 1), (1, 0)])  10.4 us
    unnamed x98, local copies, waits for them, and re-layouts  8.38 us
  transfers between devices with their start and end apart: 56, of which 27 were waited for; matrix products, arithmetic and copies ran while one was open for 5% of the time, Pallas kernels for 35%

profile of v1, /device:TPU:0, one launch (start us, length us, event | category | flops | bytes accessed | tf_op | source)
XLA Modules:
  0.0 305.4 jit_solution(15601616680088078360)
XLA Ops:
  4.8 1.8 shard_map.254
  9.0 3.8 %collective-permute-start.1 = (bf16[1,64,1664]{2,1,0:T(8,128)(2,1)S(1)}, bf16[1,64,1664]{2,1,0:T(8,128)(2,1)S(1)}, u32[]{:S(2)}, u32[]{:S(2)}) collective-permute-start(bf16[1,64,1664]{2,1,0:T(8,128)(2,1)S(1)} %maximum_bitcast_fusion.1), channel_id=1, source_target_pairs={{0,16},{1,17},{2,18},{3,19},{4,20},{5,21},{6,22},{7,23},{8,24},{9,... | collective-permute-start | bytes 638984 | tf_op jit(solution)/shard_map/ppermute | solution.py:55
  14.5 8.6 %collective-permute-done.1 = bf16[1,64,1664]{2,1,0:T(8,128)(2,1)S(1)} collective-permute-done((bf16[1,64,1664]{2,1,0:T(8,128)(2,1)S(1)}, bf16[1,64,1664]{2,1,0:T(8,128)(2,1)S(1)}, u32[]{:S(2)}, u32[]{:S(2)}) %collective-permute-start.1) | collective-permute-done | bytes 213024 | tf_op jit(solution)/shard_map/ppermute | solution.py:55
  25.6 2.7 collective-permute-done.7
  28.3 6.5 %collective-permute-done.6 = bf16[2,64,1664]{2,1,0:T(8,128)(2,1)S(1)} collective-permute-done((bf16[2,64,1664]{2,1,0:T(8,128)(2,1)S(1)}, bf16[2,64,1664]{2,1,0:T(8,128)(2,1)S(1)}, u32[]{:S(2)}, u32[]{:S(2)}) %collective-permute-start.6) | collective-permute-done | bytes 426016 | tf_op jit(solution)/shard_map/ppermute | solution.py:55
  37.8 4.9 %collective-permute-done.9 = bf16[2,32,1024]{2,1,0:T(8,128)(2,1)S(1)} collective-permute-done((bf16[2,32,1024]{2,1,0:T(8,128)(2,1)S(1)}, bf16[2,32,1024]{2,1,0:T(8,128)(2,1)S(1)}, u32[]{:S(2)}, u32[]{:S(2)}) %collective-permute-start.9) | collective-permute-done | bytes 131104 | tf_op jit(solution)/shard_map/ppermute | solution.py:55
  42.7 5.0 %collective-permute-done.8 = bf16[4,64,1664]{2,1,0:T(8,128)(2,1)S(1)} collective-permute-done((bf16[4,64,1664]{2,1,0:T(8,128)(2,1)S(1)}, bf16[4,64,1664]{2,1,0:T(8,128)(2,1)S(1)}, u32[]{:S(2)}, u32[]{:S(2)}) %collective-permute-start.8) | collective-permute-done | bytes 852000 | tf_op jit(solution)/shard_map/ppermute | solution.py:55
  49.2 3.0 collective-permute-start.11
  52.9 22.2 %collective-permute-done.11 = bf16[1,256,1024]{2,1,0:T(8,128)(2,1)S(1)} collective-permute-done((bf16[1,256,1024]{2,1,0:T(8,128)(2,1)S(1)}, bf16[1,256,1024]{2,1,0:T(8,128)(2,1)S(1)}, u32[]{:S(2)}, u32[]{:S(2)}) %collective-permute-start.11) | collective-permute-done | bytes 524320 | tf_op jit(solution)/shard_map/ppermute | solution.py:55
  76.5 7.0 %shard_map.256 = (bf16[1024,1536]{1,0:T(8,128)(2,1)}, f32[8,1024]{1,0:T(8,128)}, bf16[640,1024]{1,0:T(8,128)(2,1)}, bf16[640,1536]{1,0:T(8,128)(2,1)}) custom-call(s32[5]{0:T(128)} %pad_add_fusion.1.place.refs_0_, bf16[8,64,1664]{2,1,0:T(8,128)(2,1)} %copy-done.1, bf16[8,64,1664]{2,1,0:T(8,128)(2,1)} %copy-done.31, bf16[2,160,1024]{2,1,0:T(8,128)(2,1)} %refs_1_.1, ...), custom_call_target="tpu_custom_call" | custom-call | flops 20999999488 | bytes 1000 | tf_op jit(solution)/shard_map/pallas_call | solution.py:568
  83.5 6.1 %shard_map.257 = (bf16[160,512]{1,0:T(8,128)(2,1)}, bf16[160,512]{1,0:T(8,128)(2,1)}) custom-call(s32[5]{0:T(128)} %pad_add_fusion.1.place.refs_0_, bf16[640,1536]{1,0:T(8,128)(2,1)} %get-tuple-element.153.refs_1_.refs_2_.refs_3_, bf16[640,1536]{1,0:T(8,128)(2,1)} %get-tuple-element.153.refs_1_.refs_2_.refs_3_, ...), custom_call_target="tpu_custom_call" | custom-call | flops 17999998976 | bytes 1000 | tf_op jit(solution)/shard_map/pallas_call | solution.py:568
  90.5 2.8 collective-permute-start.14
  95.0 6.2 %shard_map.258 = (bf16[160,512]{1,0:T(8,128)(2,1)}, bf16[160,512]{1,0:T(8,128)(2,1)}) custom-call(s32[5]{0:T(128)} %pad_add_fusion.1.place.refs_0_, bf16[640,1536]{1,0:T(8,128)(2,1)} %get-tuple-element.153.refs_1_.refs_2_.refs_3_, bf16[640,1536]{1,0:T(8,128)(2,1)} %get-tuple-element.153.refs_1_.refs_2_.refs_3_, ...), custom_call_target="tpu_custom_call" | custom-call | flops 17999998976 | bytes 1000 | tf_op jit(solution)/shard_map/pallas_call | solution.py:568
  101.2 4.6 %collective-permute-done.14.refs_2_ = bf16[8,32,1024]{2,1,0:T(8,128)(2,1)S(1)} collective-permute-done((bf16[8,32,1024]{2,1,0:T(8,128)(2,1)S(1)}, bf16[8,32,1024]{2,1,0:T(8,128)(2,1)S(1)}, u32[]{:S(2)}, u32[]{:S(2)}) %collective-permute-start.14) | collective-permute-done | bytes 524320 | tf_op jit(solution)/shard_map/ppermute | solution.py:55
  106.4 1.8 collective-permute-done.17.refs_7_.refs_5_
  111.6 4.2 %shard_map.259 = (bf16[1024,1024]{1,0:T(8,128)(2,1)}, f32[320,1024]{1,0:T(8,128)}, bf16[320,1024]{1,0:T(8,128)(2,1)}) custom-call(s32[5]{0:T(128)} %pad_add_fusion.1.place.refs_0_, bf16[8,32,1024]{2,1,0:T(8,128)(2,1)} %copy-done.3, bf16[8,32,1024]{2,1,0:T(8,128)(2,1)} %copy-done.18, bf16[8,32,1024]{2,1,0:T(8,128)(2,1)} %copy-done.19, ...), custom_call_target="tpu_custom_call" | custom-call | flops 300000000 | bytes 1000 | tf_op jit(solution)/shard_map/pallas_call | solution.py:568
  116.1 3.6 %collective-permute-done.20.refs_2_ = bf16[4,256,1024]{2,1,0:T(8,128)(2,1)} collective-permute-done((bf16[4,256,1024]{2,1,0:T(8,128)(2,1)S(1)}, bf16[4,256,1024]{2,1,0:T(8,128)(2,1)}, u32[]{:S(2)}, u32[]{:S(2)}) %collective-permute-start.20) | collective-permute-done | bytes 2097184 | tf_op jit(solution)/shard_map/ppermute | solution.py:55
  119.7 4.7 %shard_map.260 = (bf16[1024,1024]{1,0:T(8,128)(2,1)}, bf16[1024,1024]{1,0:T(8,128)(2,1)}) custom-call(s32[5]{0:T(128)} %pad_add_fusion.1.place.refs_0_, bf16[4,256,1024]{2,1,0:T(8,128)(2,1)} %copy-done.17, bf16[4,256,1024]{2,1,0:T(8,128)(2,1)} %collective-permute-done.20.refs_2_, f32[320,1024]{1,0:T(8,128)} %get-tuple-element.163.refs_3_.refs_4_.refs_1_), custom_call_target="tpu_custom_call" | custom-call | flops 13500000256 | bytes 1000 | tf_op jit(solution)/shard_map/pallas_call | solution.py:568
  126.6 9.2 %shard_map.261 = (bf16[640,1024]{1,0:T(8,128)(2,1)}, bf16[640,1024]{1,0:T(8,128)(2,1)}, f32[320,1024]{1,0:T(8,128)}, bf16[320,1024]{1,0:T(8,128)(2,1)}, f32[8,10...) custom-call(s32[5]{0:T(128)} %pad_add_fusion.1.place.refs_0_, ...), custom_call_target="tpu_custom_call" | custom-call | flops 30000001024 | bytes 1000 | tf_op jit(solution)/shard_map/pallas_call | solution.py:568
  135.8 3.1 %collective-permute-done.22.refs_1_ = bf16[320,1024]{1,0:T(8,128)(2,1)S(1)} collective-permute-done((bf16[320,1024]{1,0:T(8,128)(2,1)}, bf16[320,1024]{1,0:T(8,128)(2,1)S(1)}, u32[]{:S(2)}, u32[]{:S(2)}) %collective-permute-start.22) | collective-permute-done | bytes 655392 | tf_op jit(solution)/shard_map/ppermute | solution.py:55
  142.9 9.2 %shard_map.262 = (bf16[640,1024]{1,0:T(8,128)(2,1)}, bf16[640,1024]{1,0:T(8,128)(2,1)}, f32[320,1024]{1,0:T(8,128)}, bf16[320,1024]{1,0:T(8,128)(2,1)}, f32[8,10...) custom-call(s32[5]{0:T(128)} %pad_add_fusion.1.place.refs_0_, bf16[320,1024]{1,0:T(8,128)(2,1)} %copy-done.37, ...), custom_call_target="tpu_custom_call" | custom-call | flops 30000001024 | bytes 1000 | tf_op jit(solution)/shard_map/pallas_call | solution.py:568
  152.1 5.1 %shard_map.263 = (f32[320,1024]{1,0:T(8,128)}, bf16[320,1024]{1,0:T(8,128)(2,1)}) custom-call(s32[5]{0:T(128)} %pad_add_fusion.1.place.refs_0_, bf16[640,1024]{1,0:T(8,128)(2,1)} %get-tuple-element.180.refs_1_.refs_2_, bf16[1024,1024]{1,0:T(8,128)(2,1)} %get-tuple-element.169.refs_6_.refs_2_, f32[8,1024]{1,0:T(8,128)} %get-tuple-element.181.refs_3_.refs_4_), custom_call_target="tpu_custom_call" | custom-call | flops 8999999488 | bytes 1000 | tf_op jit(solution)/shard_map/pallas_call | solution.py:568
  157.7 1.8 collective-permute-done.26.refs_4_
  161.1 3.4 %shard_map.264 = (bf16[320,1024]{1,0:T(8,128)(2,1)}, bf16[320,1024]{1,0:T(8,128)(2,1)}) custom-call(s32[5]{0:T(128)} %pad_add_fusion.1.place.refs_0_, f32[320,1024]{1,0:T(8,128)} %get-tuple-element.178.refs_1_, bf16[320,1024]{1,0:T(8,128)(2,1)} %copy-done.16, f32[320,1024]{1,0:T(8,128)} %get-tuple-element.182.refs_3_.refs_5_, bf16[320,1024]{1,0:T(8,128)(2,1)} %copy-done.15, ...), custom_call_target="tpu_custom_call" | custom-call | flops 600000000 | bytes 1000 | tf_op jit(solution)/shard_map/pallas_call | solution.py:568
  166.2 12.9 %shard_map.265 = (bf16[1024,1024]{1,0:T(8,128)(2,1)}, bf16[1024,1024]{1,0:T(8,128)(2,1)}) custom-call(s32[5]{0:T(128)} %pad_add_fusion.1.place.refs_0_, bf16[640,1024]{1,0:T(8,128)(2,1)} %get-tuple-element.171.refs_1_, bf16[640,1024]{1,0:T(8,128)(2,1)} %get-tuple-element.180.refs_1_.refs_2_, bf16[640,1024]{1,0:T(8,128)(2,1)} %get-tuple-element.188.refs_3_, ...), custom_call_target="tpu_custom_call" | custom-call | flops 44999999488 | bytes 1000 | tf_op jit(solution)/shard_map/pallas_call | solution.py:568
  179.6 1.8 collective-permute-done.28.refs_3_
  182.3 5.9 %shard_map.266 = (f32[320,1024]{1,0:T(8,128)}, bf16[320,1024]{1,0:T(8,128)(2,1)}, bf16[320,512]{1,0:T(8,128)(2,1)}, bf16[320,512]{1,0:T(8,128)(2,1)}, f32[8,1024]{1,0:T(8,128)}) custom-call(s32[5]{0:T(128)} %pad_add_fusion.1.place.refs_0_, f32[320,1024]{1,0:T(8,128)} %get-tuple-element.172.refs_1_, bf16[320,1024]{1,0:T(8,128)(2,1)} %copy-done.40, ...), custom_call_target="tpu_custom_call" | custom-call | flops 89999998976 | bytes 1000 | tf_op jit(solution)/shard_map/pallas_call | solution.py:568
  189.4 2.0 collective-permute-done.29.refs_5_
  193.2 8.4 %shard_map.267 = (bf16[640,1536]{1,0:T(8,128)(2,1)}, f32[16,1536]{1,0:T(8,128)}) custom-call(s32[5]{0:T(128)} %pad_add_fusion.1.place.refs_0_, bf16[640,1536]{1,0:T(8,128)(2,1)} %get-tuple-element.153.refs_1_.refs_2_.refs_3_, bf16[640,1536]{1,0:T(8,128)(2,1)} %get-tuple-element.153.refs_1_.refs_2_.refs_3_, ...), custom_call_target="tpu_custom_call" | custom-call | flops 600000000 | bytes 1000 | tf_op jit(solution)/shard_map/pallas_call | solution.py:568
  202.6 4.6 %shard_map.268 = (bf16[256,1024]{1,0:T(8,128)(2,1)}, bf16[256,1024]{1,0:T(8,128)(2,1)}) custom-call(s32[5]{0:T(128)} %pad_add_fusion.1.place.refs_0_, bf16[160,512]{1,0:T(8,128)(2,1)} %get-tuple-element.157.refs_4_.refs_5_.refs_1_, bf16[160,512]{1,0:T(8,128)(2,1)} %get-tuple-element.162.refs_6_.refs_11_.refs_2_, ...), custom_call_target="tpu_custom_call" | custom-call | flops 600000000 | bytes 1000 | tf_op jit(solution)/shard_map/pallas_call | solution.py:568
  207.7 1.8 fusion.15
  211.0 8.3 %shard_map.269 = (bf16[640,1536]{1,0:T(8,128)(2,1)}, f32[16,1536]{1,0:T(8,128)}) custom-call(s32[5]{0:T(128)} %pad_add_fusion.1.place.refs_0_, bf16[640,1536]{1,0:T(8,128)(2,1)} %get-tuple-element.153.refs_1_.refs_2_.refs_3_, bf16[640,1536]{1,0:T(8,128)(2,1)} %get-tuple-element.153.refs_1_.refs_2_.refs_3_, ...), custom_call_target="tpu_custom_call", output_to_operand_aliasing={{0}: (6, {}), {1}: (7, {})} | custom-call | flops 24000000000 | bytes 1000 | tf_op jit(solution)/shard_map/pallas_call | solution.py:568
  219.3 6.4 %shard_map.270 = (bf16[512,1536]{1,0:T(8,128)(2,1)}, bf16[512,1536]{1,0:T(8,128)(2,1)}) custom-call(s32[5]{0:T(128)} %pad_add_fusion.1.place.refs_0_, bf16[640,1024]{1,0:T(8,128)(2,1)} %get-tuple-element.209.refs_1_, bf16[640,1536]{1,0:T(8,128)(2,1)} %get-tuple-element.205.refs_2_.refs_1_, f32[16,1536]{1,0:T(8,128)} %get-tuple-element.210.refs_3_.refs_5_), custom_call_target="tpu_custom_call" | custom-call | flops 26100000768 | bytes 1000 | tf_op jit(solution)/shard_map/pallas_call | solution.py:568
  228.7 6.3 %shard_map.271 = (f32[2,160,1024]{2,1,0:T(8,128)}, bf16[2,160,1024]{2,1,0:T(8,128)(2,1)}) custom-call(s32[5]{0:T(128)} %pad_add_fusion.1.place.refs_0_, bf16[640,1536]{1,0:T(8,128)(2,1)} %get-tuple-element.205.refs_2_.refs_1_, bf16[1024,1536]{1,0:T(8,128)(2,1)} %get-tuple-element.206.refs_2_, bf16[512,1536]{1,0:T(8,128)(2,1)} %get-tuple-element.213.refs_3_), custom_call_target="tpu_custom_call" | custom-call | flops 17999998976 | bytes 1000 | tf_op jit(solution)/shard_map/pallas_call | solution.py:568
  235.0 4.6 %shard_map.272 = (f32[320,1024]{1,0:T(8,128)}, bf16[320,1024]{1,0:T(8,128)(2,1)}) custom-call(s32[5]{0:T(128)} %pad_add_fusion.1.place.refs_0_, bf16[640,1024]{1,0:T(8,128)(2,1)} %get-tuple-element.171.refs_1_, bf16[1024,1024]{1,0:T(8,128)(2,1)} %get-tuple-element.169.refs_6_.refs_2_, f32[2,160,1024]{2,1,0:T(8,128)} %get-tuple-element.214.refs_3_.refs_2_), custom_call_target="tpu_custom_call" | custom-call | flops 8999999488 | bytes 1000 | tf_op jit(solution)/shard_map/pallas_call | solution.py:568
  243.7 4.6 %collective-permute-done.40 = bf16[8,64,1536]{2,1,0:T(8,128)(2,1)S(1)} collective-permute-done((bf16[8,64,1536]{2,1,0:T(8,128)(2,1)}, bf16[8,64,1536]{2,1,0:T(8,128)(2,1)S(1)}, u32[]{:S(2)}, u32[]{:S(2)}) %collective-permute-start.40) | collective-permute-done | bytes 1572896 | tf_op jit(solution)/shard_map/ppermute | solution.py:55
  248.6 2.4 collective-permute-start.44
  252.0 4.2 %shard_map.273 = (f32[2,160,1024]{2,1,0:T(8,128)}, f32[8,1024]{1,0:T(8,128)}) custom-call(s32[5]{0:T(128)} %pad_add_fusion.1.place.refs_0_, bf16[2,160,1024]{2,1,0:T(8,128)(2,1)} %refs_1_.1, f32[2,160,1024]{2,1,0:T(8,128)} %get-tuple-element.214.refs_3_.refs_2_, bf16[2,160,1024]{2,1,0:T(8,128)(2,1)} %copy-done.38, f32[320,1024]{1,0:T(8,128)} %get-tuple-element.220.refs_4_, ...), custom_call_target="tpu_custom_call" | custom-call | flops 12899999744 | bytes 1000 | tf_op jit(solution)/shard_map/pallas_call | solution.py:568
  256.2 2.0 shard_map.274
  258.2 7.8 %collective-permute-done.42 = bf16[1,256,1024]{2,1,0:T(8,128)(2,1)} collective-permute-done((bf16[1,256,1024]{2,1,0:T(8,128)(2,1)}, bf16[1,256,1024]{2,1,0:T(8,128)(2,1)}, u32[]{:S(2)}, u32[]{:S(2)}) %collective-permute-start.42) | collective-permute-done | bytes 524320 | tf_op jit(solution)/shard_map/ppermute | solution.py:55
  270.3 2.1 collective-permute-done.43
  272.4 9.9 %collective-permute-done.47 = bf16[2,64,1536]{2,1,0:T(8,128)(2,1)S(1)} collective-permute-done((bf16[2,64,1536]{2,1,0:T(8,128)(2,1)S(1)}, bf16[2,64,1536]{2,1,0:T(8,128)(2,1)S(1)}, u32[]{:S(2)}, u32[]{:S(2)}) %collective-permute-start.47) | collective-permute-done | bytes 393248 | tf_op jit(solution)/shard_map/ppermute | solution.py:55
  282.7 3.3 %collective-permute-done.45 = f32[4,8,128]{2,1,0:T(8,128)S(1)} collective-permute-done((f32[4,8,128]{2,1,0:T(8,128)S(1)}, f32[4,8,128]{2,1,0:T(8,128)S(1)}, u32[]{:S(2)}, u32[]{:S(2)}) %collective-permute-start.45) | collective-permute-done | bytes 16416 | tf_op jit(solution)/shard_map/ppermute | solution.py:55
  287.4 1.8 collective-permute-start.54
  289.2 3.3 %shard_map.275.refs_5_ = bf16[2,160,1024]{2,1,0:T(8,128)(2,1)} custom-call(s32[5]{0:T(128)} %pad_add_fusion.1.place.refs_0_, f32[320,1024]{1,0:T(8,128)} %get-tuple-element.163.refs_3_.refs_4_.refs_1_, f32[320,1024]{1,0:T(8,128)} %get-tuple-element.225.refs_6_.refs_2_, bf16[320,1024]{1,0:T(8,128)(2,1)} %collective-permute-done.36.refs_3_, ...), custom_call_target="tpu_custom_call" | custom-call | flops 12000000000 | bytes 1000 | tf_op jit(solution)/shard_map/pallas_call | solution.py:568
  293.7 2.6 collective-permute-done.53
  297.8 2.1 shard_map.276.refs_3_
  303.4 1.8 shard_map.277
  (234 shorter events, 61.6 us)
Async XLA Ops:
  3.0 9.8 %collective-permute-start.2 = (bf16[2,32,1024]{2,1,0:T(8,128)(2,1)}, bf16[2,32,1024]{2,1,0:T(8,128)(2,1)S(1)}, u32[]{:S(2)}, u32[]{:S(2)}) collective-permute-start(bf16[2,32,1024]{2,1,0:T(8,128)(2,1)} %get-tuple-element.139), channel_id=1, source_target_pairs={{0,1},{1,0},{2,3},{3,2},{4,5},{5,4},{6,7},{7,6},{8,9},{9,8},{10,11... | collective-permute-start | bytes 393224 | tf_op jit(solution)/shard_map/ppermute | solution.py:47
  6.8 16.4 %collective-permute-start.5 = (bf16[2,160,1024]{2,1,0:T(8,128)(2,1)S(1)}, bf16[2,160,1024]{2,1,0:T(8,128)(2,1)S(1)}, u32[]{:S(2)}, u32[]{:S(2)}) collective-permute-start(bf16[2,160,1024]{2,1,0:T(8,128)(2,1)S(1)} %broadcast_select_fusion.refs_3_.refs_5_), channel_id=1, source_target_pairs={{0,1},{1,0},{2,3},{3,2},{4,5},{5,4},{6,7},{7,6},{8,9},{9,8},{10,11... | collective-permute-start | bytes 1966088 | tf_op jit(solution)/shard_map/ppermute | solution.py:47
  7.4 15.9 %collective-permute-start.4 = (bf16[2,160,1024]{2,1,0:T(8,128)(2,1)S(1)}, bf16[2,160,1024]{2,1,0:T(8,128)(2,1)S(1)}, u32[]{:S(2)}, u32[]{:S(2)}) collective-permute-start(bf16[2,160,1024]{2,1,0:T(8,128)(2,1)S(1)} %copy-done.14), channel_id=1, source_target_pairs={{0,1},{1,0},{2,3},{3,2},{4,5},{5,4},{6,7},{7,6},{8,9},{9,8},{10,11... | collective-permute-start | bytes 1966088 | tf_op jit(solution)/shard_map/ppermute | solution.py:47
  9.0 14.1 %collective-permute-start.1 = (bf16[1,64,1664]{2,1,0:T(8,128)(2,1)S(1)}, bf16[1,64,1664]{2,1,0:T(8,128)(2,1)S(1)}, u32[]{:S(2)}, u32[]{:S(2)}) collective-permute-start(bf16[1,64,1664]{2,1,0:T(8,128)(2,1)S(1)} %maximum_bitcast_fusion.1), channel_id=1, source_target_pairs={{0,16},{1,17},{2,18},{3,19},{4,20},{5,21},{6,22},{7,23},{8,24},{9,... | collective-permute-start | bytes 638984 | tf_op jit(solution)/shard_map/ppermute | solution.py:55
  12.9 10.3 %collective-permute-start.3 = (bf16[64,1024]{1,0:T(8,128)(2,1)S(1)}, bf16[64,1024]{1,0:T(8,128)(2,1)S(1)}, u32[]{:S(2)}, u32[]{:S(2)}) collective-permute-start(bf16[64,1024]{1,0:T(8,128)(2,1)S(1)} %pad_maximum_fusion.5), channel_id=1, source_target_pairs={{0,8},{1,9},{2,10},{3,11},{4,12},{5,13},{6,14},{7,15},{8,0},{9,1},... | collective-permute-start | bytes 393224 | tf_op jit(solution)/shard_map/ppermute | solution.py:55
  23.2 11.6 %collective-permute-start.6 = (bf16[2,64,1664]{2,1,0:T(8,128)(2,1)S(1)}, bf16[2,64,1664]{2,1,0:T(8,128)(2,1)S(1)}, u32[]{:S(2)}, u32[]{:S(2)}) collective-permute-start(bf16[2,64,1664]{2,1,0:T(8,128)(2,1)S(1)} %pad_maximum_fusion.3), channel_id=1, source_target_pairs={{0,8},{1,9},{2,10},{3,11},{4,12},{5,13},{6,14},{7,15},{8,0},{9,1},... | collective-permute-start | bytes 1277960 | tf_op jit(solution)/shard_map/ppermute | solution.py:55
  24.1 4.3 %collective-permute-start.7 = (bf16[1,32,1024]{2,1,0:T(8,128)(2,1)S(1)}, bf16[1,32,1024]{2,1,0:T(8,128)(2,1)S(1)}, u32[]{:S(2)}, u32[]{:S(2)}) collective-permute-start(bf16[1,32,1024]{2,1,0:T(8,128)(2,1)S(1)} %bitcast.76), channel_id=1, source_target_pairs={{0,2},{1,5},{2,0},{3,7},{4,6},{5,1},{6,4},{7,3},{8,10},{9,13},{10,... | collective-permute-start | bytes 196616 | tf_op jit(solution)/shard_map/ppermute | solution.py:55
  34.9 12.9 %collective-permute-start.8 = (bf16[4,64,1664]{2,1,0:T(8,128)(2,1)S(1)}, bf16[4,64,1664]{2,1,0:T(8,128)(2,1)S(1)}, u32[]{:S(2)}, u32[]{:S(2)}) collective-permute-start(bf16[4,64,1664]{2,1,0:T(8,128)(2,1)S(1)} %pad_maximum_fusion.2), channel_id=1, source_target_pairs={{0,2},{1,5},{2,0},{3,7},{4,6},{5,1},{6,4},{7,3},{8,10},{9,13},{10,... | collective-permute-start | bytes 2555912 | tf_op jit(solution)/shard_map/ppermute | solution.py:55
  36.3 6.4 %collective-permute-start.9 = (bf16[2,32,1024]{2,1,0:T(8,128)(2,1)S(1)}, bf16[2,32,1024]{2,1,0:T(8,128)(2,1)S(1)}, u32[]{:S(2)}, u32[]{:S(2)}) collective-permute-start(bf16[2,32,1024]{2,1,0:T(8,128)(2,1)S(1)} %pad_maximum_fusion.6), channel_id=1, source_target_pairs={{0,4},{1,3},{2,6},{3,1},{4,0},{5,7},{6,2},{7,5},{8,12},{9,11},{10,... | collective-permute-start | bytes 393224 | tf_op jit(solution)/shard_map/ppermute | solution.py:55
  48.0 27.3 %collective-permute-start.10 = (bf16[8,64,1664]{2,1,0:T(8,128)(2,1)S(1)}, bf16[8,64,1664]{2,1,0:T(8,128)(2,1)S(1)}, u32[]{:S(2)}, u32[]{:S(2)}) collective-permute-start(bf16[8,64,1664]{2,1,0:T(8,128)(2,1)S(1)} %pad_maximum_fusion.sent), channel_id=1, source_target_pairs={{0,4},{1,3},{2,6},{3,1},{4,0},{5,7},{6,2},{7,5},{8,12},{9,11},{10,... | collective-permute-start | bytes 5111816 | tf_op jit(solution)/shard_map/ppermute | solution.py:55
  49.2 25.9 %collective-permute-start.11 = (bf16[1,256,1024]{2,1,0:T(8,128)(2,1)S(1)}, bf16[1,256,1024]{2,1,0:T(8,128)(2,1)S(1)}, u32[]{:S(2)}, u32[]{:S(2)}) collective-permute-start(bf16[1,256,1024]{2,1,0:T(8,128)(2,1)S(1)} %maximum_bitcast_fusion), channel_id=1, source_target_pairs={{0,16},{1,17},{2,18},{3,19},{4,20},{5,21},{6,22},{7,23},{8,24},{9,... | collective-permute-start | bytes 1572872 | tf_op jit(solution)/shard_map/ppermute | solution.py:55
  75.3 15.2 %collective-permute-start.13 = (bf16[2,256,1024]{2,1,0:T(8,128)(2,1)S(1)}, bf16[2,256,1024]{2,1,0:T(8,128)(2,1)S(1)}, u32[]{:S(2)}, u32[]{:S(2)}) collective-permute-start(bf16[2,256,1024]{2,1,0:T(8,128)(2,1)S(1)} %pad_maximum_fusion.1), channel_id=1, source_target_pairs={{0,2},{1,5},{2,0},{3,7},{4,6},{5,1},{6,4},{7,3},{8,10},{9,13},{10,... | collective-permute-start | bytes 3145736 | tf_op jit(solution)/shard_map/ppermute | solution.py:55
  75.9 14.6 %collective-permute-start.12 = (bf16[4,32,1024]{2,1,0:T(8,128)(2,1)S(1)}, bf16[4,32,1024]{2,1,0:T(8,128)(2,1)S(1)}, u32[]{:S(2)}, u32[]{:S(2)}) collective-permute-start(bf16[4,32,1024]{2,1,0:T(8,128)(2,1)S(1)} %pad_maximum_fusion.4), channel_id=1, source_target_pairs={{0,16},{1,17},{2,18},{3,19},{4,20},{5,21},{6,22},{7,23},{8,24},{9,... | collective-permute-start | bytes 786440 | tf_op jit(solution)/shard_map/ppermute | solution.py:55
  90.5 15.3 %collective-permute-start.14 = (bf16[8,32,1024]{2,1,0:T(8,128)(2,1)S(1)}, bf16[8,32,1024]{2,1,0:T(8,128)(2,1)S(1)}, u32[]{:S(2)}, u32[]{:S(2)}) collective-permute-start(bf16[8,32,1024]{2,1,0:T(8,128)(2,1)S(1)} %constant_dynamic-update-slice_fusion.refs_1_), channel_id=1, source_target_pairs={{0,8},{1,9},{2,10},{3,11},{4,12},{5,13},{6,14},{7,15},{8,0},{9,1},... | collective-permute-start | bytes 1572872 | tf_op jit(solution)/shard_map/ppermute | solution.py:55
  93.3 16.6 %collective-permute-start.15 = (bf16[8,32,1024]{2,1,0:T(8,128)(2,1)S(1)}, bf16[8,32,1024]{2,1,0:T(8,128)(2,1)S(1)}, u32[]{:S(2)}, u32[]{:S(2)}) collective-permute-start(bf16[8,32,1024]{2,1,0:T(8,128)(2,1)S(1)} %constant_dynamic-update-slice_fusion.refs_1_), channel_id=1, source_target_pairs={{0,1},{1,0},{2,3},{3,2},{4,5},{5,4},{6,7},{7,6},{8,9},{9,8},{10,11... | collective-permute-start | bytes 1572872 | tf_op jit(solution)/shard_map/ppermute | solution.py:47
  93.5 26.2 %collective-permute-start.20 = (bf16[4,256,1024]{2,1,0:T(8,128)(2,1)S(1)}, bf16[4,256,1024]{2,1,0:T(8,128)(2,1)}, u32[]{:S(2)}, u32[]{:S(2)}) collective-permute-start(bf16[4,256,1024]{2,1,0:T(8,128)(2,1)S(1)} %constant_dynamic-update-slice_fusion.2.refs_1_), channel_id=1, source_target_pairs={{0,4},{1,3},{2,6},{3,1},{4,0},{5,7},{6,2},{7,5},{8,12},{9,11},{10,... | collective-permute-start | bytes 6291464 | tf_op jit(solution)/shard_map/ppermute | solution.py:55
  105.8 4.1 %collective-permute-start.16 = (bf16[8,32,1024]{2,1,0:T(8,128)(2,1)S(1)}, bf16[8,32,1024]{2,1,0:T(8,128)(2,1)S(1)}, u32[]{:S(2)}, u32[]{:S(2)}) collective-permute-start(bf16[8,32,1024]{2,1,0:T(8,128)(2,1)S(1)} %collective-permute-done.14.refs_2_), channel_id=1, source_target_pairs={{0,1},{1,0},{2,3},{3,2},{4,5},{5,4},{6,7},{7,6},{8,9},{9,8},{10,11... | collective-permute-start | bytes 1572872 | tf_op jit(solution)/shard_map/ppermute | solution.py:47
  106.3 3.6 %collective-permute-start.18 = (bf16[160,512]{1,0:T(8,128)(2,1)}, bf16[160,512]{1,0:T(8,128)(2,1)S(1)}, u32[]{:S(2)}, u32[]{:S(2)}) collective-permute-start(bf16[160,512]{1,0:T(8,128)(2,1)} %get-tuple-element.161.refs_4_), channel_id=1, source_target_pairs={{0,1},{1,0},{2,3},{3,2},{4,5},{5,4},{6,7},{7,6},{8,9},{9,8},{10,11... | collective-permute-start | bytes 491528 | tf_op jit(solution)/shard_map/ppermute | solution.py:47
  108.2 17.6 %collective-permute-start.21 = (bf16[2,160,1024]{2,1,0:T(8,128)(2,1)S(1)}, bf16[2,160,1024]{2,1,0:T(8,128)(2,1)S(1)}, u32[]{:S(2)}, u32[]{:S(2)}) collective-permute-start(bf16[2,160,1024]{2,1,0:T(8,128)(2,1)S(1)} %broadcast_select_fusion.refs_3_.refs_5_), channel_id=1, source_target_pairs={{0,8},{1,9},{2,10},{3,11},{4,12},{5,13},{6,14},{7,15},{8,0},{9,1},... | collective-permute-start | bytes 1966088 | tf_op jit(solution)/shard_map/ppermute | solution.py:55
  115.8 9.9 %collective-permute-start.19 = (bf16[320,1024]{1,0:T(8,128)(2,1)}, bf16[320,1024]{1,0:T(8,128)(2,1)S(1)}, u32[]{:S(2)}, u32[]{:S(2)}) collective-permute-start(bf16[320,1024]{1,0:T(8,128)(2,1)} %get-tuple-element.164.refs_1_), channel_id=1, source_target_pairs={{0,1},{1,0},{2,3},{3,2},{4,5},{5,4},{6,7},{7,6},{8,9},{9,8},{10,11... | collective-permute-start | bytes 1966088 | tf_op jit(solution)/shard_map/ppermute | solution.py:47
  115.8 23.2 %collective-permute-start.22 = (bf16[320,1024]{1,0:T(8,128)(2,1)}, bf16[320,1024]{1,0:T(8,128)(2,1)S(1)}, u32[]{:S(2)}, u32[]{:S(2)}) collective-permute-start(bf16[320,1024]{1,0:T(8,128)(2,1)} %get-tuple-element.164.refs_1_), channel_id=1, source_target_pairs={{0,8},{1,9},{2,10},{3,11},{4,12},{5,13},{6,14},{7,15},{8,0},{9,1},... | collective-permute-start | bytes 1966088 | tf_op jit(solution)/shard_map/ppermute | solution.py:55
  164.4 17.0 %collective-permute-start.28 = (bf16[320,1024]{1,0:T(8,128)(2,1)}, bf16[320,1024]{1,0:T(8,128)(2,1)S(1)}, u32[]{:S(2)}, u32[]{:S(2)}) collective-permute-start(bf16[320,1024]{1,0:T(8,128)(2,1)} %get-tuple-element.194.refs_9_), channel_id=1, source_target_pairs={{0,8},{1,9},{2,10},{3,11},{4,12},{5,13},{6,14},{7,15},{8,0},{9,1},... | collective-permute-start | bytes 1966088 | tf_op jit(solution)/shard_map/ppermute | solution.py:55
  166.2 13.4 %collective-permute-start.27 = (bf16[320,1024]{1,0:T(8,128)(2,1)S(1)}, bf16[320,1024]{1,0:T(8,128)(2,1)S(1)}, u32[]{:S(2)}, u32[]{:S(2)}) collective-permute-start(bf16[320,1024]{1,0:T(8,128)(2,1)S(1)} %copy-done.34), channel_id=1, source_target_pairs={{0,1},{1,0},{2,3},{3,2},{4,5},{5,4},{6,7},{7,6},{8,9},{9,8},{10,11... | collective-permute-start | bytes 1966088 | tf_op jit(solution)/shard_map/ppermute | solution.py:47
  179.1 30.4 %collective-permute-start.30 = (bf16[4,256,1024]{2,1,0:T(8,128)(2,1)}, bf16[4,256,1024]{2,1,0:T(8,128)(2,1)S(1)}, u32[]{:S(2)}, u32[]{:S(2)}) collective-permute-start(bf16[4,256,1024]{2,1,0:T(8,128)(2,1)} %bitcast.88), channel_id=1, source_target_pairs={{0,4},{1,3},{2,6},{3,1},{4,0},{5,7},{6,2},{7,5},{8,12},{9,11},{10,... | collective-permute-start | bytes 6291464 | tf_op jit(solution)/shard_map/ppermute | solution.py:55
  188.2 13.4 %collective-permute-start.33 = (bf16[320,1024]{1,0:T(8,128)(2,1)}, bf16[320,1024]{1,0:T(8,128)(2,1)S(1)}, u32[]{:S(2)}, u32[]{:S(2)}) collective-permute-start(bf16[320,1024]{1,0:T(8,128)(2,1)} %get-tuple-element.202.refs_9_), channel_id=1, source_target_pairs={{0,1},{1,0},{2,3},{3,2},{4,5},{5,4},{6,7},{7,6},{8,9},{9,8},{10,11... | collective-permute-start | bytes 1966088 | tf_op jit(solution)/shard_map/ppermute | solution.py:47
  188.2 3.2 %collective-permute-start.29 = (bf16[320,512]{1,0:T(8,128)(2,1)}, bf16[320,512]{1,0:T(8,128)(2,1)S(1)}, u32[]{:S(2)}, u32[]{:S(2)}) collective-permute-start(bf16[320,512]{1,0:T(8,128)(2,1)} %get-tuple-element.198), channel_id=1, source_target_pairs={{0,1},{1,0},{2,3},{3,2},{4,5},{5,4},{6,7},{7,6},{8,9},{9,8},{10,11... | collective-permute-start | bytes 983048 | tf_op jit(solution)/shard_map/ppermute | solution.py:47
  188.7 12.9 %collective-permute-start.31 = (bf16[160,512]{1,0:T(8,128)(2,1)S(1)}, bf16[160,512]{1,0:T(8,128)(2,1)S(1)}, u32[]{:S(2)}, u32[]{:S(2)}) collective-permute-start(bf16[160,512]{1,0:T(8,128)(2,1)S(1)} %copy-done.8), channel_id=1, source_target_pairs={{0,1},{1,0},{2,3},{3,2},{4,5},{5,4},{6,7},{7,6},{8,9},{9,8},{10,11... | collective-permute-start | bytes 491528 | tf_op jit(solution)/shard_map/ppermute | solution.py:47
  188.8 12.8 %collective-permute-start.32 = (bf16[160,512]{1,0:T(8,128)(2,1)S(1)}, bf16[160,512]{1,0:T(8,128)(2,1)S(1)}, u32[]{:S(2)}, u32[]{:S(2)}) collective-permute-start(bf16[160,512]{1,0:T(8,128)(2,1)S(1)} %copy-done.2), channel_id=1, source_target_pairs={{0,1},{1,0},{2,3},{3,2},{4,5},{5,4},{6,7},{7,6},{8,9},{9,8},{10,11... | collective-permute-start | bytes 491528 | tf_op jit(solution)/shard_map/ppermute | solution.py:47
  191.5 94.6 %collective-permute-start.37 = (bf16[320,1024]{1,0:T(8,128)(2,1)}, bf16[320,1024]{1,0:T(8,128)(2,1)}, u32[]{:S(2)}, u32[]{:S(2)}) collective-permute-start(bf16[320,1024]{1,0:T(8,128)(2,1)} %get-tuple-element.218), channel_id=1, source_target_pairs={{0,8},{1,9},{2,10},{3,11},{4,12},{5,13},{6,14},{7,15},{8,0},{9,1},... | collective-permute-start | bytes 1966088 | tf_op jit(solution)/shard_map/ppermute | solution.py:55
  207.2 21.5 %collective-permute-start.34 = (bf16[8,32,1024]{2,1,0:T(8,128)(2,1)}, bf16[8,32,1024]{2,1,0:T(8,128)(2,1)}, u32[]{:S(2)}, u32[]{:S(2)}) collective-permute-start(bf16[8,32,1024]{2,1,0:T(8,128)(2,1)} %bitcast.90), channel_id=1, source_target_pairs={{0,4},{1,3},{2,6},{3,1},{4,0},{5,7},{6,2},{7,5},{8,12},{9,11},{10,... | collective-permute-start | bytes 1572872 | tf_op jit(solution)/shard_map/ppermute | solution.py:55
  210.4 18.3 %collective-permute-start.35 = (bf16[2,256,1024]{2,1,0:T(8,128)(2,1)S(1)}, bf16[2,256,1024]{2,1,0:T(8,128)(2,1)S(1)}, u32[]{:S(2)}, u32[]{:S(2)}) collective-permute-start(bf16[2,256,1024]{2,1,0:T(8,128)(2,1)S(1)} %get-tuple-element.261), channel_id=1, source_target_pairs={{0,2},{1,5},{2,0},{3,7},{4,6},{5,1},{6,4},{7,3},{8,10},{9,13},{10,... | collective-permute-start | bytes 3145736 | tf_op jit(solution)/shard_map/ppermute | solution.py:55
  225.7 22.6 %collective-permute-start.40 = (bf16[8,64,1536]{2,1,0:T(8,128)(2,1)}, bf16[8,64,1536]{2,1,0:T(8,128)(2,1)S(1)}, u32[]{:S(2)}, u32[]{:S(2)}) collective-permute-start(bf16[8,64,1536]{2,1,0:T(8,128)(2,1)} %bitcast.89), channel_id=1, source_target_pairs={{0,4},{1,3},{2,6},{3,1},{4,0},{5,7},{6,2},{7,5},{8,12},{9,11},{10,... | collective-permute-start | bytes 4718600 | tf_op jit(solution)/shard_map/ppermute | solution.py:55
  240.6 25.4 %collective-permute-start.42 = (bf16[1,256,1024]{2,1,0:T(8,128)(2,1)}, bf16[1,256,1024]{2,1,0:T(8,128)(2,1)}, u32[]{:S(2)}, u32[]{:S(2)}) collective-permute-start(bf16[1,256,1024]{2,1,0:T(8,128)(2,1)} %fusion.3), channel_id=1, source_target_pairs={{0,16},{1,17},{2,18},{3,19},{4,20},{5,21},{6,22},{7,23},{8,24},{9,... | collective-permute-start | bytes 1572872 | tf_op jit(solution)/shard_map/ppermute | solution.py:55
  242.1 6.5 %collective-permute-start.39 = (bf16[4,32,1024]{2,1,0:T(8,128)(2,1)S(1)}, bf16[4,32,1024]{2,1,0:T(8,128)(2,1)S(1)}, u32[]{:S(2)}, u32[]{:S(2)}) collective-permute-start(bf16[4,32,1024]{2,1,0:T(8,128)(2,1)S(1)} %get-tuple-element.273), channel_id=1, source_target_pairs={{0,2},{1,5},{2,0},{3,7},{4,6},{5,1},{6,4},{7,3},{8,10},{9,13},{10,... | collective-permute-start | bytes 786440 | tf_op jit(solution)/shard_map/ppermute | solution.py:55
  243.6 7.5 %collective-permute-start.38 = (bf16[2,160,1024]{2,1,0:T(8,128)(2,1)S(1)}, bf16[2,160,1024]{2,1,0:T(8,128)(2,1)S(1)}, u32[]{:S(2)}, u32[]{:S(2)}) collective-permute-start(bf16[2,160,1024]{2,1,0:T(8,128)(2,1)S(1)} %copy-done.36), channel_id=1, source_target_pairs={{0,1},{1,0},{2,3},{3,2},{4,5},{5,4},{6,7},{7,6},{8,9},{9,8},{10,11... | collective-permute-start | bytes 1966088 | tf_op jit(solution)/shard_map/ppermute | solution.py:47
  248.2 39.1 %collective-permute-start.36 = (bf16[320,1024]{1,0:T(8,128)(2,1)}, bf16[320,1024]{1,0:T(8,128)(2,1)}, u32[]{:S(2)}, u32[]{:S(2)}) collective-permute-start(bf16[320,1024]{1,0:T(8,128)(2,1)} %get-tuple-element.217), channel_id=1, source_target_pairs={{0,1},{1,0},{2,3},{3,2},{4,5},{5,4},{6,7},{7,6},{8,9},{9,8},{10,11... | collective-permute-start | bytes 1966088 | tf_op jit(solution)/shard_map/ppermute | solution.py:47
  248.6 21.3 %collective-permute-start.44 = (bf16[4,64,1536]{2,1,0:T(8,128)(2,1)S(1)}, bf16[4,64,1536]{2,1,0:T(8,128)(2,1)S(1)}, u32[]{:S(2)}, u32[]{:S(2)}) collective-permute-start(bf16[4,64,1536]{2,1,0:T(8,128)(2,1)S(1)} %get-tuple-element.265), channel_id=1, source_target_pairs={{0,2},{1,5},{2,0},{3,7},{4,6},{5,1},{6,4},{7,3},{8,10},{9,13},{10,... | collective-permute-start | bytes 2359304 | tf_op jit(solution)/shard_map/ppermute | solution.py:55
  251.2 31.1 %collective-permute-start.46 = (bf16[2,32,1024]{2,1,0:T(8,128)(2,1)S(1)}, bf16[2,32,1024]{2,1,0:T(8,128)(2,1)S(1)}, u32[]{:S(2)}, u32[]{:S(2)}) collective-permute-start(bf16[2,32,1024]{2,1,0:T(8,128)(2,1)S(1)} %get-tuple-element.271), channel_id=1, source_target_pairs={{0,8},{1,9},{2,10},{3,11},{4,12},{5,13},{6,14},{7,15},{8,0},{9,1},... | collective-permute-start | bytes 393224 | tf_op jit(solution)/shard_map/ppermute | solution.py:55
  268.4 4.0 %collective-permute-start.43 = (f32[8,8,128]{2,1,0:T(8,128)S(1)}, f32[8,8,128]{2,1,0:T(8,128)S(1)}, u32[]{:S(2)}, u32[]{:S(2)}) collective-permute-start(f32[8,8,128]{2,1,0:T(8,128)S(1)} %slice.288), channel_id=1, source_target_pairs={{0,4},{1,3},{2,6},{3,1},{4,0},{5,7},{6,2},{7,5},{8,12},{9,11},{10,... | collective-permute-start | bytes 98312 | tf_op jit(solution)/shard_map/ppermute | solution.py:55
  270.2 12.1 %collective-permute-start.47 = (bf16[2,64,1536]{2,1,0:T(8,128)(2,1)S(1)}, bf16[2,64,1536]{2,1,0:T(8,128)(2,1)S(1)}, u32[]{:S(2)}, u32[]{:S(2)}) collective-permute-start(bf16[2,64,1536]{2,1,0:T(8,128)(2,1)S(1)} %get-tuple-element.259), channel_id=1, source_target_pairs={{0,8},{1,9},{2,10},{3,11},{4,12},{5,13},{6,14},{7,15},{8,0},{9,1},... | collective-permute-start | bytes 1179656 | tf_op jit(solution)/shard_map/ppermute | solution.py:55
  272.4 20.0 %collective-permute-start.50 = (f32[64,1024]{1,0:T(8,128)S(1)}, f32[64,1024]{1,0:T(8,128)S(1)}, u32[]{:S(2)}, u32[]{:S(2)}) collective-permute-start(f32[64,1024]{1,0:T(8,128)S(1)} %slice_bitcast_fusion.2), channel_id=1, source_target_pairs={{0,8},{1,9},{2,10},{3,11},{4,12},{5,13},{6,14},{7,15},{8,0},{9,1},... | collective-permute-start | bytes 786440 | tf_op jit(solution)/shard_map/ppermute | solution.py:55
  282.3 14.8 %collective-permute-start.51 = (f32[32,1024]{1,0:T(8,128)S(1)}, f32[32,1024]{1,0:T(8,128)S(1)}, u32[]{:S(2)}, u32[]{:S(2)}) collective-permute-start(f32[32,1024]{1,0:T(8,128)S(1)} %slice_bitcast_fusion.4), channel_id=1, source_target_pairs={{0,1},{1,0},{2,3},{3,2},{4,5},{5,4},{6,7},{7,6},{8,9},{9,8},{10,11... | collective-permute-start | bytes 393224 | tf_op jit(solution)/shard_map/ppermute | solution.py:47
  282.3 3.7 %collective-permute-start.45 = (f32[4,8,128]{2,1,0:T(8,128)S(1)}, f32[4,8,128]{2,1,0:T(8,128)S(1)}, u32[]{:S(2)}, u32[]{:S(2)}) collective-permute-start(f32[4,8,128]{2,1,0:T(8,128)S(1)} %get-tuple-element.281), channel_id=1, source_target_pairs={{0,2},{1,5},{2,0},{3,7},{4,6},{5,1},{6,4},{7,3},{8,10},{9,13},{10,... | collective-permute-start | bytes 49160 | tf_op jit(solution)/shard_map/ppermute | solution.py:55
  286.0 10.4 %collective-permute-start.53 = (bf16[1,32,1024]{2,1,0:T(8,128)(2,1)S(1)}, bf16[1,32,1024]{2,1,0:T(8,128)(2,1)S(1)}, u32[]{:S(2)}, u32[]{:S(2)}) collective-permute-start(bf16[1,32,1024]{2,1,0:T(8,128)(2,1)S(1)} %fusion.11), channel_id=1, source_target_pairs={{0,16},{1,17},{2,18},{3,19},{4,20},{5,21},{6,22},{7,23},{8,24},{9,... | collective-permute-start | bytes 196616 | tf_op jit(solution)/shard_map/ppermute | solution.py:55
  286.1 6.3 %collective-permute-start.48 = (f32[2,8,128]{2,1,0:T(8,128)S(1)}, f32[2,8,128]{2,1,0:T(8,128)S(1)}, u32[]{:S(2)}, u32[]{:S(2)}) collective-permute-start(f32[2,8,128]{2,1,0:T(8,128)S(1)} %get-tuple-element.282), channel_id=1, source_target_pairs={{0,8},{1,9},{2,10},{3,11},{4,12},{5,13},{6,14},{7,15},{8,0},{9,1},... | collective-permute-start | bytes 24584 | tf_op jit(solution)/shard_map/ppermute | solution.py:55
  287.4 13.7 %collective-permute-start.54 = (bf16[1,64,1536]{2,1,0:T(8,128)(2,1)S(1)}, bf16[1,64,1536]{2,1,0:T(8,128)(2,1)S(1)}, u32[]{:S(2)}, u32[]{:S(2)}) collective-permute-start(bf16[1,64,1536]{2,1,0:T(8,128)(2,1)S(1)} %fusion.6), channel_id=1, source_target_pairs={{0,16},{1,17},{2,18},{3,19},{4,20},{5,21},{6,22},{7,23},{8,24},{9,... | collective-permute-start | bytes 589832 | tf_op jit(solution)/shard_map/ppermute | solution.py:55
  292.5 4.6 %collective-permute-start.52 = (f32[32,1024]{1,0:T(8,128)S(1)}, f32[32,1024]{1,0:T(8,128)S(1)}, u32[]{:S(2)}, u32[]{:S(2)}) collective-permute-start(f32[32,1024]{1,0:T(8,128)S(1)} %slice.259), channel_id=1, source_target_pairs={{0,1},{1,0},{2,3},{3,2},{4,5},{5,4},{6,7},{7,6},{8,9},{9,8},{10,11... | collective-permute-start | bytes 393224 | tf_op jit(solution)/shard_map/ppermute | solution.py:47
  292.5 7.5 %collective-permute-start.49 = (f32[1,8,128]{2,1,0:T(8,128)S(1)}, f32[1,8,128]{2,1,0:T(8,128)S(1)}, u32[]{:S(2)}, u32[]{:S(2)}) collective-permute-start(f32[1,8,128]{2,1,0:T(8,128)S(1)} %slice_add_fusion.14), channel_id=1, source_target_pairs={{0,16},{1,17},{2,18},{3,19},{4,20},{5,21},{6,22},{7,23},{8,24},{9,... | collective-permute-start | bytes 12296 | tf_op jit(solution)/shard_map/ppermute | solution.py:55
  (56 other events, 331.5 us)

commit v2 on v1

--- a/solution.py
+++ b/solution.py
@@ -527,7 +527,7 @@
 LANES = 128
 MEASURED_US = {
     "k_pack_heads": 1.6, "k_heads": 7, "k_attend": 6, "k_project": 0.1,
-    "k_unpack_units": 4.5, "k_feed": 10, "k_feed_out": 3, "k_pair_send": 0.2, "k_grad_feed": 15,
+    "k_feed_first": 14, "k_feed": 10, "k_feed_out": 3, "k_pair_send": 0.2, "k_grad_feed": 15,
     "k_middle_back": 30, "k_attend_back": 8, "k_grad_proj": 0.2, "k_grad_heads": 8.7,
     "k_first_back": 6, "k_input_back": 4.3, "k_small": 2, "k_output": 4, "k_columns": 2, "k_rows": 1.8,
 }
@@ -723,7 +723,7 @@
     outs = []
     for e in range(2):
         part = slice(e * HEAD_DIM, (e + 1) * HEAD_DIM)
-        raw = dot_nt(q[:, part], k[:, part]) * (HEAD_DIM**-0.5)
+        raw = dot_nt(q[:, part] * (HEAD_DIM**-0.5), k[:, part])
         raw = jnp.where(live, raw, -1e30)
         expo = jnp.exp(raw - jnp.max(raw, axis=-1, keepdims=True))
         probs = expo * (1.0 / jnp.sum(expo, axis=-1, keepdims=True))
@@ -743,7 +743,7 @@
     for e in range(2):
         part = slice(e * HEAD_DIM, (e + 1) * HEAD_DIM)
         qe, ke, ve, ge = q[:, part], k[:, part], v[:, part], g[:, part]
-        raw = jnp.where(live, dot_nt(ke, qe) * scale, -1e30)
+        raw = jnp.where(live, dot_nt(ke, qe * scale), -1e30)
         expo = jnp.exp(raw - jnp.max(raw, axis=0, keepdims=True))
         probs = expo * (1.0 / jnp.sum(expo, axis=0, keepdims=True))
         d_probs = dot_nt(ve, ge)
@@ -803,6 +803,11 @@
         sums[:, part] = jnp.broadcast_to(total, (8, tile))
     ds_other[...] = dot_nt(d_pre[tokens:, :], w1[...]).astype(b16)
     ds_own[...] = dot_nt(d_pre[:tokens, :], w1[...])
+
+
+def k_feed_first(orders, place, sent, got, s0, s1, u0, u1, vectors, w1, w2, *outs):
+    k_unpack_units(orders, place, sent, got, w1, w2)
+    k_feed(place, s0, s1, u0, u1, w1, w2, vectors, *outs)
 
 
 def k_feed_out(place, act, w2, own, other):
@@ -1095,15 +1100,20 @@
     )
     heads.step()
     proj.step()
-    feed = Gather(jnp.concatenate([fc1_mine[0], fc1_got[0], fc1_pair, fc2_weight], axis=0), most)
-    heads.held, proj.held, feed.held = tie(heads.held, proj.held, feed.held)
+    fc2 = Gather(fc2_weight, most)
+    heads.held, proj.held, fc2.held = tie(heads.held, proj.held, fc2.held)
     while len(heads.steps) > 1:
         heads.step()
     proj.step()
-    heads.held, proj.held, feed.held = tie(heads.held, proj.held, feed.held)
+    fc2.step()
+    fc1 = Gather(jnp.concatenate([fc1_mine[0], fc1_got[0], fc1_pair], axis=0), most)
+    heads.held, proj.held, fc1.held, fc2.held = tie(heads.held, proj.held, fc1.held, fc2.held)
     heads.step()
-    feed.step()
-    heads.got, feed.held, proj.held = tie(heads.got, feed.held, proj.held)
+    fc1.step()
+    heads.got, fc1.held, proj.held = tie(heads.got, fc1.held, proj.held)
+    feed = Gather(None, most)
+    feed.steps = fc1.steps
+    feed.held = jnp.concatenate([fc1.held, fc2.held], axis=1)
     feed.step()
     proj.step()
 
@@ -1157,11 +1167,6 @@
     )
     second_other = core_swap(second)
     second_pair = bit_swap(second, pair)
-    w_fc1, w_fc2 = on(
-        bind(k_unpack_units, most),
-        (shape((width, hidden), b16), shape((hidden, width), b16)),
-        (feed.sent, feed.got),
-    )
     up_pair = run.now(up_pair)
     up_other_pair = core_swap(up_pair)
     tile = 256
@@ -1172,9 +1177,12 @@
         wide_rows(width), wide_rows(width),
     )
     feeds = []
-    feeds.append(
-        on(k_feed, feed_shapes, (second, second_other, up, up_other, w_fc1, w_fc2, vectors))
-    )
+    w_fc1, w_fc2, *own_feed = on(
+        bind(k_feed_first, most),
+        (shape((width, hidden), b16), shape((hidden, width), b16)) + feed_shapes,
+        (feed.sent, feed.got, second, second_other, up, up_other, vectors),
+    )
+    feeds.append(own_feed)
     second_pair = run.now(second_pair)
     second_other_pair = core_swap(second_pair)
     feeds.append(

time: 311 us -> 307 us (0.987)
  Pallas kernels: 129 us -> 125 us
    pallas_call x23 -> x22, Pallas kernels: 128 us -> 123 us  [call(): pl.pallas_call(kernel, out_shape=outs, in_specs=specs, out_specs=tuple(ou...]
    ppermute x32 -> x33, waiting for transfers between devices: 95.8 us -> 94.6 us  [bit_swap(): return lax.ppermute(value, ('img', 'seq'), pairs)]
    ppermute x32 -> x33, starting transfers between devices: 39.8 us -> 40.8 us  [bit_swap(): return lax.ppermute(value, ('img', 'seq'), pairs)]
  transfers between devices with their start and end apart: 56 -> 57, of which waited for: 27 -> 25; matrix products, arithmetic and copies ran while one was open for 5% -> 5% of each run, Pallas kernels for 35% -> 34%
where the time goes in v2:
time: 307 us; the launch traced here: 301 us
  Pallas kernels  125 us (41%)
  waiting for transfers between devices  105 us (34%)
  starting transfers between devices  44.8 us (15%)
  local copies, waits for them, and re-layouts  15.2 us (5%)
  other arithmetic  10.1 us (3%)
    pallas_call x22, Pallas kernels, call(): pl.pallas_call(kernel, out_shape=outs, in_specs=specs, out_specs=tuple(ou...  123 us
    ppermute x33, waiting for transfers between devices, bit_swap(): return lax.ppermute(value, ('img', 'seq'), pairs)  94.6 us
    ppermute x33, starting transfers between devices, bit_swap(): return lax.ppermute(value, ('img', 'seq'), pairs)  40.8 us
    ppermute x24, waiting for transfers between devices, core_swap(): return lax.ppermute(value, 'seq', [(0, 1), (1, 0)])  10 us
    unnamed x98, local copies, waits for them, and re-layouts  8.96 us
  transfers between devices with their start and end apart: 57, of which 25 were waited for; matrix products, arithmetic and copies ran while one was open for 5% of the time, Pallas kernels for 34%

profile of v2, /device:TPU:0, one launch (start us, length us, event | category | flops | bytes accessed | tf_op | source)
XLA Modules:
  0.0 301.4 jit_solution(1503194272905898655)
XLA Ops:
  4.8 1.8 shard_map.254
  9.0 3.8 %collective-permute-start.1 = (bf16[1,64,1664]{2,1,0:T(8,128)(2,1)S(1)}, bf16[1,64,1664]{2,1,0:T(8,128)(2,1)S(1)}, u32[]{:S(2)}, u32[]{:S(2)}) collective-permute-start(bf16[1,64,1664]{2,1,0:T(8,128)(2,1)S(1)} %maximum_bitcast_fusion.1), channel_id=1, source_target_pairs={{0,16},{1,17},{2,18},{3,19},{4,20},{5,21},{6,22},{7,23},{8,24},{9,... | collective-permute-start | bytes 638984 | tf_op jit(solution)/shard_map/ppermute | solution.py:55
  14.5 8.6 %collective-permute-done.1 = bf16[1,64,1664]{2,1,0:T(8,128)(2,1)S(1)} collective-permute-done((bf16[1,64,1664]{2,1,0:T(8,128)(2,1)S(1)}, bf16[1,64,1664]{2,1,0:T(8,128)(2,1)S(1)}, u32[]{:S(2)}, u32[]{:S(2)}) %collective-permute-start.1) | collective-permute-done | bytes 213024 | tf_op jit(solution)/shard_map/ppermute | solution.py:55
  25.6 2.8 collective-permute-done.7
  28.4 6.5 %collective-permute-done.6 = bf16[2,64,1664]{2,1,0:T(8,128)(2,1)S(1)} collective-permute-done((bf16[2,64,1664]{2,1,0:T(8,128)(2,1)S(1)}, bf16[2,64,1664]{2,1,0:T(8,128)(2,1)S(1)}, u32[]{:S(2)}, u32[]{:S(2)}) %collective-permute-start.6) | collective-permute-done | bytes 426016 | tf_op jit(solution)/shard_map/ppermute | solution.py:55
  36.3 2.8 collective-permute-start.10
  40.7 4.9 %collective-permute-done.9 = bf16[2,32,1024]{2,1,0:T(8,128)(2,1)S(1)} collective-permute-done((bf16[2,32,1024]{2,1,0:T(8,128)(2,1)S(1)}, bf16[2,32,1024]{2,1,0:T(8,128)(2,1)S(1)}, u32[]{:S(2)}, u32[]{:S(2)}) %collective-permute-start.9) | collective-permute-done | bytes 131104 | tf_op jit(solution)/shard_map/ppermute | solution.py:55
  45.6 4.9 %collective-permute-done.10 = bf16[1,128,1024]{2,1,0:T(8,128)(2,1)S(1)} collective-permute-done((bf16[1,128,1024]{2,1,0:T(8,128)(2,1)S(1)}, bf16[1,128,1024]{2,1,0:T(8,128)(2,1)S(1)}, u32[]{:S(2)}, u32[]{:S(2)}) %collective-permute-start.10) | collective-permute-done | bytes 262176 | tf_op jit(solution)/shard_map/ppermute | solution.py:55
  52.9 13.2 %collective-permute-done.12 = bf16[1,128,1024]{2,1,0:T(8,128)(2,1)S(1)} collective-permute-done((bf16[1,128,1024]{2,1,0:T(8,128)(2,1)S(1)}, bf16[1,128,1024]{2,1,0:T(8,128)(2,1)S(1)}, u32[]{:S(2)}, u32[]{:S(2)}) %collective-permute-start.12) | collective-permute-done | bytes 262176 | tf_op jit(solution)/shard_map/ppermute | solution.py:55
  66.2 6.4 %collective-permute-done.11.got = bf16[8,64,1664]{2,1,0:T(8,128)(2,1)S(1)} collective-permute-done((bf16[8,64,1664]{2,1,0:T(8,128)(2,1)S(1)}, bf16[8,64,1664]{2,1,0:T(8,128)(2,1)S(1)}, u32[]{:S(2)}, u32[]{:S(2)}) %collective-permute-start.11) | collective-permute-done | bytes 1703968 | tf_op jit(solution)/shard_map/ppermute | solution.py:55
  76.4 7.0 %shard_map.256 = (bf16[1024,1536]{1,0:T(8,128)(2,1)}, f32[8,1024]{1,0:T(8,128)}, bf16[640,1024]{1,0:T(8,128)(2,1)}, bf16[640,1536]{1,0:T(8,128)(2,1)}) custom-call(s32[5]{0:T(128)} %pad_add_fusion.1.place.refs_0_, bf16[8,64,1664]{2,1,0:T(8,128)(2,1)} %copy-done.2, bf16[8,64,1664]{2,1,0:T(8,128)(2,1)} %copy-done.31, bf16[2,160,1024]{2,1,0:T(8,128)(2,1)} %refs_1_.1, ...), custom_call_target="tpu_custom_call" | custom-call | flops 20999999488 | bytes 1000 | tf_op jit(solution)/shard_map/pallas_call | solution.py:568
  83.4 6.1 %shard_map.257 = (bf16[160,512]{1,0:T(8,128)(2,1)}, bf16[160,512]{1,0:T(8,128)(2,1)}) custom-call(s32[5]{0:T(128)} %pad_add_fusion.1.place.refs_0_, bf16[640,1536]{1,0:T(8,128)(2,1)} %get-tuple-element.155.refs_1_.refs_2_.refs_3_, bf16[640,1536]{1,0:T(8,128)(2,1)} %get-tuple-element.155.refs_1_.refs_2_.refs_3_, ...), custom_call_target="tpu_custom_call" | custom-call | flops 17999998976 | bytes 1000 | tf_op jit(solution)/shard_map/pallas_call | solution.py:568
  89.6 3.2 %collective-permute-start.15 = (bf16[8,32,1024]{2,1,0:T(8,128)(2,1)S(1)}, bf16[8,32,1024]{2,1,0:T(8,128)(2,1)S(1)}, u32[]{:S(2)}, u32[]{:S(2)}) collective-permute-start(bf16[8,32,1024]{2,1,0:T(8,128)(2,1)S(1)} %constant_dynamic-update-slice_fusion.2.refs_1_), channel_id=1, source_target_pairs={{0,8},{1,9},{2,10},{3,11},{4,12},{5,13},{6,14},{7,15},{8,0},{9,1},... | collective-permute-start | bytes 1572872 | tf_op jit(solution)/shard_map/ppermute | solution.py:55
  93.5 6.4 %shard_map.258 = (bf16[160,512]{1,0:T(8,128)(2,1)}, bf16[160,512]{1,0:T(8,128)(2,1)}) custom-call(s32[5]{0:T(128)} %pad_add_fusion.1.place.refs_0_, bf16[640,1536]{1,0:T(8,128)(2,1)} %get-tuple-element.155.refs_1_.refs_2_.refs_3_, bf16[640,1536]{1,0:T(8,128)(2,1)} %get-tuple-element.155.refs_1_.refs_2_.refs_3_, ...), custom_call_target="tpu_custom_call" | custom-call | flops 17999998976 | bytes 1000 | tf_op jit(solution)/shard_map/pallas_call | solution.py:568
  100.0 2.4 collective-permute-done.15.refs_2_
  103.0 1.8 collective-permute-done.18.refs_7_.refs_5_
  104.8 1.7 collective-permute-start.22
  108.2 4.2 %shard_map.259 = (bf16[1024,1024]{1,0:T(8,128)(2,1)}, f32[320,1024]{1,0:T(8,128)}, bf16[320,1024]{1,0:T(8,128)(2,1)}) custom-call(s32[5]{0:T(128)} %pad_add_fusion.1.place.refs_0_, bf16[8,32,1024]{2,1,0:T(8,128)(2,1)} %copy-done.4, bf16[8,32,1024]{2,1,0:T(8,128)(2,1)} %copy-done.18, bf16[8,32,1024]{2,1,0:T(8,128)(2,1)} %copy-done.19, ...), custom_call_target="tpu_custom_call" | custom-call | flops 300000000 | bytes 1000 | tf_op jit(solution)/shard_map/pallas_call | solution.py:568
  112.8 9.6 %collective-permute-done.22.refs_3_ = bf16[2,160,1024]{2,1,0:T(8,128)(2,1)S(1)} collective-permute-done((bf16[2,160,1024]{2,1,0:T(8,128)(2,1)S(1)}, bf16[2,160,1024]{2,1,0:T(8,128)(2,1)S(1)}, u32[]{:S(2)}, u32[]{:S(2)}) %collective-permute-start.22) | collective-permute-done | bytes 655392 | tf_op jit(solution)/shard_map/ppermute | solution.py:55
  123.3 9.5 %shard_map.260 = (bf16[1024,1024]{1,0:T(8,128)(2,1)}, bf16[1024,1024]{1,0:T(8,128)(2,1)}, bf16[640,1024]{1,0:T(8,128)(2,1)}, bf16[640,1024]{1,0:T(8,128)(2,1)}, ...) custom-call(s32[5]{0:T(128)} %pad_add_fusion.1.place.refs_0_, ...), custom_call_target="tpu_custom_call" | custom-call | flops 41999998976 | bytes 1000 | tf_op jit(solution)/shard_map/pallas_call | solution.py:568
  132.7 2.8 collective-permute-done.23.refs_1_
  135.6 2.1 collective-permute-done.24.refs_2_
  138.5 9.2 %shard_map.261 = (bf16[640,1024]{1,0:T(8,128)(2,1)}, bf16[640,1024]{1,0:T(8,128)(2,1)}, f32[320,1024]{1,0:T(8,128)}, bf16[320,1024]{1,0:T(8,128)(2,1)}, f32[8,10...) custom-call(s32[5]{0:T(128)} %pad_add_fusion.1.place.refs_0_, bf16[320,1024]{1,0:T(8,128)(2,1)} %copy-done.37, ...), custom_call_target="tpu_custom_call" | custom-call | flops 30000001024 | bytes 1000 | tf_op jit(solution)/shard_map/pallas_call | solution.py:568
  147.8 5.1 %shard_map.262 = (f32[320,1024]{1,0:T(8,128)}, bf16[320,1024]{1,0:T(8,128)(2,1)}) custom-call(s32[5]{0:T(128)} %pad_add_fusion.1.place.refs_0_, bf16[640,1024]{1,0:T(8,128)(2,1)} %get-tuple-element.182.refs_1_.refs_2_, bf16[1024,1024]{1,0:T(8,128)(2,1)} %get-tuple-element.172.refs_6_.refs_2_, f32[8,1024]{1,0:T(8,128)} %get-tuple-element.183.refs_3_.refs_4_), custom_call_target="tpu_custom_call" | custom-call | flops 8999999488 | bytes 1000 | tf_op jit(solution)/shard_map/pallas_call | solution.py:568
  153.4 1.8 collective-permute-done.27.refs_4_
  156.7 3.3 %shard_map.263 = (bf16[320,1024]{1,0:T(8,128)(2,1)}, bf16[320,1024]{1,0:T(8,128)(2,1)}) custom-call(s32[5]{0:T(128)} %pad_add_fusion.1.place.refs_0_, f32[320,1024]{1,0:T(8,128)} %get-tuple-element.180.refs_1_, bf16[320,1024]{1,0:T(8,128)(2,1)} %copy-done.17, f32[320,1024]{1,0:T(8,128)} %get-tuple-element.184.refs_3_.refs_5_, bf16[320,1024]{1,0:T(8,128)(2,1)} %copy-done.16, ...), custom_call_target="tpu_custom_call" | custom-call | flops 600000000 | bytes 1000 | tf_op jit(solution)/shard_map/pallas_call | solution.py:568
  160.0 1.7 collective-permute-start.29
  161.8 12.9 %shard_map.264 = (bf16[1024,1024]{1,0:T(8,128)(2,1)}, bf16[1024,1024]{1,0:T(8,128)(2,1)}) custom-call(s32[5]{0:T(128)} %pad_add_fusion.1.place.refs_0_, bf16[640,1024]{1,0:T(8,128)(2,1)} %get-tuple-element.171.refs_1_, bf16[640,1024]{1,0:T(8,128)(2,1)} %get-tuple-element.182.refs_1_.refs_2_, bf16[640,1024]{1,0:T(8,128)(2,1)} %get-tuple-element.190.refs_3_, ...), custom_call_target="tpu_custom_call" | custom-call | flops 44999999488 | bytes 1000 | tf_op jit(solution)/shard_map/pallas_call | solution.py:568
  177.9 5.9 %shard_map.265 = (f32[320,1024]{1,0:T(8,128)}, bf16[320,1024]{1,0:T(8,128)(2,1)}, bf16[320,512]{1,0:T(8,128)(2,1)}, bf16[320,512]{1,0:T(8,128)(2,1)}, f32[8,1024]{1,0:T(8,128)}) custom-call(s32[5]{0:T(128)} %pad_add_fusion.1.place.refs_0_, f32[320,1024]{1,0:T(8,128)} %get-tuple-element.173.refs_1_, bf16[320,1024]{1,0:T(8,128)(2,1)} %copy-done.41, ...), custom_call_target="tpu_custom_call" | custom-call | flops 89999998976 | bytes 1000 | tf_op jit(solution)/shard_map/pallas_call | solution.py:568
  185.0 2.0 collective-permute-done.30.refs_5_
  188.8 8.5 %shard_map.266 = (bf16[640,1536]{1,0:T(8,128)(2,1)}, f32[16,1536]{1,0:T(8,128)}) custom-call(s32[5]{0:T(128)} %pad_add_fusion.1.place.refs_0_, bf16[640,1536]{1,0:T(8,128)(2,1)} %get-tuple-element.155.refs_1_.refs_2_.refs_3_, bf16[640,1536]{1,0:T(8,128)(2,1)} %get-tuple-element.155.refs_1_.refs_2_.refs_3_, ...), custom_call_target="tpu_custom_call" | custom-call | flops 600000000 | bytes 1000 | tf_op jit(solution)/shard_map/pallas_call | solution.py:568
  198.2 4.6 %shard_map.267 = (bf16[256,1024]{1,0:T(8,128)(2,1)}, bf16[256,1024]{1,0:T(8,128)(2,1)}) custom-call(s32[5]{0:T(128)} %pad_add_fusion.1.place.refs_0_, bf16[160,512]{1,0:T(8,128)(2,1)} %get-tuple-element.159.refs_4_.refs_5_.refs_1_, bf16[160,512]{1,0:T(8,128)(2,1)} %get-tuple-element.164.refs_6_.refs_11_.refs_2_, ...), custom_call_target="tpu_custom_call" | custom-call | flops 600000000 | bytes 1000 | tf_op jit(solution)/shard_map/pallas_call | solution.py:568
  204.4 1.8 fusion.15
  208.6 8.4 %shard_map.268 = (bf16[640,1536]{1,0:T(8,128)(2,1)}, f32[16,1536]{1,0:T(8,128)}) custom-call(s32[5]{0:T(128)} %pad_add_fusion.1.place.refs_0_, bf16[640,1536]{1,0:T(8,128)(2,1)} %get-tuple-element.155.refs_1_.refs_2_.refs_3_, bf16[640,1536]{1,0:T(8,128)(2,1)} %get-tuple-element.155.refs_1_.refs_2_.refs_3_, ...), custom_call_target="tpu_custom_call", output_to_operand_aliasing={{0}: (6, {}), {1}: (7, {})} | custom-call | flops 24000000000 | bytes 1000 | tf_op jit(solution)/shard_map/pallas_call | solution.py:568
  217.0 6.3 %shard_map.269 = (bf16[512,1536]{1,0:T(8,128)(2,1)}, bf16[512,1536]{1,0:T(8,128)(2,1)}) custom-call(s32[5]{0:T(128)} %pad_add_fusion.1.place.refs_0_, bf16[640,1024]{1,0:T(8,128)(2,1)} %get-tuple-element.211.refs_1_, bf16[640,1536]{1,0:T(8,128)(2,1)} %get-tuple-element.207.refs_2_.refs_1_, f32[16,1536]{1,0:T(8,128)} %get-tuple-element.212.refs_3_.refs_5_), custom_call_target="tpu_custom_call" | custom-call | flops 26100000768 | bytes 1000 | tf_op jit(solution)/shard_map/pallas_call | solution.py:568
  225.4 6.3 %shard_map.270 = (f32[2,160,1024]{2,1,0:T(8,128)}, bf16[2,160,1024]{2,1,0:T(8,128)(2,1)}) custom-call(s32[5]{0:T(128)} %pad_add_fusion.1.place.refs_0_, bf16[640,1536]{1,0:T(8,128)(2,1)} %get-tuple-element.207.refs_2_.refs_1_, bf16[1024,1536]{1,0:T(8,128)(2,1)} %get-tuple-element.208.refs_2_, bf16[512,1536]{1,0:T(8,128)(2,1)} %get-tuple-element.215.refs_3_), custom_call_target="tpu_custom_call" | custom-call | flops 17999998976 | bytes 1000 | tf_op jit(solution)/shard_map/pallas_call | solution.py:568
  231.7 4.6 %shard_map.271 = (f32[320,1024]{1,0:T(8,128)}, bf16[320,1024]{1,0:T(8,128)(2,1)}) custom-call(s32[5]{0:T(128)} %pad_add_fusion.1.place.refs_0_, bf16[640,1024]{1,0:T(8,128)(2,1)} %get-tuple-element.171.refs_1_, bf16[1024,1024]{1,0:T(8,128)(2,1)} %get-tuple-element.172.refs_6_.refs_2_, f32[2,160,1024]{2,1,0:T(8,128)} %get-tuple-element.216.refs_3_.refs_2_), custom_call_target="tpu_custom_call" | custom-call | flops 8999999488 | bytes 1000 | tf_op jit(solution)/shard_map/pallas_call | solution.py:568
  239.9 6.9 %collective-permute-done.41 = bf16[8,64,1536]{2,1,0:T(8,128)(2,1)S(1)} collective-permute-done((bf16[8,64,1536]{2,1,0:T(8,128)(2,1)}, bf16[8,64,1536]{2,1,0:T(8,128)(2,1)S(1)}, u32[]{:S(2)}, u32[]{:S(2)}) %collective-permute-start.41) | collective-permute-done | bytes 1572896 | tf_op jit(solution)/shard_map/ppermute | solution.py:55
  248.7 4.2 %shard_map.272 = (f32[2,160,1024]{2,1,0:T(8,128)}, f32[8,1024]{1,0:T(8,128)}) custom-call(s32[5]{0:T(128)} %pad_add_fusion.1.place.refs_0_, bf16[2,160,1024]{2,1,0:T(8,128)(2,1)} %refs_1_.1, f32[2,160,1024]{2,1,0:T(8,128)} %get-tuple-element.216.refs_3_.refs_2_, bf16[2,160,1024]{2,1,0:T(8,128)(2,1)} %copy-done.39, f32[320,1024]{1,0:T(8,128)} %get-tuple-element.222.refs_4_, ...), custom_call_target="tpu_custom_call" | custom-call | flops 12899999744 | bytes 1000 | tf_op jit(solution)/shard_map/pallas_call | solution.py:568
  252.9 2.0 shard_map.273
  254.9 7.8 %collective-permute-done.43 = bf16[1,256,1024]{2,1,0:T(8,128)(2,1)} collective-permute-done((bf16[1,256,1024]{2,1,0:T(8,128)(2,1)}, bf16[1,256,1024]{2,1,0:T(8,128)(2,1)}, u32[]{:S(2)}, u32[]{:S(2)}) %collective-permute-start.43) | collective-permute-done | bytes 524320 | tf_op jit(solution)/shard_map/ppermute | solution.py:55
  265.9 3.1 %collective-permute-done.44 = f32[8,8,128]{2,1,0:T(8,128)S(1)} collective-permute-done((f32[8,8,128]{2,1,0:T(8,128)S(1)}, f32[8,8,128]{2,1,0:T(8,128)S(1)}, u32[]{:S(2)}, u32[]{:S(2)}) %collective-permute-start.44) | collective-permute-done | bytes 32800 | tf_op jit(solution)/shard_map/ppermute | solution.py:55
  269.1 8.6 %collective-permute-done.48 = bf16[2,64,1536]{2,1,0:T(8,128)(2,1)S(1)} collective-permute-done((bf16[2,64,1536]{2,1,0:T(8,128)(2,1)S(1)}, bf16[2,64,1536]{2,1,0:T(8,128)(2,1)S(1)}, u32[]{:S(2)}, u32[]{:S(2)}) %collective-permute-start.48) | collective-permute-done | bytes 393248 | tf_op jit(solution)/shard_map/ppermute | solution.py:55
  279.4 2.6 collective-permute-done.46
  285.2 3.3 %shard_map.274.refs_5_ = bf16[2,160,1024]{2,1,0:T(8,128)(2,1)} custom-call(s32[5]{0:T(128)} %pad_add_fusion.1.place.refs_0_, f32[320,1024]{1,0:T(8,128)} %get-tuple-element.170.refs_8_.refs_4_.refs_1_, f32[320,1024]{1,0:T(8,128)} %get-tuple-element.227.refs_6_.refs_2_, bf16[320,1024]{1,0:T(8,128)(2,1)} %collective-permute-done.37.refs_3_, ...), custom_call_target="tpu_custom_call" | custom-call | flops 12000000000 | bytes 1000 | tf_op jit(solution)/shard_map/pallas_call | solution.py:568
  290.0 2.4 collective-permute-done.54
  293.7 2.1 shard_map.275.refs_3_
  299.4 1.8 shard_map.276
  (237 shorter events, 60.1 us)
Async XLA Ops:
  3.0 9.9 %collective-permute-start.2 = (bf16[2,32,1024]{2,1,0:T(8,128)(2,1)}, bf16[2,32,1024]{2,1,0:T(8,128)(2,1)S(1)}, u32[]{:S(2)}, u32[]{:S(2)}) collective-permute-start(bf16[2,32,1024]{2,1,0:T(8,128)(2,1)} %get-tuple-element.140), channel_id=1, source_target_pairs={{0,1},{1,0},{2,3},{3,2},{4,5},{5,4},{6,7},{7,6},{8,9},{9,8},{10,11... | collective-permute-start | bytes 393224 | tf_op jit(solution)/shard_map/ppermute | solution.py:47
  6.8 16.4 %collective-permute-start.5 = (bf16[2,160,1024]{2,1,0:T(8,128)(2,1)S(1)}, bf16[2,160,1024]{2,1,0:T(8,128)(2,1)S(1)}, u32[]{:S(2)}, u32[]{:S(2)}) collective-permute-start(bf16[2,160,1024]{2,1,0:T(8,128)(2,1)S(1)} %broadcast_select_fusion.refs_5_), channel_id=1, source_target_pairs={{0,1},{1,0},{2,3},{3,2},{4,5},{5,4},{6,7},{7,6},{8,9},{9,8},{10,11... | collective-permute-start | bytes 1966088 | tf_op jit(solution)/shard_map/ppermute | solution.py:47
  7.4 15.9 %collective-permute-start.4 = (bf16[2,160,1024]{2,1,0:T(8,128)(2,1)S(1)}, bf16[2,160,1024]{2,1,0:T(8,128)(2,1)S(1)}, u32[]{:S(2)}, u32[]{:S(2)}) collective-permute-start(bf16[2,160,1024]{2,1,0:T(8,128)(2,1)S(1)} %copy-done.15), channel_id=1, source_target_pairs={{0,1},{1,0},{2,3},{3,2},{4,5},{5,4},{6,7},{7,6},{8,9},{9,8},{10,11... | collective-permute-start | bytes 1966088 | tf_op jit(solution)/shard_map/ppermute | solution.py:47
  9.0 14.1 %collective-permute-start.1 = (bf16[1,64,1664]{2,1,0:T(8,128)(2,1)S(1)}, bf16[1,64,1664]{2,1,0:T(8,128)(2,1)S(1)}, u32[]{:S(2)}, u32[]{:S(2)}) collective-permute-start(bf16[1,64,1664]{2,1,0:T(8,128)(2,1)S(1)} %maximum_bitcast_fusion.1), channel_id=1, source_target_pairs={{0,16},{1,17},{2,18},{3,19},{4,20},{5,21},{6,22},{7,23},{8,24},{9,... | collective-permute-start | bytes 638984 | tf_op jit(solution)/shard_map/ppermute | solution.py:55
  12.9 10.3 %collective-permute-start.3 = (bf16[64,1024]{1,0:T(8,128)(2,1)S(1)}, bf16[64,1024]{1,0:T(8,128)(2,1)S(1)}, u32[]{:S(2)}, u32[]{:S(2)}) collective-permute-start(bf16[64,1024]{1,0:T(8,128)(2,1)S(1)} %pad_maximum_fusion.7), channel_id=1, source_target_pairs={{0,8},{1,9},{2,10},{3,11},{4,12},{5,13},{6,14},{7,15},{8,0},{9,1},... | collective-permute-start | bytes 393224 | tf_op jit(solution)/shard_map/ppermute | solution.py:55
  23.3 11.6 %collective-permute-start.6 = (bf16[2,64,1664]{2,1,0:T(8,128)(2,1)S(1)}, bf16[2,64,1664]{2,1,0:T(8,128)(2,1)S(1)}, u32[]{:S(2)}, u32[]{:S(2)}) collective-permute-start(bf16[2,64,1664]{2,1,0:T(8,128)(2,1)S(1)} %pad_maximum_fusion.5), channel_id=1, source_target_pairs={{0,8},{1,9},{2,10},{3,11},{4,12},{5,13},{6,14},{7,15},{8,0},{9,1},... | collective-permute-start | bytes 1277960 | tf_op jit(solution)/shard_map/ppermute | solution.py:55
  24.1 4.3 %collective-permute-start.7 = (bf16[1,32,1024]{2,1,0:T(8,128)(2,1)S(1)}, bf16[1,32,1024]{2,1,0:T(8,128)(2,1)S(1)}, u32[]{:S(2)}, u32[]{:S(2)}) collective-permute-start(bf16[1,32,1024]{2,1,0:T(8,128)(2,1)S(1)} %bitcast.79), channel_id=1, source_target_pairs={{0,2},{1,5},{2,0},{3,7},{4,6},{5,1},{6,4},{7,3},{8,10},{9,13},{10,... | collective-permute-start | bytes 196616 | tf_op jit(solution)/shard_map/ppermute | solution.py:55
  34.9 15.6 %collective-permute-start.8 = (bf16[4,64,1664]{2,1,0:T(8,128)(2,1)S(1)}, bf16[4,64,1664]{2,1,0:T(8,128)(2,1)S(1)}, u32[]{:S(2)}, u32[]{:S(2)}) collective-permute-start(bf16[4,64,1664]{2,1,0:T(8,128)(2,1)S(1)} %pad_maximum_fusion.2), channel_id=1, source_target_pairs={{0,2},{1,5},{2,0},{3,7},{4,6},{5,1},{6,4},{7,3},{8,10},{9,13},{10,... | collective-permute-start | bytes 2555912 | tf_op jit(solution)/shard_map/ppermute | solution.py:55
  36.3 14.2 %collective-permute-start.10 = (bf16[1,128,1024]{2,1,0:T(8,128)(2,1)S(1)}, bf16[1,128,1024]{2,1,0:T(8,128)(2,1)S(1)}, u32[]{:S(2)}, u32[]{:S(2)}) collective-permute-start(bf16[1,128,1024]{2,1,0:T(8,128)(2,1)S(1)} %bitcast.77), channel_id=1, source_target_pairs={{0,16},{1,17},{2,18},{3,19},{4,20},{5,21},{6,22},{7,23},{8,24},{9,... | collective-permute-start | bytes 786440 | tf_op jit(solution)/shard_map/ppermute | solution.py:55
  39.1 6.4 %collective-permute-start.9 = (bf16[2,32,1024]{2,1,0:T(8,128)(2,1)S(1)}, bf16[2,32,1024]{2,1,0:T(8,128)(2,1)S(1)}, u32[]{:S(2)}, u32[]{:S(2)}) collective-permute-start(bf16[2,32,1024]{2,1,0:T(8,128)(2,1)S(1)} %pad_maximum_fusion.8), channel_id=1, source_target_pairs={{0,4},{1,3},{2,6},{3,1},{4,0},{5,7},{6,2},{7,5},{8,12},{9,11},{10,... | collective-permute-start | bytes 393224 | tf_op jit(solution)/shard_map/ppermute | solution.py:55
  50.7 21.9 %collective-permute-start.11 = (bf16[8,64,1664]{2,1,0:T(8,128)(2,1)S(1)}, bf16[8,64,1664]{2,1,0:T(8,128)(2,1)S(1)}, u32[]{:S(2)}, u32[]{:S(2)}) collective-permute-start(bf16[8,64,1664]{2,1,0:T(8,128)(2,1)S(1)} %pad_maximum_fusion.1.sent), channel_id=1, source_target_pairs={{0,4},{1,3},{2,6},{3,1},{4,0},{5,7},{6,2},{7,5},{8,12},{9,11},{10,... | collective-permute-start | bytes 5111816 | tf_op jit(solution)/shard_map/ppermute | solution.py:55
  51.3 14.8 %collective-permute-start.12 = (bf16[1,128,1024]{2,1,0:T(8,128)(2,1)S(1)}, bf16[1,128,1024]{2,1,0:T(8,128)(2,1)S(1)}, u32[]{:S(2)}, u32[]{:S(2)}) collective-permute-start(bf16[1,128,1024]{2,1,0:T(8,128)(2,1)S(1)} %maximum_bitcast_fusion), channel_id=1, source_target_pairs={{0,16},{1,17},{2,18},{3,19},{4,20},{5,21},{6,22},{7,23},{8,24},{9,... | collective-permute-start | bytes 786440 | tf_op jit(solution)/shard_map/ppermute | solution.py:55
  73.9 15.6 %collective-permute-start.14 = (bf16[2,256,1024]{2,1,0:T(8,128)(2,1)S(1)}, bf16[2,256,1024]{2,1,0:T(8,128)(2,1)S(1)}, u32[]{:S(2)}, u32[]{:S(2)}) collective-permute-start(bf16[2,256,1024]{2,1,0:T(8,128)(2,1)S(1)} %constant_dynamic-update-slice_fusion), channel_id=1, source_target_pairs={{0,2},{1,5},{2,0},{3,7},{4,6},{5,1},{6,4},{7,3},{8,10},{9,13},{10,... | collective-permute-start | bytes 3145736 | tf_op jit(solution)/shard_map/ppermute | solution.py:55
  75.4 14.1 %collective-permute-start.13 = (bf16[4,32,1024]{2,1,0:T(8,128)(2,1)S(1)}, bf16[4,32,1024]{2,1,0:T(8,128)(2,1)S(1)}, u32[]{:S(2)}, u32[]{:S(2)}) collective-permute-start(bf16[4,32,1024]{2,1,0:T(8,128)(2,1)S(1)} %pad_maximum_fusion.6), channel_id=1, source_target_pairs={{0,16},{1,17},{2,18},{3,19},{4,20},{5,21},{6,22},{7,23},{8,24},{9,... | collective-permute-start | bytes 786440 | tf_op jit(solution)/shard_map/ppermute | solution.py:55
  89.6 12.8 %collective-permute-start.15 = (bf16[8,32,1024]{2,1,0:T(8,128)(2,1)S(1)}, bf16[8,32,1024]{2,1,0:T(8,128)(2,1)S(1)}, u32[]{:S(2)}, u32[]{:S(2)}) collective-permute-start(bf16[8,32,1024]{2,1,0:T(8,128)(2,1)S(1)} %constant_dynamic-update-slice_fusion.2.refs_1_), channel_id=1, source_target_pairs={{0,8},{1,9},{2,10},{3,11},{4,12},{5,13},{6,14},{7,15},{8,0},{9,1},... | collective-permute-start | bytes 1572872 | tf_op jit(solution)/shard_map/ppermute | solution.py:55
  92.7 13.8 %collective-permute-start.16 = (bf16[8,32,1024]{2,1,0:T(8,128)(2,1)S(1)}, bf16[8,32,1024]{2,1,0:T(8,128)(2,1)S(1)}, u32[]{:S(2)}, u32[]{:S(2)}) collective-permute-start(bf16[8,32,1024]{2,1,0:T(8,128)(2,1)S(1)} %constant_dynamic-update-slice_fusion.2.refs_1_), channel_id=1, source_target_pairs={{0,1},{1,0},{2,3},{3,2},{4,5},{5,4},{6,7},{7,6},{8,9},{9,8},{10,11... | collective-permute-start | bytes 1572872 | tf_op jit(solution)/shard_map/ppermute | solution.py:47
  92.9 29.4 %collective-permute-start.20 = (bf16[4,256,1024]{2,1,0:T(8,128)(2,1)S(1)}, bf16[4,256,1024]{2,1,0:T(8,128)(2,1)}, u32[]{:S(2)}, u32[]{:S(2)}) collective-permute-start(bf16[4,256,1024]{2,1,0:T(8,128)(2,1)S(1)} %pad_maximum_fusion.refs_1_), channel_id=1, source_target_pairs={{0,4},{1,3},{2,6},{3,1},{4,0},{5,7},{6,2},{7,5},{8,12},{9,11},{10,... | collective-permute-start | bytes 6291464 | tf_op jit(solution)/shard_map/ppermute | solution.py:55
  102.4 4.1 %collective-permute-start.17 = (bf16[8,32,1024]{2,1,0:T(8,128)(2,1)S(1)}, bf16[8,32,1024]{2,1,0:T(8,128)(2,1)S(1)}, u32[]{:S(2)}, u32[]{:S(2)}) collective-permute-start(bf16[8,32,1024]{2,1,0:T(8,128)(2,1)S(1)} %collective-permute-done.15.refs_2_), channel_id=1, source_target_pairs={{0,1},{1,0},{2,3},{3,2},{4,5},{5,4},{6,7},{7,6},{8,9},{9,8},{10,11... | collective-permute-start | bytes 1572872 | tf_op jit(solution)/shard_map/ppermute | solution.py:47
  104.8 17.6 %collective-permute-start.22 = (bf16[2,160,1024]{2,1,0:T(8,128)(2,1)S(1)}, bf16[2,160,1024]{2,1,0:T(8,128)(2,1)S(1)}, u32[]{:S(2)}, u32[]{:S(2)}) collective-permute-start(bf16[2,160,1024]{2,1,0:T(8,128)(2,1)S(1)} %broadcast_select_fusion.refs_5_), channel_id=1, source_target_pairs={{0,8},{1,9},{2,10},{3,11},{4,12},{5,13},{6,14},{7,15},{8,0},{9,1},... | collective-permute-start | bytes 1966088 | tf_op jit(solution)/shard_map/ppermute | solution.py:55
  112.4 9.9 %collective-permute-start.21 = (bf16[320,1024]{1,0:T(8,128)(2,1)}, bf16[320,1024]{1,0:T(8,128)(2,1)S(1)}, u32[]{:S(2)}, u32[]{:S(2)}) collective-permute-start(bf16[320,1024]{1,0:T(8,128)(2,1)} %get-tuple-element.167.refs_3_), channel_id=1, source_target_pairs={{0,1},{1,0},{2,3},{3,2},{4,5},{5,4},{6,7},{7,6},{8,9},{9,8},{10,11... | collective-permute-start | bytes 1966088 | tf_op jit(solution)/shard_map/ppermute | solution.py:47
  112.4 23.2 %collective-permute-start.23 = (bf16[320,1024]{1,0:T(8,128)(2,1)}, bf16[320,1024]{1,0:T(8,128)(2,1)S(1)}, u32[]{:S(2)}, u32[]{:S(2)}) collective-permute-start(bf16[320,1024]{1,0:T(8,128)(2,1)} %get-tuple-element.167.refs_3_), channel_id=1, source_target_pairs={{0,8},{1,9},{2,10},{3,11},{4,12},{5,13},{6,14},{7,15},{8,0},{9,1},... | collective-permute-start | bytes 1966088 | tf_op jit(solution)/shard_map/ppermute | solution.py:55
  122.3 13.2 %collective-permute-start.25 = (bf16[2,160,1024]{2,1,0:T(8,128)(2,1)S(1)}, bf16[2,160,1024]{2,1,0:T(8,128)(2,1)S(1)}, u32[]{:S(2)}, u32[]{:S(2)}) collective-permute-start(bf16[2,160,1024]{2,1,0:T(8,128)(2,1)S(1)} %collective-permute-done.22.refs_3_), channel_id=1, source_target_pairs={{0,1},{1,0},{2,3},{3,2},{4,5},{5,4},{6,7},{7,6},{8,9},{9,8},{10,11... | collective-permute-start | bytes 1966088 | tf_op jit(solution)/shard_map/ppermute | solution.py:47
  160.0 17.0 %collective-permute-start.29 = (bf16[320,1024]{1,0:T(8,128)(2,1)}, bf16[320,1024]{1,0:T(8,128)(2,1)S(1)}, u32[]{:S(2)}, u32[]{:S(2)}) collective-permute-start(bf16[320,1024]{1,0:T(8,128)(2,1)} %get-tuple-element.196.refs_9_), channel_id=1, source_target_pairs={{0,8},{1,9},{2,10},{3,11},{4,12},{5,13},{6,14},{7,15},{8,0},{9,1},... | collective-permute-start | bytes 1966088 | tf_op jit(solution)/shard_map/ppermute | solution.py:55
  161.8 14.4 %collective-permute-start.28 = (bf16[320,1024]{1,0:T(8,128)(2,1)S(1)}, bf16[320,1024]{1,0:T(8,128)(2,1)S(1)}, u32[]{:S(2)}, u32[]{:S(2)}) collective-permute-start(bf16[320,1024]{1,0:T(8,128)(2,1)S(1)} %copy-done.34), channel_id=1, source_target_pairs={{0,1},{1,0},{2,3},{3,2},{4,5},{5,4},{6,7},{7,6},{8,9},{9,8},{10,11... | collective-permute-start | bytes 1966088 | tf_op jit(solution)/shard_map/ppermute | solution.py:47
  174.7 31.5 %collective-permute-start.31 = (bf16[4,256,1024]{2,1,0:T(8,128)(2,1)}, bf16[4,256,1024]{2,1,0:T(8,128)(2,1)S(1)}, u32[]{:S(2)}, u32[]{:S(2)}) collective-permute-start(bf16[4,256,1024]{2,1,0:T(8,128)(2,1)} %bitcast.91), channel_id=1, source_target_pairs={{0,4},{1,3},{2,6},{3,1},{4,0},{5,7},{6,2},{7,5},{8,12},{9,11},{10,... | collective-permute-start | bytes 6291464 | tf_op jit(solution)/shard_map/ppermute | solution.py:55
  183.8 13.5 %collective-permute-start.34 = (bf16[320,1024]{1,0:T(8,128)(2,1)}, bf16[320,1024]{1,0:T(8,128)(2,1)S(1)}, u32[]{:S(2)}, u32[]{:S(2)}) collective-permute-start(bf16[320,1024]{1,0:T(8,128)(2,1)} %get-tuple-element.204.refs_9_), channel_id=1, source_target_pairs={{0,1},{1,0},{2,3},{3,2},{4,5},{5,4},{6,7},{7,6},{8,9},{9,8},{10,11... | collective-permute-start | bytes 1966088 | tf_op jit(solution)/shard_map/ppermute | solution.py:47
  184.3 13.0 %collective-permute-start.32 = (bf16[160,512]{1,0:T(8,128)(2,1)S(1)}, bf16[160,512]{1,0:T(8,128)(2,1)S(1)}, u32[]{:S(2)}, u32[]{:S(2)}) collective-permute-start(bf16[160,512]{1,0:T(8,128)(2,1)S(1)} %copy-done.9), channel_id=1, source_target_pairs={{0,1},{1,0},{2,3},{3,2},{4,5},{5,4},{6,7},{7,6},{8,9},{9,8},{10,11... | collective-permute-start | bytes 491528 | tf_op jit(solution)/shard_map/ppermute | solution.py:47
  184.4 12.9 %collective-permute-start.33 = (bf16[160,512]{1,0:T(8,128)(2,1)S(1)}, bf16[160,512]{1,0:T(8,128)(2,1)S(1)}, u32[]{:S(2)}, u32[]{:S(2)}) collective-permute-start(bf16[160,512]{1,0:T(8,128)(2,1)S(1)} %copy-done.3), channel_id=1, source_target_pairs={{0,1},{1,0},{2,3},{3,2},{4,5},{5,4},{6,7},{7,6},{8,9},{9,8},{10,11... | collective-permute-start | bytes 491528 | tf_op jit(solution)/shard_map/ppermute | solution.py:47
  187.0 95.0 %collective-permute-start.38 = (bf16[320,1024]{1,0:T(8,128)(2,1)}, bf16[320,1024]{1,0:T(8,128)(2,1)}, u32[]{:S(2)}, u32[]{:S(2)}) collective-permute-start(bf16[320,1024]{1,0:T(8,128)(2,1)} %get-tuple-element.220), channel_id=1, source_target_pairs={{0,8},{1,9},{2,10},{3,11},{4,12},{5,13},{6,14},{7,15},{8,0},{9,1},... | collective-permute-start | bytes 1966088 | tf_op jit(solution)/shard_map/ppermute | solution.py:55
  202.9 22.5 %collective-permute-start.35 = (bf16[8,32,1024]{2,1,0:T(8,128)(2,1)}, bf16[8,32,1024]{2,1,0:T(8,128)(2,1)}, u32[]{:S(2)}, u32[]{:S(2)}) collective-permute-start(bf16[8,32,1024]{2,1,0:T(8,128)(2,1)} %bitcast.93), channel_id=1, source_target_pairs={{0,4},{1,3},{2,6},{3,1},{4,0},{5,7},{6,2},{7,5},{8,12},{9,11},{10,... | collective-permute-start | bytes 1572872 | tf_op jit(solution)/shard_map/ppermute | solution.py:55
  207.1 18.2 %collective-permute-start.36 = (bf16[2,256,1024]{2,1,0:T(8,128)(2,1)S(1)}, bf16[2,256,1024]{2,1,0:T(8,128)(2,1)S(1)}, u32[]{:S(2)}, u32[]{:S(2)}) collective-permute-start(bf16[2,256,1024]{2,1,0:T(8,128)(2,1)S(1)} %get-tuple-element.263), channel_id=1, source_target_pairs={{0,2},{1,5},{2,0},{3,7},{4,6},{5,1},{6,4},{7,3},{8,10},{9,13},{10,... | collective-permute-start | bytes 3145736 | tf_op jit(solution)/shard_map/ppermute | solution.py:55
  223.3 23.4 %collective-permute-start.41 = (bf16[8,64,1536]{2,1,0:T(8,128)(2,1)}, bf16[8,64,1536]{2,1,0:T(8,128)(2,1)S(1)}, u32[]{:S(2)}, u32[]{:S(2)}) collective-permute-start(bf16[8,64,1536]{2,1,0:T(8,128)(2,1)} %bitcast.92), channel_id=1, source_target_pairs={{0,4},{1,3},{2,6},{3,1},{4,0},{5,7},{6,2},{7,5},{8,12},{9,11},{10,... | collective-permute-start | bytes 4718600 | tf_op jit(solution)/shard_map/ppermute | solution.py:55
  237.2 25.4 %collective-permute-start.43 = (bf16[1,256,1024]{2,1,0:T(8,128)(2,1)}, bf16[1,256,1024]{2,1,0:T(8,128)(2,1)}, u32[]{:S(2)}, u32[]{:S(2)}) collective-permute-start(bf16[1,256,1024]{2,1,0:T(8,128)(2,1)} %fusion.3), channel_id=1, source_target_pairs={{0,16},{1,17},{2,18},{3,19},{4,20},{5,21},{6,22},{7,23},{8,24},{9,... | collective-permute-start | bytes 1572872 | tf_op jit(solution)/shard_map/ppermute | solution.py:55
  239.3 7.9 %collective-permute-start.40 = (bf16[4,32,1024]{2,1,0:T(8,128)(2,1)S(1)}, bf16[4,32,1024]{2,1,0:T(8,128)(2,1)S(1)}, u32[]{:S(2)}, u32[]{:S(2)}) collective-permute-start(bf16[4,32,1024]{2,1,0:T(8,128)(2,1)S(1)} %get-tuple-element.275), channel_id=1, source_target_pairs={{0,2},{1,5},{2,0},{3,7},{4,6},{5,1},{6,4},{7,3},{8,10},{9,13},{10,... | collective-permute-start | bytes 786440 | tf_op jit(solution)/shard_map/ppermute | solution.py:55
  239.9 8.0 %collective-permute-start.39 = (bf16[2,160,1024]{2,1,0:T(8,128)(2,1)S(1)}, bf16[2,160,1024]{2,1,0:T(8,128)(2,1)S(1)}, u32[]{:S(2)}, u32[]{:S(2)}) collective-permute-start(bf16[2,160,1024]{2,1,0:T(8,128)(2,1)S(1)} %copy-done.36), channel_id=1, source_target_pairs={{0,1},{1,0},{2,3},{3,2},{4,5},{5,4},{6,7},{7,6},{8,9},{9,8},{10,11... | collective-permute-start | bytes 1966088 | tf_op jit(solution)/shard_map/ppermute | solution.py:47
  246.8 36.8 %collective-permute-start.37 = (bf16[320,1024]{1,0:T(8,128)(2,1)}, bf16[320,1024]{1,0:T(8,128)(2,1)}, u32[]{:S(2)}, u32[]{:S(2)}) collective-permute-start(bf16[320,1024]{1,0:T(8,128)(2,1)} %get-tuple-element.219), channel_id=1, source_target_pairs={{0,1},{1,0},{2,3},{3,2},{4,5},{5,4},{6,7},{7,6},{8,9},{9,8},{10,11... | collective-permute-start | bytes 1966088 | tf_op jit(solution)/shard_map/ppermute | solution.py:47
  247.2 18.5 %collective-permute-start.45 = (bf16[4,64,1536]{2,1,0:T(8,128)(2,1)S(1)}, bf16[4,64,1536]{2,1,0:T(8,128)(2,1)S(1)}, u32[]{:S(2)}, u32[]{:S(2)}) collective-permute-start(bf16[4,64,1536]{2,1,0:T(8,128)(2,1)S(1)} %get-tuple-element.267), channel_id=1, source_target_pairs={{0,2},{1,5},{2,0},{3,7},{4,6},{5,1},{6,4},{7,3},{8,10},{9,13},{10,... | collective-permute-start | bytes 2359304 | tf_op jit(solution)/shard_map/ppermute | solution.py:55
  247.9 30.4 %collective-permute-start.47 = (bf16[2,32,1024]{2,1,0:T(8,128)(2,1)S(1)}, bf16[2,32,1024]{2,1,0:T(8,128)(2,1)S(1)}, u32[]{:S(2)}, u32[]{:S(2)}) collective-permute-start(bf16[2,32,1024]{2,1,0:T(8,128)(2,1)S(1)} %get-tuple-element.273), channel_id=1, source_target_pairs={{0,8},{1,9},{2,10},{3,11},{4,12},{5,13},{6,14},{7,15},{8,0},{9,1},... | collective-permute-start | bytes 393224 | tf_op jit(solution)/shard_map/ppermute | solution.py:55
  265.1 4.0 %collective-permute-start.44 = (f32[8,8,128]{2,1,0:T(8,128)S(1)}, f32[8,8,128]{2,1,0:T(8,128)S(1)}, u32[]{:S(2)}, u32[]{:S(2)}) collective-permute-start(f32[8,8,128]{2,1,0:T(8,128)S(1)} %slice.288), channel_id=1, source_target_pairs={{0,4},{1,3},{2,6},{3,1},{4,0},{5,7},{6,2},{7,5},{8,12},{9,11},{10,... | collective-permute-start | bytes 98312 | tf_op jit(solution)/shard_map/ppermute | solution.py:55
  265.8 11.8 %collective-permute-start.48 = (bf16[2,64,1536]{2,1,0:T(8,128)(2,1)S(1)}, bf16[2,64,1536]{2,1,0:T(8,128)(2,1)S(1)}, u32[]{:S(2)}, u32[]{:S(2)}) collective-permute-start(bf16[2,64,1536]{2,1,0:T(8,128)(2,1)S(1)} %get-tuple-element.261), channel_id=1, source_target_pairs={{0,8},{1,9},{2,10},{3,11},{4,12},{5,13},{6,14},{7,15},{8,0},{9,1},... | collective-permute-start | bytes 1179656 | tf_op jit(solution)/shard_map/ppermute | solution.py:55
  269.1 19.4 %collective-permute-start.51 = (f32[64,1024]{1,0:T(8,128)S(1)}, f32[64,1024]{1,0:T(8,128)S(1)}, u32[]{:S(2)}, u32[]{:S(2)}) collective-permute-start(f32[64,1024]{1,0:T(8,128)S(1)} %slice_bitcast_fusion.2), channel_id=1, source_target_pairs={{0,8},{1,9},{2,10},{3,11},{4,12},{5,13},{6,14},{7,15},{8,0},{9,1},... | collective-permute-start | bytes 786440 | tf_op jit(solution)/shard_map/ppermute | solution.py:55
  277.6 15.4 %collective-permute-start.52 = (f32[32,1024]{1,0:T(8,128)S(1)}, f32[32,1024]{1,0:T(8,128)S(1)}, u32[]{:S(2)}, u32[]{:S(2)}) collective-permute-start(f32[32,1024]{1,0:T(8,128)S(1)} %slice_bitcast_fusion.4), channel_id=1, source_target_pairs={{0,1},{1,0},{2,3},{3,2},{4,5},{5,4},{6,7},{7,6},{8,9},{9,8},{10,11... | collective-permute-start | bytes 393224 | tf_op jit(solution)/shard_map/ppermute | solution.py:47
  278.2 3.7 %collective-permute-start.46 = (f32[4,8,128]{2,1,0:T(8,128)S(1)}, f32[4,8,128]{2,1,0:T(8,128)S(1)}, u32[]{:S(2)}, u32[]{:S(2)}) collective-permute-start(f32[4,8,128]{2,1,0:T(8,128)S(1)} %get-tuple-element.283), channel_id=1, source_target_pairs={{0,2},{1,5},{2,0},{3,7},{4,6},{5,1},{6,4},{7,3},{8,10},{9,13},{10,... | collective-permute-start | bytes 49160 | tf_op jit(solution)/shard_map/ppermute | solution.py:55
  282.0 10.4 %collective-permute-start.54 = (bf16[1,32,1024]{2,1,0:T(8,128)(2,1)S(1)}, bf16[1,32,1024]{2,1,0:T(8,128)(2,1)S(1)}, u32[]{:S(2)}, u32[]{:S(2)}) collective-permute-start(bf16[1,32,1024]{2,1,0:T(8,128)(2,1)S(1)} %fusion.11), channel_id=1, source_target_pairs={{0,16},{1,17},{2,18},{3,19},{4,20},{5,21},{6,22},{7,23},{8,24},{9,... | collective-permute-start | bytes 196616 | tf_op jit(solution)/shard_map/ppermute | solution.py:55
  282.0 6.5 %collective-permute-start.49 = (f32[2,8,128]{2,1,0:T(8,128)S(1)}, f32[2,8,128]{2,1,0:T(8,128)S(1)}, u32[]{:S(2)}, u32[]{:S(2)}) collective-permute-start(f32[2,8,128]{2,1,0:T(8,128)S(1)} %get-tuple-element.284), channel_id=1, source_target_pairs={{0,8},{1,9},{2,10},{3,11},{4,12},{5,13},{6,14},{7,15},{8,0},{9,1},... | collective-permute-start | bytes 24584 | tf_op jit(solution)/shard_map/ppermute | solution.py:55
  283.6 13.5 %collective-permute-start.55 = (bf16[1,64,1536]{2,1,0:T(8,128)(2,1)S(1)}, bf16[1,64,1536]{2,1,0:T(8,128)(2,1)S(1)}, u32[]{:S(2)}, u32[]{:S(2)}) collective-permute-start(bf16[1,64,1536]{2,1,0:T(8,128)(2,1)S(1)} %fusion.6), channel_id=1, source_target_pairs={{0,16},{1,17},{2,18},{3,19},{4,20},{5,21},{6,22},{7,23},{8,24},{9,... | collective-permute-start | bytes 589832 | tf_op jit(solution)/shard_map/ppermute | solution.py:55
  288.5 4.5 %collective-permute-start.53 = (f32[32,1024]{1,0:T(8,128)S(1)}, f32[32,1024]{1,0:T(8,128)S(1)}, u32[]{:S(2)}, u32[]{:S(2)}) collective-permute-start(f32[32,1024]{1,0:T(8,128)S(1)} %slice.259), channel_id=1, source_target_pairs={{0,1},{1,0},{2,3},{3,2},{4,5},{5,4},{6,7},{7,6},{8,9},{9,8},{10,11... | collective-permute-start | bytes 393224 | tf_op jit(solution)/shard_map/ppermute | solution.py:47
  288.6 7.4 %collective-permute-start.50 = (f32[1,8,128]{2,1,0:T(8,128)S(1)}, f32[1,8,128]{2,1,0:T(8,128)S(1)}, u32[]{:S(2)}, u32[]{:S(2)}) collective-permute-start(f32[1,8,128]{2,1,0:T(8,128)S(1)} %slice_add_fusion.14), channel_id=1, source_target_pairs={{0,16},{1,17},{2,18},{3,19},{4,20},{5,21},{6,22},{7,23},{8,24},{9,... | collective-permute-start | bytes 12296 | tf_op jit(solution)/shard_map/ppermute | solution.py:55
  (57 other events, 351.2 us)

commit v3 on v2

--- a/solution.py
+++ b/solution.py
@@ -1107,10 +1107,14 @@
     proj.step()
     fc2.step()
     fc1 = Gather(jnp.concatenate([fc1_mine[0], fc1_got[0], fc1_pair], axis=0), most)
-    heads.held, proj.held, fc1.held, fc2.held = tie(heads.held, proj.held, fc1.held, fc2.held)
+    heads.held, proj.held, fc1.held, fc2.held, up = tie(
+        heads.held, proj.held, fc1.held, fc2.held, up
+    )
     heads.step()
     fc1.step()
-    heads.got, fc1.held, proj.held = tie(heads.got, fc1.held, proj.held)
+    up_pair = bit_swap(up, pair)
+    heads.got, fc1.held, proj.held, up_pair = tie(heads.got, fc1.held, proj.held, up_pair)
+    up_other_pair = core_swap(up_pair)
     feed = Gather(None, most)
     feed.steps = fc1.steps
     feed.held = jnp.concatenate([fc1.held, fc2.held], axis=1)
@@ -1157,8 +1161,7 @@
             feed.step()
             proj.step()
             proj_sent_far = core_swap(proj.sent)
-    proj.got, up = run.now(proj.got, up)
-    up_pair = bit_swap(up, pair)
+    proj.got = run.now(proj.got)
     proj_far = proj_sent_far, core_swap(proj.got)
     w_proj, middle, second = on(
         bind(k_project, last),
@@ -1167,8 +1170,6 @@
     )
     second_other = core_swap(second)
     second_pair = bit_swap(second, pair)
-    up_pair = run.now(up_pair)
-    up_other_pair = core_swap(up_pair)
     tile = 256
     fixed = lambda dims: block(dims, lambda *_: (0,) * len(dims))
     wide_rows = lambda cols: shape((2 * tok, cols), b16)

time: 307 us -> 302 us (0.984)
  waiting for transfers between devices: 105 us -> 93 us
  starting transfers between devices: 44.8 us -> 50.6 us
    ppermute x33, waiting for transfers between devices: 94.6 us -> 82.8 us  [bit_swap(): return lax.ppermute(value, ('img', 'seq'), pairs)]
    ppermute x33, starting transfers between devices: 40.8 us -> 46.7 us  [bit_swap(): return lax.ppermute(value, ('img', 'seq'), pairs)]
    unnamed x98 -> x102, local copies, waits for them, and re-layouts: 8.96 us -> 9.5 us
  transfers between devices with their start and end apart: 57 -> 57, of which waited for: 25 -> 27; matrix products, arithmetic and copies ran while one was open for 5% -> 5% of each run, Pallas kernels for 34% -> 35%
where the time goes in v3:
time: 302 us; the launch traced here: 296 us
  Pallas kernels  125 us (41%)
  waiting for transfers between devices  93 us (31%)
  starting transfers between devices  50.6 us (17%)
  local copies, waits for them, and re-layouts  15.7 us (5%)
  other arithmetic  9.99 us (3%)
    pallas_call x22, Pallas kernels, call(): pl.pallas_call(kernel, out_shape=outs, in_specs=specs, out_specs=tuple(ou...  124 us
    ppermute x33, waiting for transfers between devices, bit_swap(): return lax.ppermute(value, ('img', 'seq'), pairs)  82.8 us
    ppermute x33, starting transfers between devices, bit_swap(): return lax.ppermute(value, ('img', 'seq'), pairs)  46.7 us
    ppermute x24, waiting for transfers between devices, core_swap(): return lax.ppermute(value, 'seq', [(0, 1), (1, 0)])  10.2 us
    unnamed x102, local copies, waits for them, and re-layouts  9.5 us
  transfers between devices with their start and end apart: 57, of which 27 were waited for; matrix products, arithmetic and copies ran while one was open for 5% of the time, Pallas kernels for 35%

profile of v3, /device:TPU:0, one launch (start us, length us, event | category | flops | bytes accessed | tf_op | source)
XLA Modules:
  0.0 296.2 jit_solution(8917388466553162915)
XLA Ops:
  9.0 3.8 %collective-permute-start.1 = (bf16[1,64,1664]{2,1,0:T(8,128)(2,1)S(1)}, bf16[1,64,1664]{2,1,0:T(8,128)(2,1)S(1)}, u32[]{:S(2)}, u32[]{:S(2)}) collective-permute-start(bf16[1,64,1664]{2,1,0:T(8,128)(2,1)S(1)} %maximum_bitcast_fusion.1), channel_id=1, source_target_pairs={{0,16},{1,17},{2,18},{3,19},{4,20},{5,21},{6,22},{7,23},{8,24},{9,... | collective-permute-start | bytes 638984 | tf_op jit(solution)/shard_map/ppermute | solution.py:55
  14.5 8.6 %collective-permute-done.1 = bf16[1,64,1664]{2,1,0:T(8,128)(2,1)S(1)} collective-permute-done((bf16[1,64,1664]{2,1,0:T(8,128)(2,1)S(1)}, bf16[1,64,1664]{2,1,0:T(8,128)(2,1)S(1)}, u32[]{:S(2)}, u32[]{:S(2)}) %collective-permute-start.1) | collective-permute-done | bytes 213024 | tf_op jit(solution)/shard_map/ppermute | solution.py:55
  25.6 2.8 collective-permute-done.7
  28.4 6.5 %collective-permute-done.6 = bf16[2,64,1664]{2,1,0:T(8,128)(2,1)S(1)} collective-permute-done((bf16[2,64,1664]{2,1,0:T(8,128)(2,1)S(1)}, bf16[2,64,1664]{2,1,0:T(8,128)(2,1)S(1)}, u32[]{:S(2)}, u32[]{:S(2)}) %collective-permute-start.6) | collective-permute-done | bytes 426016 | tf_op jit(solution)/shard_map/ppermute | solution.py:55
  36.3 2.8 collective-permute-start.10
  40.7 4.9 %collective-permute-done.9 = bf16[2,32,1024]{2,1,0:T(8,128)(2,1)S(1)} collective-permute-done((bf16[2,32,1024]{2,1,0:T(8,128)(2,1)S(1)}, bf16[2,32,1024]{2,1,0:T(8,128)(2,1)S(1)}, u32[]{:S(2)}, u32[]{:S(2)}) %collective-permute-start.9) | collective-permute-done | bytes 131104 | tf_op jit(solution)/shard_map/ppermute | solution.py:55
  45.6 4.9 %collective-permute-done.10 = bf16[1,128,1024]{2,1,0:T(8,128)(2,1)S(1)} collective-permute-done((bf16[1,128,1024]{2,1,0:T(8,128)(2,1)S(1)}, bf16[1,128,1024]{2,1,0:T(8,128)(2,1)S(1)}, u32[]{:S(2)}, u32[]{:S(2)}) %collective-permute-start.10) | collective-permute-done | bytes 262176 | tf_op jit(solution)/shard_map/ppermute | solution.py:55
  52.0 3.4 %collective-permute-start.12 = (bf16[1,128,1024]{2,1,0:T(8,128)(2,1)S(1)}, bf16[1,128,1024]{2,1,0:T(8,128)(2,1)S(1)}, u32[]{:S(2)}, u32[]{:S(2)}) collective-permute-start(bf16[1,128,1024]{2,1,0:T(8,128)(2,1)S(1)} %maximum_bitcast_fusion), channel_id=1, source_target_pairs={{0,16},{1,17},{2,18},{3,19},{4,20},{5,21},{6,22},{7,23},{8,24},{9,... | collective-permute-start | bytes 786440 | tf_op jit(solution)/shard_map/ppermute | solution.py:55
  55.9 16.5 %collective-permute-done.12 = bf16[1,128,1024]{2,1,0:T(8,128)(2,1)S(1)} collective-permute-done((bf16[1,128,1024]{2,1,0:T(8,128)(2,1)S(1)}, bf16[1,128,1024]{2,1,0:T(8,128)(2,1)S(1)}, u32[]{:S(2)}, u32[]{:S(2)}) %collective-permute-start.12) | collective-permute-done | bytes 262176 | tf_op jit(solution)/shard_map/ppermute | solution.py:55
  75.5 2.3 collective-permute-start.14
  77.8 7.0 %shard_map.256 = (bf16[1024,1536]{1,0:T(8,128)(2,1)}, f32[8,1024]{1,0:T(8,128)}, bf16[640,1024]{1,0:T(8,128)(2,1)}, bf16[640,1536]{1,0:T(8,128)(2,1)}) custom-call(s32[5]{0:T(128)} %pad_add_fusion.1.place.refs_0_, bf16[8,64,1664]{2,1,0:T(8,128)(2,1)} %copy-done.2, bf16[8,64,1664]{2,1,0:T(8,128)(2,1)} %copy-done.32, bf16[2,160,1024]{2,1,0:T(8,128)(2,1)} %refs_1_.1, ...), custom_call_target="tpu_custom_call" | custom-call | flops 20999999488 | bytes 1000 | tf_op jit(solution)/shard_map/pallas_call | solution.py:568
  84.8 6.1 %shard_map.257 = (bf16[160,512]{1,0:T(8,128)(2,1)}, bf16[160,512]{1,0:T(8,128)(2,1)}) custom-call(s32[5]{0:T(128)} %pad_add_fusion.1.place.refs_0_, bf16[640,1536]{1,0:T(8,128)(2,1)} %get-tuple-element.155.refs_1_.refs_2_.refs_3_, bf16[640,1536]{1,0:T(8,128)(2,1)} %get-tuple-element.155.refs_1_.refs_2_.refs_3_, ...), custom_call_target="tpu_custom_call" | custom-call | flops 17999998976 | bytes 1000 | tf_op jit(solution)/shard_map/pallas_call | solution.py:568
  91.0 2.5 collective-permute-start.16
  94.2 6.4 %shard_map.258 = (bf16[160,512]{1,0:T(8,128)(2,1)}, bf16[160,512]{1,0:T(8,128)(2,1)}) custom-call(s32[5]{0:T(128)} %pad_add_fusion.1.place.refs_0_, bf16[640,1536]{1,0:T(8,128)(2,1)} %get-tuple-element.155.refs_1_.refs_2_.refs_3_, bf16[640,1536]{1,0:T(8,128)(2,1)} %get-tuple-element.155.refs_1_.refs_2_.refs_3_, ...), custom_call_target="tpu_custom_call" | custom-call | flops 17999998976 | bytes 1000 | tf_op jit(solution)/shard_map/pallas_call | solution.py:568
  100.7 3.9 %collective-permute-done.16.refs_2_ = bf16[8,32,1024]{2,1,0:T(8,128)(2,1)S(1)} collective-permute-done((bf16[8,32,1024]{2,1,0:T(8,128)(2,1)S(1)}, bf16[8,32,1024]{2,1,0:T(8,128)(2,1)S(1)}, u32[]{:S(2)}, u32[]{:S(2)}) %collective-permute-start.16) | collective-permute-done | bytes 524320 | tf_op jit(solution)/shard_map/ppermute | solution.py:55
  105.2 1.8 collective-permute-done.19.refs_7_.refs_5_
  108.9 4.2 %shard_map.259 = (bf16[1024,1024]{1,0:T(8,128)(2,1)}, f32[320,1024]{1,0:T(8,128)}, bf16[320,1024]{1,0:T(8,128)(2,1)}) custom-call(s32[5]{0:T(128)} %pad_add_fusion.1.place.refs_0_, bf16[8,32,1024]{2,1,0:T(8,128)(2,1)} %copy-done.4, bf16[8,32,1024]{2,1,0:T(8,128)(2,1)} %copy-done.18, bf16[8,32,1024]{2,1,0:T(8,128)(2,1)} %copy-done.19, ...), custom_call_target="tpu_custom_call" | custom-call | flops 300000000 | bytes 1000 | tf_op jit(solution)/shard_map/pallas_call | solution.py:568
  115.4 4.3 %collective-permute-done.21.refs_2_ = bf16[4,256,1024]{2,1,0:T(8,128)(2,1)S(1)} collective-permute-done((bf16[4,256,1024]{2,1,0:T(8,128)(2,1)S(1)}, bf16[4,256,1024]{2,1,0:T(8,128)(2,1)S(1)}, u32[]{:S(2)}, u32[]{:S(2)}) %collective-permute-start.21) | collective-permute-done | bytes 2097184 | tf_op jit(solution)/shard_map/ppermute | solution.py:55
  121.1 9.5 %shard_map.260 = (bf16[1024,1024]{1,0:T(8,128)(2,1)}, bf16[1024,1024]{1,0:T(8,128)(2,1)}, bf16[640,1024]{1,0:T(8,128)(2,1)}, bf16[640,1024]{1,0:T(8,128)(2,1)}, ...) custom-call(s32[5]{0:T(128)} %pad_add_fusion.1.place.refs_0_, ...), custom_call_target="tpu_custom_call" | custom-call | flops 41999998976 | bytes 1000 | tf_op jit(solution)/shard_map/pallas_call | solution.py:568
  130.7 2.1 collective-permute-done.24.refs_2_
  133.6 9.2 %shard_map.261 = (bf16[640,1024]{1,0:T(8,128)(2,1)}, bf16[640,1024]{1,0:T(8,128)(2,1)}, f32[320,1024]{1,0:T(8,128)}, bf16[320,1024]{1,0:T(8,128)(2,1)}, f32[8,10...) custom-call(s32[5]{0:T(128)} %pad_add_fusion.1.place.refs_0_, bf16[320,1024]{1,0:T(8,128)(2,1)} %copy-done.40, ...), custom_call_target="tpu_custom_call" | custom-call | flops 30000001024 | bytes 1000 | tf_op jit(solution)/shard_map/pallas_call | solution.py:568
  142.8 5.2 %shard_map.262 = (f32[320,1024]{1,0:T(8,128)}, bf16[320,1024]{1,0:T(8,128)(2,1)}) custom-call(s32[5]{0:T(128)} %pad_add_fusion.1.place.refs_0_, bf16[640,1024]{1,0:T(8,128)(2,1)} %get-tuple-element.180.refs_1_.refs_2_, bf16[1024,1024]{1,0:T(8,128)(2,1)} %get-tuple-element.170.refs_6_.refs_2_, f32[8,1024]{1,0:T(8,128)} %get-tuple-element.181.refs_3_.refs_4_), custom_call_target="tpu_custom_call" | custom-call | flops 8999999488 | bytes 1000 | tf_op jit(solution)/shard_map/pallas_call | solution.py:568
  148.5 1.8 collective-permute-done.27.refs_4_
  151.8 3.4 %shard_map.263 = (bf16[320,1024]{1,0:T(8,128)(2,1)}, bf16[320,1024]{1,0:T(8,128)(2,1)}) custom-call(s32[5]{0:T(128)} %pad_add_fusion.1.place.refs_0_, f32[320,1024]{1,0:T(8,128)} %get-tuple-element.178.refs_1_, bf16[320,1024]{1,0:T(8,128)(2,1)} %copy-done.17, f32[320,1024]{1,0:T(8,128)} %get-tuple-element.182.refs_3_.refs_5_, bf16[320,1024]{1,0:T(8,128)(2,1)} %copy-done.16, ...), custom_call_target="tpu_custom_call" | custom-call | flops 600000000 | bytes 1000 | tf_op jit(solution)/shard_map/pallas_call | solution.py:568
  156.9 12.9 %shard_map.264 = (bf16[1024,1024]{1,0:T(8,128)(2,1)}, bf16[1024,1024]{1,0:T(8,128)(2,1)}) custom-call(s32[5]{0:T(128)} %pad_add_fusion.1.place.refs_0_, bf16[640,1024]{1,0:T(8,128)(2,1)} %get-tuple-element.169.refs_1_, bf16[640,1024]{1,0:T(8,128)(2,1)} %get-tuple-element.180.refs_1_.refs_2_, bf16[640,1024]{1,0:T(8,128)(2,1)} %get-tuple-element.188.refs_3_, ...), custom_call_target="tpu_custom_call" | custom-call | flops 44999999488 | bytes 1000 | tf_op jit(solution)/shard_map/pallas_call | solution.py:568
  173.0 5.9 %shard_map.265 = (f32[320,1024]{1,0:T(8,128)}, bf16[320,1024]{1,0:T(8,128)(2,1)}, bf16[320,512]{1,0:T(8,128)(2,1)}, bf16[320,512]{1,0:T(8,128)(2,1)}, f32[8,1024]{1,0:T(8,128)}) custom-call(s32[5]{0:T(128)} %pad_add_fusion.1.place.refs_0_, f32[320,1024]{1,0:T(8,128)} %get-tuple-element.171.refs_1_, bf16[320,1024]{1,0:T(8,128)(2,1)} %copy-done.43, ...), custom_call_target="tpu_custom_call" | custom-call | flops 89999998976 | bytes 1000 | tf_op jit(solution)/shard_map/pallas_call | solution.py:568
  180.2 2.0 collective-permute-done.30.refs_5_
  183.9 8.5 %shard_map.266 = (bf16[640,1536]{1,0:T(8,128)(2,1)}, f32[16,1536]{1,0:T(8,128)}) custom-call(s32[5]{0:T(128)} %pad_add_fusion.1.place.refs_0_, bf16[640,1536]{1,0:T(8,128)(2,1)} %get-tuple-element.155.refs_1_.refs_2_.refs_3_, bf16[640,1536]{1,0:T(8,128)(2,1)} %get-tuple-element.155.refs_1_.refs_2_.refs_3_, ...), custom_call_target="tpu_custom_call" | custom-call | flops 600000000 | bytes 1000 | tf_op jit(solution)/shard_map/pallas_call | solution.py:568
  193.3 4.6 %shard_map.267 = (bf16[256,1024]{1,0:T(8,128)(2,1)}, bf16[256,1024]{1,0:T(8,128)(2,1)}) custom-call(s32[5]{0:T(128)} %pad_add_fusion.1.place.refs_0_, bf16[160,512]{1,0:T(8,128)(2,1)} %get-tuple-element.159.refs_4_.refs_5_.refs_1_, bf16[160,512]{1,0:T(8,128)(2,1)} %get-tuple-element.164.refs_6_.refs_11_.refs_2_, ...), custom_call_target="tpu_custom_call" | custom-call | flops 600000000 | bytes 1000 | tf_op jit(solution)/shard_map/pallas_call | solution.py:568
  199.7 1.8 fusion.15
  202.4 8.4 %shard_map.268 = (bf16[640,1536]{1,0:T(8,128)(2,1)}, f32[16,1536]{1,0:T(8,128)}) custom-call(s32[5]{0:T(128)} %pad_add_fusion.1.place.refs_0_, bf16[640,1536]{1,0:T(8,128)(2,1)} %get-tuple-element.155.refs_1_.refs_2_.refs_3_, bf16[640,1536]{1,0:T(8,128)(2,1)} %get-tuple-element.155.refs_1_.refs_2_.refs_3_, ...), custom_call_target="tpu_custom_call", output_to_operand_aliasing={{0}: (6, {}), {1}: (7, {})} | custom-call | flops 24000000000 | bytes 1000 | tf_op jit(solution)/shard_map/pallas_call | solution.py:568
  210.8 6.3 %shard_map.269 = (bf16[512,1536]{1,0:T(8,128)(2,1)}, bf16[512,1536]{1,0:T(8,128)(2,1)}) custom-call(s32[5]{0:T(128)} %pad_add_fusion.1.place.refs_0_, bf16[640,1024]{1,0:T(8,128)(2,1)} %get-tuple-element.209.refs_1_, bf16[640,1536]{1,0:T(8,128)(2,1)} %get-tuple-element.205.refs_2_.refs_1_, f32[16,1536]{1,0:T(8,128)} %get-tuple-element.210.refs_3_.refs_5_), custom_call_target="tpu_custom_call" | custom-call | flops 26100000768 | bytes 1000 | tf_op jit(solution)/shard_map/pallas_call | solution.py:568
  219.5 6.3 %shard_map.270 = (f32[2,160,1024]{2,1,0:T(8,128)}, bf16[2,160,1024]{2,1,0:T(8,128)(2,1)}) custom-call(s32[5]{0:T(128)} %pad_add_fusion.1.place.refs_0_, bf16[640,1536]{1,0:T(8,128)(2,1)} %get-tuple-element.205.refs_2_.refs_1_, bf16[1024,1536]{1,0:T(8,128)(2,1)} %get-tuple-element.206.refs_2_, bf16[512,1536]{1,0:T(8,128)(2,1)} %get-tuple-element.213.refs_3_), custom_call_target="tpu_custom_call" | custom-call | flops 17999998976 | bytes 1000 | tf_op jit(solution)/shard_map/pallas_call | solution.py:568
  225.8 4.6 %shard_map.271 = (f32[320,1024]{1,0:T(8,128)}, bf16[320,1024]{1,0:T(8,128)(2,1)}) custom-call(s32[5]{0:T(128)} %pad_add_fusion.1.place.refs_0_, bf16[640,1024]{1,0:T(8,128)(2,1)} %get-tuple-element.169.refs_1_, bf16[1024,1024]{1,0:T(8,128)(2,1)} %get-tuple-element.170.refs_6_.refs_2_, f32[2,160,1024]{2,1,0:T(8,128)} %get-tuple-element.214.refs_3_.refs_2_), custom_call_target="tpu_custom_call" | custom-call | flops 8999999488 | bytes 1000 | tf_op jit(solution)/shard_map/pallas_call | solution.py:568
  233.8 1.9 collective-permute-start.40
  235.7 3.1 %collective-permute-done.41 = bf16[8,64,1536]{2,1,0:T(8,128)(2,1)S(1)} collective-permute-done((bf16[8,64,1536]{2,1,0:T(8,128)(2,1)}, bf16[8,64,1536]{2,1,0:T(8,128)(2,1)S(1)}, u32[]{:S(2)}, u32[]{:S(2)}) %collective-permute-start.41) | collective-permute-done | bytes 1572896 | tf_op jit(solution)/shard_map/ppermute | solution.py:55
  240.2 2.7 collective-permute-start.45
  243.9 4.2 %shard_map.272 = (f32[2,160,1024]{2,1,0:T(8,128)}, f32[8,1024]{1,0:T(8,128)}) custom-call(s32[5]{0:T(128)} %pad_add_fusion.1.place.refs_0_, bf16[2,160,1024]{2,1,0:T(8,128)(2,1)} %refs_1_.1, f32[2,160,1024]{2,1,0:T(8,128)} %get-tuple-element.214.refs_3_.refs_2_, bf16[2,160,1024]{2,1,0:T(8,128)(2,1)} %copy-done.41, f32[320,1024]{1,0:T(8,128)} %get-tuple-element.220.refs_4_, ...), custom_call_target="tpu_custom_call" | custom-call | flops 12899999744 | bytes 1000 | tf_op jit(solution)/shard_map/pallas_call | solution.py:568
  248.1 2.0 shard_map.273
  250.1 7.8 %collective-permute-done.43 = bf16[1,256,1024]{2,1,0:T(8,128)(2,1)} collective-permute-done((bf16[1,256,1024]{2,1,0:T(8,128)(2,1)}, bf16[1,256,1024]{2,1,0:T(8,128)(2,1)}, u32[]{:S(2)}, u32[]{:S(2)}) %collective-permute-start.43) | collective-permute-done | bytes 524320 | tf_op jit(solution)/shard_map/ppermute | solution.py:55
  261.2 3.2 %collective-permute-done.44 = f32[8,8,128]{2,1,0:T(8,128)S(1)} collective-permute-done((f32[8,8,128]{2,1,0:T(8,128)S(1)}, f32[8,8,128]{2,1,0:T(8,128)S(1)}, u32[]{:S(2)}, u32[]{:S(2)}) %collective-permute-start.44) | collective-permute-done | bytes 32800 | tf_op jit(solution)/shard_map/ppermute | solution.py:55
  264.3 8.8 %collective-permute-done.48 = bf16[2,64,1536]{2,1,0:T(8,128)(2,1)S(1)} collective-permute-done((bf16[2,64,1536]{2,1,0:T(8,128)(2,1)S(1)}, bf16[2,64,1536]{2,1,0:T(8,128)(2,1)S(1)}, u32[]{:S(2)}, u32[]{:S(2)}) %collective-permute-start.48) | collective-permute-done | bytes 393248 | tf_op jit(solution)/shard_map/ppermute | solution.py:55
  274.0 2.8 collective-permute-done.46
  277.2 2.1 collective-permute-start.49
  280.0 3.3 %shard_map.274.refs_5_ = bf16[2,160,1024]{2,1,0:T(8,128)(2,1)} custom-call(s32[5]{0:T(128)} %pad_add_fusion.1.place.refs_0_, f32[320,1024]{1,0:T(8,128)} %get-tuple-element.165.refs_8_.refs_4_.refs_1_, f32[320,1024]{1,0:T(8,128)} %get-tuple-element.225.refs_6_.refs_2_, bf16[320,1024]{1,0:T(8,128)(2,1)} %collective-permute-done.37.refs_3_, ...), custom_call_target="tpu_custom_call" | custom-call | flops 12000000000 | bytes 1000 | tf_op jit(solution)/shard_map/pallas_call | solution.py:568
  283.4 2.4 collective-permute-start.50
  288.2 2.1 shard_map.275.refs_3_
  294.1 1.8 shard_map.276
  (241 shorter events, 61.4 us)
Async XLA Ops:
  3.0 9.9 %collective-permute-start.2 = (bf16[2,32,1024]{2,1,0:T(8,128)(2,1)}, bf16[2,32,1024]{2,1,0:T(8,128)(2,1)S(1)}, u32[]{:S(2)}, u32[]{:S(2)}) collective-permute-start(bf16[2,32,1024]{2,1,0:T(8,128)(2,1)} %get-tuple-element.139), channel_id=1, source_target_pairs={{0,1},{1,0},{2,3},{3,2},{4,5},{5,4},{6,7},{7,6},{8,9},{9,8},{10,11... | collective-permute-start | bytes 393224 | tf_op jit(solution)/shard_map/ppermute | solution.py:47
  6.8 16.4 %collective-permute-start.5 = (bf16[2,160,1024]{2,1,0:T(8,128)(2,1)S(1)}, bf16[2,160,1024]{2,1,0:T(8,128)(2,1)S(1)}, u32[]{:S(2)}, u32[]{:S(2)}) collective-permute-start(bf16[2,160,1024]{2,1,0:T(8,128)(2,1)S(1)} %broadcast_select_fusion.refs_5_), channel_id=1, source_target_pairs={{0,1},{1,0},{2,3},{3,2},{4,5},{5,4},{6,7},{7,6},{8,9},{9,8},{10,11... | collective-permute-start | bytes 1966088 | tf_op jit(solution)/shard_map/ppermute | solution.py:47
  7.4 15.9 %collective-permute-start.4 = (bf16[2,160,1024]{2,1,0:T(8,128)(2,1)S(1)}, bf16[2,160,1024]{2,1,0:T(8,128)(2,1)S(1)}, u32[]{:S(2)}, u32[]{:S(2)}) collective-permute-start(bf16[2,160,1024]{2,1,0:T(8,128)(2,1)S(1)} %copy-done.15), channel_id=1, source_target_pairs={{0,1},{1,0},{2,3},{3,2},{4,5},{5,4},{6,7},{7,6},{8,9},{9,8},{10,11... | collective-permute-start | bytes 1966088 | tf_op jit(solution)/shard_map/ppermute | solution.py:47
  9.0 14.1 %collective-permute-start.1 = (bf16[1,64,1664]{2,1,0:T(8,128)(2,1)S(1)}, bf16[1,64,1664]{2,1,0:T(8,128)(2,1)S(1)}, u32[]{:S(2)}, u32[]{:S(2)}) collective-permute-start(bf16[1,64,1664]{2,1,0:T(8,128)(2,1)S(1)} %maximum_bitcast_fusion.1), channel_id=1, source_target_pairs={{0,16},{1,17},{2,18},{3,19},{4,20},{5,21},{6,22},{7,23},{8,24},{9,... | collective-permute-start | bytes 638984 | tf_op jit(solution)/shard_map/ppermute | solution.py:55
  12.9 10.3 %collective-permute-start.3 = (bf16[64,1024]{1,0:T(8,128)(2,1)S(1)}, bf16[64,1024]{1,0:T(8,128)(2,1)S(1)}, u32[]{:S(2)}, u32[]{:S(2)}) collective-permute-start(bf16[64,1024]{1,0:T(8,128)(2,1)S(1)} %pad_maximum_fusion.7), channel_id=1, source_target_pairs={{0,8},{1,9},{2,10},{3,11},{4,12},{5,13},{6,14},{7,15},{8,0},{9,1},... | collective-permute-start | bytes 393224 | tf_op jit(solution)/shard_map/ppermute | solution.py:55
  23.3 11.6 %collective-permute-start.6 = (bf16[2,64,1664]{2,1,0:T(8,128)(2,1)S(1)}, bf16[2,64,1664]{2,1,0:T(8,128)(2,1)S(1)}, u32[]{:S(2)}, u32[]{:S(2)}) collective-permute-start(bf16[2,64,1664]{2,1,0:T(8,128)(2,1)S(1)} %pad_maximum_fusion.5), channel_id=1, source_target_pairs={{0,8},{1,9},{2,10},{3,11},{4,12},{5,13},{6,14},{7,15},{8,0},{9,1},... | collective-permute-start | bytes 1277960 | tf_op jit(solution)/shard_map/ppermute | solution.py:55
  24.1 4.3 %collective-permute-start.7 = (bf16[1,32,1024]{2,1,0:T(8,128)(2,1)S(1)}, bf16[1,32,1024]{2,1,0:T(8,128)(2,1)S(1)}, u32[]{:S(2)}, u32[]{:S(2)}) collective-permute-start(bf16[1,32,1024]{2,1,0:T(8,128)(2,1)S(1)} %bitcast.79), channel_id=1, source_target_pairs={{0,2},{1,5},{2,0},{3,7},{4,6},{5,1},{6,4},{7,3},{8,10},{9,13},{10,... | collective-permute-start | bytes 196616 | tf_op jit(solution)/shard_map/ppermute | solution.py:55
  34.9 15.6 %collective-permute-start.8 = (bf16[4,64,1664]{2,1,0:T(8,128)(2,1)S(1)}, bf16[4,64,1664]{2,1,0:T(8,128)(2,1)S(1)}, u32[]{:S(2)}, u32[]{:S(2)}) collective-permute-start(bf16[4,64,1664]{2,1,0:T(8,128)(2,1)S(1)} %pad_maximum_fusion.2), channel_id=1, source_target_pairs={{0,2},{1,5},{2,0},{3,7},{4,6},{5,1},{6,4},{7,3},{8,10},{9,13},{10,... | collective-permute-start | bytes 2555912 | tf_op jit(solution)/shard_map/ppermute | solution.py:55
  36.3 14.2 %collective-permute-start.10 = (bf16[1,128,1024]{2,1,0:T(8,128)(2,1)S(1)}, bf16[1,128,1024]{2,1,0:T(8,128)(2,1)S(1)}, u32[]{:S(2)}, u32[]{:S(2)}) collective-permute-start(bf16[1,128,1024]{2,1,0:T(8,128)(2,1)S(1)} %bitcast.77), channel_id=1, source_target_pairs={{0,16},{1,17},{2,18},{3,19},{4,20},{5,21},{6,22},{7,23},{8,24},{9,... | collective-permute-start | bytes 786440 | tf_op jit(solution)/shard_map/ppermute | solution.py:55
  39.1 6.4 %collective-permute-start.9 = (bf16[2,32,1024]{2,1,0:T(8,128)(2,1)S(1)}, bf16[2,32,1024]{2,1,0:T(8,128)(2,1)S(1)}, u32[]{:S(2)}, u32[]{:S(2)}) collective-permute-start(bf16[2,32,1024]{2,1,0:T(8,128)(2,1)S(1)} %pad_maximum_fusion.8), channel_id=1, source_target_pairs={{0,4},{1,3},{2,6},{3,1},{4,0},{5,7},{6,2},{7,5},{8,12},{9,11},{10,... | collective-permute-start | bytes 393224 | tf_op jit(solution)/shard_map/ppermute | solution.py:55
  50.7 23.0 %collective-permute-start.11 = (bf16[8,64,1664]{2,1,0:T(8,128)(2,1)S(1)}, bf16[8,64,1664]{2,1,0:T(8,128)(2,1)S(1)}, u32[]{:S(2)}, u32[]{:S(2)}) collective-permute-start(bf16[8,64,1664]{2,1,0:T(8,128)(2,1)S(1)} %pad_maximum_fusion.1.sent), channel_id=1, source_target_pairs={{0,4},{1,3},{2,6},{3,1},{4,0},{5,7},{6,2},{7,5},{8,12},{9,11},{10,... | collective-permute-start | bytes 5111816 | tf_op jit(solution)/shard_map/ppermute | solution.py:55
  51.3 22.4 %collective-permute-start.13 = (bf16[2,160,1024]{2,1,0:T(8,128)(2,1)S(1)}, bf16[2,160,1024]{2,1,0:T(8,128)(2,1)S(1)}, u32[]{:S(2)}, u32[]{:S(2)}) collective-permute-start(bf16[2,160,1024]{2,1,0:T(8,128)(2,1)S(1)} %broadcast_select_fusion.refs_5_), channel_id=1, source_target_pairs={{0,8},{1,9},{2,10},{3,11},{4,12},{5,13},{6,14},{7,15},{8,0},{9,1},... | collective-permute-start | bytes 1966088 | tf_op jit(solution)/shard_map/ppermute | solution.py:55
  52.0 20.5 %collective-permute-start.12 = (bf16[1,128,1024]{2,1,0:T(8,128)(2,1)S(1)}, bf16[1,128,1024]{2,1,0:T(8,128)(2,1)S(1)}, u32[]{:S(2)}, u32[]{:S(2)}) collective-permute-start(bf16[1,128,1024]{2,1,0:T(8,128)(2,1)S(1)} %maximum_bitcast_fusion), channel_id=1, source_target_pairs={{0,16},{1,17},{2,18},{3,19},{4,20},{5,21},{6,22},{7,23},{8,24},{9,... | collective-permute-start | bytes 786440 | tf_op jit(solution)/shard_map/ppermute | solution.py:55
  74.9 16.0 %collective-permute-start.15 = (bf16[2,256,1024]{2,1,0:T(8,128)(2,1)S(1)}, bf16[2,256,1024]{2,1,0:T(8,128)(2,1)S(1)}, u32[]{:S(2)}, u32[]{:S(2)}) collective-permute-start(bf16[2,256,1024]{2,1,0:T(8,128)(2,1)S(1)} %constant_dynamic-update-slice_fusion), channel_id=1, source_target_pairs={{0,2},{1,5},{2,0},{3,7},{4,6},{5,1},{6,4},{7,3},{8,10},{9,13},{10,... | collective-permute-start | bytes 3145736 | tf_op jit(solution)/shard_map/ppermute | solution.py:55
  75.5 15.4 %collective-permute-start.14 = (bf16[4,32,1024]{2,1,0:T(8,128)(2,1)S(1)}, bf16[4,32,1024]{2,1,0:T(8,128)(2,1)S(1)}, u32[]{:S(2)}, u32[]{:S(2)}) collective-permute-start(bf16[4,32,1024]{2,1,0:T(8,128)(2,1)S(1)} %pad_maximum_fusion.6), channel_id=1, source_target_pairs={{0,16},{1,17},{2,18},{3,19},{4,20},{5,21},{6,22},{7,23},{8,24},{9,... | collective-permute-start | bytes 786440 | tf_op jit(solution)/shard_map/ppermute | solution.py:55
  91.0 13.6 %collective-permute-start.16 = (bf16[8,32,1024]{2,1,0:T(8,128)(2,1)S(1)}, bf16[8,32,1024]{2,1,0:T(8,128)(2,1)S(1)}, u32[]{:S(2)}, u32[]{:S(2)}) collective-permute-start(bf16[8,32,1024]{2,1,0:T(8,128)(2,1)S(1)} %constant_dynamic-update-slice_fusion.2.refs_1_), channel_id=1, source_target_pairs={{0,8},{1,9},{2,10},{3,11},{4,12},{5,13},{6,14},{7,15},{8,0},{9,1},... | collective-permute-start | bytes 1572872 | tf_op jit(solution)/shard_map/ppermute | solution.py:55
  93.4 13.8 %collective-permute-start.17 = (bf16[8,32,1024]{2,1,0:T(8,128)(2,1)S(1)}, bf16[8,32,1024]{2,1,0:T(8,128)(2,1)S(1)}, u32[]{:S(2)}, u32[]{:S(2)}) collective-permute-start(bf16[8,32,1024]{2,1,0:T(8,128)(2,1)S(1)} %constant_dynamic-update-slice_fusion.2.refs_1_), channel_id=1, source_target_pairs={{0,1},{1,0},{2,3},{3,2},{4,5},{5,4},{6,7},{7,6},{8,9},{9,8},{10,11... | collective-permute-start | bytes 1572872 | tf_op jit(solution)/shard_map/ppermute | solution.py:47
  93.6 26.1 %collective-permute-start.21 = (bf16[4,256,1024]{2,1,0:T(8,128)(2,1)S(1)}, bf16[4,256,1024]{2,1,0:T(8,128)(2,1)S(1)}, u32[]{:S(2)}, u32[]{:S(2)}) collective-permute-start(bf16[4,256,1024]{2,1,0:T(8,128)(2,1)S(1)} %pad_maximum_fusion.refs_1_), channel_id=1, source_target_pairs={{0,4},{1,3},{2,6},{3,1},{4,0},{5,7},{6,2},{7,5},{8,12},{9,11},{10,... | collective-permute-start | bytes 6291464 | tf_op jit(solution)/shard_map/ppermute | solution.py:55
  113.2 17.4 %collective-permute-start.25 = (bf16[2,160,1024]{2,1,0:T(8,128)(2,1)S(1)}, bf16[2,160,1024]{2,1,0:T(8,128)(2,1)S(1)}, u32[]{:S(2)}, u32[]{:S(2)}) collective-permute-start(bf16[2,160,1024]{2,1,0:T(8,128)(2,1)S(1)} %copy-done.35), channel_id=1, source_target_pairs={{0,1},{1,0},{2,3},{3,2},{4,5},{5,4},{6,7},{7,6},{8,9},{9,8},{10,11... | collective-permute-start | bytes 1966088 | tf_op jit(solution)/shard_map/ppermute | solution.py:47
  113.6 17.0 %collective-permute-start.23 = (bf16[320,1024]{1,0:T(8,128)(2,1)}, bf16[320,1024]{1,0:T(8,128)(2,1)S(1)}, u32[]{:S(2)}, u32[]{:S(2)}) collective-permute-start(bf16[320,1024]{1,0:T(8,128)(2,1)} %get-tuple-element.167.refs_3_), channel_id=1, source_target_pairs={{0,8},{1,9},{2,10},{3,11},{4,12},{5,13},{6,14},{7,15},{8,0},{9,1},... | collective-permute-start | bytes 1966088 | tf_op jit(solution)/shard_map/ppermute | solution.py:55
  148.1 2.9 collective-permute-start.26
  155.2 17.0 %collective-permute-start.29 = (bf16[320,1024]{1,0:T(8,128)(2,1)}, bf16[320,1024]{1,0:T(8,128)(2,1)S(1)}, u32[]{:S(2)}, u32[]{:S(2)}) collective-permute-start(bf16[320,1024]{1,0:T(8,128)(2,1)} %get-tuple-element.194.refs_9_), channel_id=1, source_target_pairs={{0,8},{1,9},{2,10},{3,11},{4,12},{5,13},{6,14},{7,15},{8,0},{9,1},... | collective-permute-start | bytes 1966088 | tf_op jit(solution)/shard_map/ppermute | solution.py:55
  156.9 14.6 %collective-permute-start.28 = (bf16[320,1024]{1,0:T(8,128)(2,1)S(1)}, bf16[320,1024]{1,0:T(8,128)(2,1)S(1)}, u32[]{:S(2)}, u32[]{:S(2)}) collective-permute-start(bf16[320,1024]{1,0:T(8,128)(2,1)S(1)} %copy-done.37), channel_id=1, source_target_pairs={{0,1},{1,0},{2,3},{3,2},{4,5},{5,4},{6,7},{7,6},{8,9},{9,8},{10,11... | collective-permute-start | bytes 1966088 | tf_op jit(solution)/shard_map/ppermute | solution.py:47
  169.8 31.6 %collective-permute-start.31 = (bf16[4,256,1024]{2,1,0:T(8,128)(2,1)}, bf16[4,256,1024]{2,1,0:T(8,128)(2,1)S(1)}, u32[]{:S(2)}, u32[]{:S(2)}) collective-permute-start(bf16[4,256,1024]{2,1,0:T(8,128)(2,1)} %bitcast.91), channel_id=1, source_target_pairs={{0,4},{1,3},{2,6},{3,1},{4,0},{5,7},{6,2},{7,5},{8,12},{9,11},{10,... | collective-permute-start | bytes 6291464 | tf_op jit(solution)/shard_map/ppermute | solution.py:55
  179.0 13.5 %collective-permute-start.34 = (bf16[320,1024]{1,0:T(8,128)(2,1)}, bf16[320,1024]{1,0:T(8,128)(2,1)S(1)}, u32[]{:S(2)}, u32[]{:S(2)}) collective-permute-start(bf16[320,1024]{1,0:T(8,128)(2,1)} %get-tuple-element.202.refs_9_), channel_id=1, source_target_pairs={{0,1},{1,0},{2,3},{3,2},{4,5},{5,4},{6,7},{7,6},{8,9},{9,8},{10,11... | collective-permute-start | bytes 1966088 | tf_op jit(solution)/shard_map/ppermute | solution.py:47
  179.0 3.2 %collective-permute-start.30 = (bf16[320,512]{1,0:T(8,128)(2,1)}, bf16[320,512]{1,0:T(8,128)(2,1)S(1)}, u32[]{:S(2)}, u32[]{:S(2)}) collective-permute-start(bf16[320,512]{1,0:T(8,128)(2,1)} %get-tuple-element.198), channel_id=1, source_target_pairs={{0,1},{1,0},{2,3},{3,2},{4,5},{5,4},{6,7},{7,6},{8,9},{9,8},{10,11... | collective-permute-start | bytes 983048 | tf_op jit(solution)/shard_map/ppermute | solution.py:47
  179.5 12.9 %collective-permute-start.32 = (bf16[160,512]{1,0:T(8,128)(2,1)S(1)}, bf16[160,512]{1,0:T(8,128)(2,1)S(1)}, u32[]{:S(2)}, u32[]{:S(2)}) collective-permute-start(bf16[160,512]{1,0:T(8,128)(2,1)S(1)} %copy-done.9), channel_id=1, source_target_pairs={{0,1},{1,0},{2,3},{3,2},{4,5},{5,4},{6,7},{7,6},{8,9},{9,8},{10,11... | collective-permute-start | bytes 491528 | tf_op jit(solution)/shard_map/ppermute | solution.py:47
  179.5 12.9 %collective-permute-start.33 = (bf16[160,512]{1,0:T(8,128)(2,1)S(1)}, bf16[160,512]{1,0:T(8,128)(2,1)S(1)}, u32[]{:S(2)}, u32[]{:S(2)}) collective-permute-start(bf16[160,512]{1,0:T(8,128)(2,1)S(1)} %copy-done.3), channel_id=1, source_target_pairs={{0,1},{1,0},{2,3},{3,2},{4,5},{5,4},{6,7},{7,6},{8,9},{9,8},{10,11... | collective-permute-start | bytes 491528 | tf_op jit(solution)/shard_map/ppermute | solution.py:47
  182.2 95.0 %collective-permute-start.38 = (bf16[320,1024]{1,0:T(8,128)(2,1)}, bf16[320,1024]{1,0:T(8,128)(2,1)}, u32[]{:S(2)}, u32[]{:S(2)}) collective-permute-start(bf16[320,1024]{1,0:T(8,128)(2,1)} %get-tuple-element.218), channel_id=1, source_target_pairs={{0,8},{1,9},{2,10},{3,11},{4,12},{5,13},{6,14},{7,15},{8,0},{9,1},... | collective-permute-start | bytes 1966088 | tf_op jit(solution)/shard_map/ppermute | solution.py:55
  198.0 21.5 %collective-permute-start.35 = (bf16[8,32,1024]{2,1,0:T(8,128)(2,1)}, bf16[8,32,1024]{2,1,0:T(8,128)(2,1)}, u32[]{:S(2)}, u32[]{:S(2)}) collective-permute-start(bf16[8,32,1024]{2,1,0:T(8,128)(2,1)} %bitcast.93), channel_id=1, source_target_pairs={{0,4},{1,3},{2,6},{3,1},{4,0},{5,7},{6,2},{7,5},{8,12},{9,11},{10,... | collective-permute-start | bytes 1572872 | tf_op jit(solution)/shard_map/ppermute | solution.py:55
  202.4 17.1 %collective-permute-start.36 = (bf16[2,256,1024]{2,1,0:T(8,128)(2,1)S(1)}, bf16[2,256,1024]{2,1,0:T(8,128)(2,1)S(1)}, u32[]{:S(2)}, u32[]{:S(2)}) collective-permute-start(bf16[2,256,1024]{2,1,0:T(8,128)(2,1)S(1)} %get-tuple-element.261), channel_id=1, source_target_pairs={{0,2},{1,5},{2,0},{3,7},{4,6},{5,1},{6,4},{7,3},{8,10},{9,13},{10,... | collective-permute-start | bytes 3145736 | tf_op jit(solution)/shard_map/ppermute | solution.py:55
  217.1 21.7 %collective-permute-start.41 = (bf16[8,64,1536]{2,1,0:T(8,128)(2,1)}, bf16[8,64,1536]{2,1,0:T(8,128)(2,1)S(1)}, u32[]{:S(2)}, u32[]{:S(2)}) collective-permute-start(bf16[8,64,1536]{2,1,0:T(8,128)(2,1)} %bitcast.92), channel_id=1, source_target_pairs={{0,4},{1,3},{2,6},{3,1},{4,0},{5,7},{6,2},{7,5},{8,12},{9,11},{10,... | collective-permute-start | bytes 4718600 | tf_op jit(solution)/shard_map/ppermute | solution.py:55
  231.3 26.5 %collective-permute-start.43 = (bf16[1,256,1024]{2,1,0:T(8,128)(2,1)}, bf16[1,256,1024]{2,1,0:T(8,128)(2,1)}, u32[]{:S(2)}, u32[]{:S(2)}) collective-permute-start(bf16[1,256,1024]{2,1,0:T(8,128)(2,1)} %fusion.3), channel_id=1, source_target_pairs={{0,16},{1,17},{2,18},{3,19},{4,20},{5,21},{6,22},{7,23},{8,24},{9,... | collective-permute-start | bytes 1572872 | tf_op jit(solution)/shard_map/ppermute | solution.py:55
  233.8 6.4 %collective-permute-start.40 = (bf16[4,32,1024]{2,1,0:T(8,128)(2,1)S(1)}, bf16[4,32,1024]{2,1,0:T(8,128)(2,1)S(1)}, u32[]{:S(2)}, u32[]{:S(2)}) collective-permute-start(bf16[4,32,1024]{2,1,0:T(8,128)(2,1)S(1)} %get-tuple-element.273), channel_id=1, source_target_pairs={{0,2},{1,5},{2,0},{3,7},{4,6},{5,1},{6,4},{7,3},{8,10},{9,13},{10,... | collective-permute-start | bytes 786440 | tf_op jit(solution)/shard_map/ppermute | solution.py:55
  235.7 7.4 %collective-permute-start.39 = (bf16[2,160,1024]{2,1,0:T(8,128)(2,1)S(1)}, bf16[2,160,1024]{2,1,0:T(8,128)(2,1)S(1)}, u32[]{:S(2)}, u32[]{:S(2)}) collective-permute-start(bf16[2,160,1024]{2,1,0:T(8,128)(2,1)S(1)} %copy-done.38), channel_id=1, source_target_pairs={{0,1},{1,0},{2,3},{3,2},{4,5},{5,4},{6,7},{7,6},{8,9},{9,8},{10,11... | collective-permute-start | bytes 1966088 | tf_op jit(solution)/shard_map/ppermute | solution.py:47
  238.8 40.6 %collective-permute-start.37 = (bf16[320,1024]{1,0:T(8,128)(2,1)}, bf16[320,1024]{1,0:T(8,128)(2,1)}, u32[]{:S(2)}, u32[]{:S(2)}) collective-permute-start(bf16[320,1024]{1,0:T(8,128)(2,1)} %get-tuple-element.217), channel_id=1, source_target_pairs={{0,1},{1,0},{2,3},{3,2},{4,5},{5,4},{6,7},{7,6},{8,9},{9,8},{10,11... | collective-permute-start | bytes 1966088 | tf_op jit(solution)/shard_map/ppermute | solution.py:47
  240.2 20.6 %collective-permute-start.45 = (bf16[4,64,1536]{2,1,0:T(8,128)(2,1)S(1)}, bf16[4,64,1536]{2,1,0:T(8,128)(2,1)S(1)}, u32[]{:S(2)}, u32[]{:S(2)}) collective-permute-start(bf16[4,64,1536]{2,1,0:T(8,128)(2,1)S(1)} %get-tuple-element.265), channel_id=1, source_target_pairs={{0,2},{1,5},{2,0},{3,7},{4,6},{5,1},{6,4},{7,3},{8,10},{9,13},{10,... | collective-permute-start | bytes 2359304 | tf_op jit(solution)/shard_map/ppermute | solution.py:55
  243.1 30.1 %collective-permute-start.47 = (bf16[2,32,1024]{2,1,0:T(8,128)(2,1)S(1)}, bf16[2,32,1024]{2,1,0:T(8,128)(2,1)S(1)}, u32[]{:S(2)}, u32[]{:S(2)}) collective-permute-start(bf16[2,32,1024]{2,1,0:T(8,128)(2,1)S(1)} %get-tuple-element.271), channel_id=1, source_target_pairs={{0,8},{1,9},{2,10},{3,11},{4,12},{5,13},{6,14},{7,15},{8,0},{9,1},... | collective-permute-start | bytes 393224 | tf_op jit(solution)/shard_map/ppermute | solution.py:55
  260.3 4.0 %collective-permute-start.44 = (f32[8,8,128]{2,1,0:T(8,128)S(1)}, f32[8,8,128]{2,1,0:T(8,128)S(1)}, u32[]{:S(2)}, u32[]{:S(2)}) collective-permute-start(f32[8,8,128]{2,1,0:T(8,128)S(1)} %slice.288), channel_id=1, source_target_pairs={{0,4},{1,3},{2,6},{3,1},{4,0},{5,7},{6,2},{7,5},{8,12},{9,11},{10,... | collective-permute-start | bytes 98312 | tf_op jit(solution)/shard_map/ppermute | solution.py:55
  261.1 12.0 %collective-permute-start.48 = (bf16[2,64,1536]{2,1,0:T(8,128)(2,1)S(1)}, bf16[2,64,1536]{2,1,0:T(8,128)(2,1)S(1)}, u32[]{:S(2)}, u32[]{:S(2)}) collective-permute-start(bf16[2,64,1536]{2,1,0:T(8,128)(2,1)S(1)} %get-tuple-element.259), channel_id=1, source_target_pairs={{0,8},{1,9},{2,10},{3,11},{4,12},{5,13},{6,14},{7,15},{8,0},{9,1},... | collective-permute-start | bytes 1179656 | tf_op jit(solution)/shard_map/ppermute | solution.py:55
  264.3 18.9 %collective-permute-start.51 = (f32[64,1024]{1,0:T(8,128)S(1)}, f32[64,1024]{1,0:T(8,128)S(1)}, u32[]{:S(2)}, u32[]{:S(2)}) collective-permute-start(f32[64,1024]{1,0:T(8,128)S(1)} %slice_bitcast_fusion.2), channel_id=1, source_target_pairs={{0,8},{1,9},{2,10},{3,11},{4,12},{5,13},{6,14},{7,15},{8,0},{9,1},... | collective-permute-start | bytes 786440 | tf_op jit(solution)/shard_map/ppermute | solution.py:55
  273.1 14.4 %collective-permute-start.52 = (f32[32,1024]{1,0:T(8,128)S(1)}, f32[32,1024]{1,0:T(8,128)S(1)}, u32[]{:S(2)}, u32[]{:S(2)}) collective-permute-start(f32[32,1024]{1,0:T(8,128)S(1)} %slice_bitcast_fusion.4), channel_id=1, source_target_pairs={{0,1},{1,0},{2,3},{3,2},{4,5},{5,4},{6,7},{7,6},{8,9},{9,8},{10,11... | collective-permute-start | bytes 393224 | tf_op jit(solution)/shard_map/ppermute | solution.py:47
  273.1 3.7 %collective-permute-start.46 = (f32[4,8,128]{2,1,0:T(8,128)S(1)}, f32[4,8,128]{2,1,0:T(8,128)S(1)}, u32[]{:S(2)}, u32[]{:S(2)}) collective-permute-start(f32[4,8,128]{2,1,0:T(8,128)S(1)} %get-tuple-element.281), channel_id=1, source_target_pairs={{0,2},{1,5},{2,0},{3,7},{4,6},{5,1},{6,4},{7,3},{8,10},{9,13},{10,... | collective-permute-start | bytes 49160 | tf_op jit(solution)/shard_map/ppermute | solution.py:55
  276.8 10.0 %collective-permute-start.54 = (bf16[1,32,1024]{2,1,0:T(8,128)(2,1)S(1)}, bf16[1,32,1024]{2,1,0:T(8,128)(2,1)S(1)}, u32[]{:S(2)}, u32[]{:S(2)}) collective-permute-start(bf16[1,32,1024]{2,1,0:T(8,128)(2,1)S(1)} %fusion.11), channel_id=1, source_target_pairs={{0,16},{1,17},{2,18},{3,19},{4,20},{5,21},{6,22},{7,23},{8,24},{9,... | collective-permute-start | bytes 196616 | tf_op jit(solution)/shard_map/ppermute | solution.py:55
  277.2 6.0 %collective-permute-start.49 = (f32[2,8,128]{2,1,0:T(8,128)S(1)}, f32[2,8,128]{2,1,0:T(8,128)S(1)}, u32[]{:S(2)}, u32[]{:S(2)}) collective-permute-start(f32[2,8,128]{2,1,0:T(8,128)S(1)} %get-tuple-element.282), channel_id=1, source_target_pairs={{0,8},{1,9},{2,10},{3,11},{4,12},{5,13},{6,14},{7,15},{8,0},{9,1},... | collective-permute-start | bytes 24584 | tf_op jit(solution)/shard_map/ppermute | solution.py:55
  279.4 12.5 %collective-permute-start.55 = (bf16[1,64,1536]{2,1,0:T(8,128)(2,1)S(1)}, bf16[1,64,1536]{2,1,0:T(8,128)(2,1)S(1)}, u32[]{:S(2)}, u32[]{:S(2)}) collective-permute-start(bf16[1,64,1536]{2,1,0:T(8,128)(2,1)S(1)} %fusion.6), channel_id=1, source_target_pairs={{0,16},{1,17},{2,18},{3,19},{4,20},{5,21},{6,22},{7,23},{8,24},{9,... | collective-permute-start | bytes 589832 | tf_op jit(solution)/shard_map/ppermute | solution.py:55
  283.3 4.3 %collective-permute-start.53 = (f32[32,1024]{1,0:T(8,128)S(1)}, f32[32,1024]{1,0:T(8,128)S(1)}, u32[]{:S(2)}, u32[]{:S(2)}) collective-permute-start(f32[32,1024]{1,0:T(8,128)S(1)} %slice.259), channel_id=1, source_target_pairs={{0,1},{1,0},{2,3},{3,2},{4,5},{5,4},{6,7},{7,6},{8,9},{9,8},{10,11... | collective-permute-start | bytes 393224 | tf_op jit(solution)/shard_map/ppermute | solution.py:47
  283.4 7.4 %collective-permute-start.50 = (f32[1,8,128]{2,1,0:T(8,128)S(1)}, f32[1,8,128]{2,1,0:T(8,128)S(1)}, u32[]{:S(2)}, u32[]{:S(2)}) collective-permute-start(f32[1,8,128]{2,1,0:T(8,128)S(1)} %slice_add_fusion.14), channel_id=1, source_target_pairs={{0,16},{1,17},{2,18},{3,19},{4,20},{5,21},{6,22},{7,23},{8,24},{9,... | collective-permute-start | bytes 12296 | tf_op jit(solution)/shard_map/ppermute | solution.py:55
  (59 other events, 310.1 us)
